TPU v7x, 32 devices: a whole 2x2x4 slice. The times are simulated.
32 devices in a mesh: ctx: 8 (over y, x, core), shard: 4 (over z).
Axes of the slice: x: 2, y: 2, z: 4, core: 2. Of those that a mesh axis runs over, the one named last changes fastest.
Arguments:
- layer_input: bfloat16 [4, 1024, 2048], P('shard', 'ctx'), may hold values from -6 to 6
- w_query: bfloat16 [2048, 2048], P(None, 'shard'), may hold values from -0.125 to 0.125
- w_key: bfloat16 [2048, 1024], P(None, 'shard'), may hold values from -0.125 to 0.125
- w_value: bfloat16 [2048, 1024], P(None, 'shard'), may hold values from -0.125 to 0.125
- w_out: bfloat16 [2048, 2048], P(None, 'shard'), may hold values from -1.5 to 1.5
- w_gate: bfloat16 [2048, 8192], P(None, 'shard'), may hold values from -0.125 to 0.125
- w_up: bfloat16 [2048, 8192], P(None, 'shard'), may hold values from -0.125 to 0.125
- w_down: bfloat16 [8192, 2048], P(None, 'shard'), may hold values from -0.0625 to 0.0625
- attn_gain: float32 [2048], replicated, may hold values from 0.5 to 1.5
- mlp_gain: float32 [2048], replicated, may hold values from 0.5 to 1.5
- block_pairs: int32 [4, 8], P('shard'), may hold values from 0 to 7, each once within a row
- doc_ids: int32 [4, 1024], P('shard'), may hold values from 0 to 3, never falling along the last dimension, each value on 1 to 512 neighbouring positions
- cotangent: bfloat16 [4, 1024, 2048], P('shard', 'ctx'), may hold values from -6 to 6
Outputs:
- output: bfloat16 [4, 1024, 2048], P('shard', 'ctx')
- grad_input: bfloat16 [4, 1024, 2048], P('shard', 'ctx')
- grad_query: float32 [2048, 2048], P(('ctx', 'shard'))
- grad_key: float32 [2048, 1024], P(('ctx', 'shard'))
- grad_value: float32 [2048, 1024], P(('ctx', 'shard'))
- grad_out: float32 [2048, 2048], P(('ctx', 'shard'))
- grad_gate: float32 [2048, 8192], P(('ctx', 'shard'))
- grad_up: float32 [2048, 8192], P(('ctx', 'shard'))
- grad_down: float32 [8192, 2048], P(('ctx', 'shard'))
- grad_attn_gain: float32 [2048], P(('ctx', 'shard'))
- grad_mlp_gain: float32 [2048], P(('ctx', 'shard'))
Inputs may be any that keep to these rules, and one draw needn't show every extreme that they name: Each row holds each number once: in sequence s, ctx index c holds blocks block_pairs[s, c] and 15 - block_pairs[s, c] of the sequence's 2 * 8 blocks. `doc_ids`: each row never falls along positions; every document has 1 to 512 positions, one of each row exactly 512.
All inputs are finite; a program needn't handle non-finite values.
Results may differ from a plain program's by a relative error of at most 0.02.
Values may be sent and summed in bfloat16 or wider, within the bound.
A program may use at most 320 MiB of HBM per device.

v0:
```python
import math

import jax
import jax.numpy as jnp
from jax import lax
from jax.sharding import PartitionSpec as P

HQ = 8
HK = 4
HD = 256
WINDOW = 1024


EPSILON = 1e-06
SCORE_SCALE = 0.0625
MASKED = -1e30
ROPE_BASE = 1000042.0


def position_of(rows, pairs, per_device, blocks_total):
    device = rows // per_device
    within = rows % per_device
    half = per_device // 2
    chosen = jnp.take(pairs, device)
    first = chosen * half + within
    second = (blocks_total - 1 - chosen) * half + within - half
    return jnp.where(within < half, first, second)


def rope_tables(positions, head):
    half = head // 2
    freq = ROPE_BASE ** (-(jnp.arange(half, dtype=jnp.float32) * 2.0) / head)
    angle = positions.astype(jnp.float32)[:, None] * freq[None, :]
    return (jnp.cos(angle), jnp.sin(angle))


def rotate(values, cosine, sine):
    half = values.shape[-1] // 2
    first = values[..., :half]
    second = values[..., half:]
    cosine = cosine[:, None, :]
    sine = sine[:, None, :]
    return jnp.concatenate(
        [first * cosine - second * sine, second * cosine + first * sine], axis=-1
    )


def rotate_back(grads, cosine, sine):
    half = grads.shape[-1] // 2
    first = grads[..., :half]
    second = grads[..., half:]
    cosine = cosine[:, None, :]
    sine = sine[:, None, :]
    return jnp.concatenate(
        [first * cosine + second * sine, second * cosine - first * sine], axis=-1
    )


def visible(query_pos, query_doc, key_pos, key_doc):
    distance = query_pos[:, None] - key_pos[None, :]
    return (query_doc[:, None] == key_doc[None, :]) & (distance >= 0) & (distance < WINDOW)


def write_columns(left, piece):
    made = jnp.dot(left, piece, preferred_element_type=jnp.float32)
    return made


def contract_full(grads, weight):
    return lax.dot_general(
        grads, weight, (((1,), (1,)), ((), ())), preferred_element_type=jnp.float32
    )


def alternate(parts, shard_count, rows):
    return jnp.concatenate([part.reshape(rows, shard_count, -1) for part in parts], axis=2).reshape(
        rows, -1
    )


def outer_sum(left, right):
    return lax.dot_general(
        left, right, (((0,), (0,)), ((), ())), preferred_element_type=jnp.float32
    )


def term_rows(lefts, rights, gain_block, count):
    normed_all, attended_all, second_all, act_all = lefts
    query_g, key_g, value_g, branch_g, gate_g, up_g, upstream_g = rights
    down_part = outer_sum(act_all, upstream_g).reshape(count, -1)
    return jnp.concatenate(
        [
            outer_sum(normed_all, query_g),
            outer_sum(normed_all, key_g),
            outer_sum(normed_all, value_g),
            outer_sum(attended_all, branch_g),
            outer_sum(second_all, gate_g),
            outer_sum(second_all, up_g),
            down_part,
            gain_block,
        ],
        axis=1,
    )


def deal_columns(values, ctx_count, shard_count):
    rows = values.shape[0]
    return (
        values.reshape(rows, ctx_count, shard_count, -1)
        .transpose(0, 2, 1, 3)
        .reshape(rows, shard_count, -1)
    )


def on_device(
    layer_input,
    w_query,
    w_key,
    w_value,
    w_out,
    w_gate,
    w_up,
    w_down,
    attn_gain,
    mlp_gain,
    block_pairs,
    doc_ids,
    cotangent,
):
    tok_rows = layer_input.shape[1]
    model_width = layer_input.shape[2]
    shard_count = lax.axis_size("shard")
    ctx_count = lax.axis_size("ctx")
    device_count = lax.axis_size(("ctx", "shard"))
    group_size = HQ // HK
    blocks_total = 2 * ctx_count
    pairs = block_pairs[0]
    documents = doc_ids[0]
    own_rows = lax.axis_index("ctx") * tok_rows + jnp.arange(tok_rows, dtype=jnp.int32)
    own_pos = position_of(own_rows, pairs, tok_rows, blocks_total)
    own_doc = jnp.take(documents, own_pos)
    cosine, sine = rope_tables(own_pos, HD)
    stack_qkv = jnp.concatenate([w_query, w_key, w_value], axis=1)
    stack_mlp = jnp.concatenate([w_gate, w_up], axis=1)
    per_query = w_query.shape[1]
    per_key = w_key.shape[1]
    per_hidden = w_gate.shape[1]
    hidden_width = w_down.shape[0]
    inputs = layer_input.reshape(tok_rows, model_width).astype(jnp.float32)
    factor_one = lax.rsqrt(jnp.mean(inputs * inputs, axis=-1, keepdims=True) + EPSILON)
    normed = (inputs * factor_one * attn_gain).astype(jnp.bfloat16)
    projected = write_columns(normed, lax.all_gather(stack_qkv, "shard", axis=1, tiled=True))
    projected = projected.reshape(tok_rows, shard_count, -1)
    query_lin = projected[:, :, :per_query].reshape(tok_rows, HQ, HD)
    key_lin = projected[:, :, per_query : per_query + per_key].reshape(tok_rows, HK, HD)
    value_lin = projected[:, :, per_query + per_key :].reshape(tok_rows, HK * HD)
    query_rot = (
        rotate(query_lin, cosine, sine).astype(jnp.bfloat16).reshape(tok_rows, HK, group_size, HD)
    )
    key_rot = rotate(key_lin, cosine, sine).astype(jnp.bfloat16).reshape(tok_rows, HK * HD)
    value_low = value_lin.astype(jnp.bfloat16)

    def key_mask(first_row, count):
        key_pos = position_of(
            first_row + jnp.arange(count, dtype=jnp.int32), pairs, tok_rows, blocks_total
        )
        return visible(own_pos, own_doc, key_pos, jnp.take(documents, key_pos))[:, None, None, :]

    start_state = (
        jnp.full((tok_rows, HK, group_size), MASKED, jnp.float32),
        jnp.zeros((tok_rows, HK, group_size), jnp.float32),
        jnp.zeros((tok_rows, HK, group_size, HD), jnp.float32),
    )
    keys = lax.all_gather(key_rot, "ctx", axis=0, tiled=True)
    values = lax.all_gather(value_low, "ctx", axis=0, tiled=True)
    count = keys.shape[0]
    step = math.gcd(count, 4 * tok_rows)
    keys = keys.reshape(count // step, step, HK, HD)
    values = values.reshape(count // step, step, HK, HD)

    def attend_step(i, running):
        top, total, accum = running
        mask = key_mask(i * step, step)
        scores = (
            jnp.einsum("tkgd,skd->tkgs", query_rot, keys[i], preferred_element_type=jnp.float32)
            * SCORE_SCALE
        )
        scores = jnp.where(mask, scores, MASKED)
        new_top = jnp.maximum(top, jnp.max(scores, axis=-1))
        weights = jnp.where(mask, jnp.exp(scores - new_top[..., None]), 0.0)
        shrink = jnp.exp(top - new_top)
        total = total * shrink + jnp.sum(weights, axis=-1)
        accum = accum * shrink[..., None] + jnp.einsum(
            "tkgs,skd->tkgd",
            weights.astype(jnp.bfloat16),
            values[i],
            preferred_element_type=jnp.float32,
        )
        return (new_top, total, accum)

    top, total, accum = lax.fori_loop(0, count // step, attend_step, start_state)
    log_total = top + jnp.log(total)
    attended_full = accum / total[..., None]
    attended = attended_full.astype(jnp.bfloat16).reshape(tok_rows, HQ * HD)
    branch_one = write_columns(attended, lax.all_gather(w_out, "shard", axis=1, tiled=True))
    mid = inputs + branch_one
    factor_two = lax.rsqrt(jnp.mean(mid * mid, axis=-1, keepdims=True) + EPSILON)
    normed_two = (mid * factor_two * mlp_gain).astype(jnp.bfloat16)
    gate_up = write_columns(normed_two, lax.all_gather(stack_mlp, "shard", axis=1, tiled=True))
    gate_up = gate_up.reshape(tok_rows, shard_count, -1)
    gate = gate_up[:, :, :per_hidden].reshape(tok_rows, hidden_width)
    up_lin = gate_up[:, :, per_hidden:].reshape(tok_rows, hidden_width)
    sigma = jax.nn.sigmoid(gate)
    swish = gate * sigma
    act = (swish * up_lin).astype(jnp.bfloat16)
    branch_two = write_columns(act, lax.all_gather(w_down, "shard", axis=1, tiled=True))
    output = (mid + branch_two).astype(jnp.bfloat16).reshape(1, tok_rows, model_width)
    full_qkv, full_out, full_mlp, full_down = (
        lax.all_gather(stack_qkv, "shard", axis=1, tiled=True),
        lax.all_gather(w_out, "shard", axis=1, tiled=True),
        lax.all_gather(stack_mlp, "shard", axis=1, tiled=True),
        lax.all_gather(w_down, "shard", axis=1, tiled=True),
    )
    upstream_low = cotangent.reshape(tok_rows, model_width)
    upstream = upstream_low.astype(jnp.float32)
    act_grad = contract_full(upstream_low, full_down)
    gate_grad = (act_grad * up_lin * (sigma * (1.0 + gate * (1.0 - sigma)))).astype(jnp.bfloat16)
    up_grad = (act_grad * swish).astype(jnp.bfloat16)
    stacked_mlp_grad = alternate((gate_grad, up_grad), shard_count, tok_rows)
    norm_two_grad = contract_full(stacked_mlp_grad, full_mlp)
    mlp_gain_term = jnp.sum(norm_two_grad * mid * factor_two, axis=0)
    scaled_two = norm_two_grad * mlp_gain
    mid_grad = (
        upstream
        + factor_two * scaled_two
        - mid * factor_two**3 * jnp.mean(scaled_two * mid, axis=-1, keepdims=True)
    )
    branch_grad = mid_grad.astype(jnp.bfloat16)
    attended_grad = contract_full(branch_grad, full_out)
    attended_low = attended_grad.astype(jnp.bfloat16).reshape(tok_rows, HK, group_size, HD)
    delta = jnp.sum(attended_low.astype(jnp.float32) * attended_full, axis=-1)

    def query_grads(carry, piece):
        keys, values = piece
        count = keys.shape[0]
        step = math.gcd(count, 4 * tok_rows)
        keys = keys.reshape(count // step, step, HK, HD)
        values = values.reshape(count // step, step, HK, HD)

        def query_step(i, query_sum):
            mask = key_mask(i * step, step)
            scores = (
                jnp.einsum("tkgd,skd->tkgs", query_rot, keys[i], preferred_element_type=jnp.float32)
                * SCORE_SCALE
            )
            probs = jnp.where(mask, jnp.exp(scores - log_total[..., None]), 0.0)
            prob_grad = jnp.einsum(
                "tkgd,skd->tkgs", attended_low, values[i], preferred_element_type=jnp.float32
            )
            score_grad = (probs * (prob_grad - delta[..., None])).astype(jnp.bfloat16)
            return query_sum + jnp.einsum(
                "tkgs,skd->tkgd", score_grad, keys[i], preferred_element_type=jnp.float32
            )

        return lax.fori_loop(0, count // step, query_step, carry)

    query_sum = query_grads(
        jnp.zeros((tok_rows, HK, group_size, HD), jnp.float32),
        (
            lax.all_gather(key_rot, "ctx", axis=0, tiled=True),
            lax.all_gather(value_low, "ctx", axis=0, tiled=True),
        ),
    )
    all_log_total, all_delta = (
        lax.all_gather(log_total, "ctx", axis=0, tiled=True),
        lax.all_gather(delta, "ctx", axis=0, tiled=True),
    )
    key_three = key_rot.reshape(tok_rows, HK, HD)
    value_three = value_low.reshape(tok_rows, HK, HD)

    def key_grads(carry, piece):
        queries, outgrads = piece
        count = queries.shape[0]
        step = math.gcd(count, 4 * tok_rows)
        queries = queries.reshape(count // step, step, HK, group_size, HD)
        outgrads = outgrads.reshape(count // step, step, HK, group_size, HD)

        def key_step(i, running):
            key_sum, value_sum = running
            first_row = i * step
            query_pos = position_of(
                first_row + jnp.arange(step, dtype=jnp.int32), pairs, tok_rows, blocks_total
            )
            mask = visible(query_pos, jnp.take(documents, query_pos), own_pos, own_doc)[
                :, None, None, :
            ]
            lse_part = lax.dynamic_slice_in_dim(all_log_total, first_row, step, 0)
            delta_part = lax.dynamic_slice_in_dim(all_delta, first_row, step, 0)
            scores = (
                jnp.einsum(
                    "skgd,tkd->skgt", queries[i], key_three, preferred_element_type=jnp.float32
                )
                * SCORE_SCALE
            )
            probs = jnp.where(mask, jnp.exp(scores - lse_part[..., None]), 0.0)
            prob_grad = jnp.einsum(
                "skgd,tkd->skgt", outgrads[i], value_three, preferred_element_type=jnp.float32
            )
            score_grad = (probs * (prob_grad - delta_part[..., None])).astype(jnp.bfloat16)
            value_sum = value_sum + jnp.einsum(
                "skgt,skgd->tkd",
                probs.astype(jnp.bfloat16),
                outgrads[i],
                preferred_element_type=jnp.float32,
            )
            key_sum = key_sum + jnp.einsum(
                "skgt,skgd->tkd", score_grad, queries[i], preferred_element_type=jnp.float32
            )
            return (key_sum, value_sum)

        return lax.fori_loop(0, count // step, key_step, carry)

    key_sum, value_sum = key_grads(
        (jnp.zeros((tok_rows, HK, HD), jnp.float32), jnp.zeros((tok_rows, HK, HD), jnp.float32)),
        (
            lax.all_gather(query_rot.reshape(tok_rows, HQ * HD), "ctx", axis=0, tiled=True),
            lax.all_gather(attended_low.reshape(tok_rows, HQ * HD), "ctx", axis=0, tiled=True),
        ),
    )
    query_grad = (
        rotate_back(query_sum.reshape(tok_rows, HQ, HD) * SCORE_SCALE, cosine, sine)
        .astype(jnp.bfloat16)
        .reshape(tok_rows, HQ * HD)
    )
    key_grad = (
        rotate_back(key_sum * SCORE_SCALE, cosine, sine)
        .astype(jnp.bfloat16)
        .reshape(tok_rows, HK * HD)
    )
    value_grad = value_sum.astype(jnp.bfloat16).reshape(tok_rows, HK * HD)
    stacked_qkv_grad = alternate((query_grad, key_grad, value_grad), shard_count, tok_rows)
    normed_grad = contract_full(stacked_qkv_grad, full_qkv)
    attn_gain_term = jnp.sum(normed_grad * inputs * factor_one, axis=0)
    scaled_one = normed_grad * attn_gain
    input_grad = (
        mid_grad
        + factor_one * scaled_one
        - inputs * factor_one**3 * jnp.mean(scaled_one * inputs, axis=-1, keepdims=True)
    )
    grad_input = input_grad.astype(jnp.bfloat16).reshape(1, tok_rows, model_width)
    ratio = hidden_width // model_width
    own_share = model_width // device_count
    rights = (query_grad, key_grad, value_grad, branch_grad, gate_grad, up_grad, upstream_low)
    group_rights = (
        lax.all_gather(rights[0], "shard", axis=0, tiled=True),
        lax.all_gather(rights[1], "shard", axis=0, tiled=True),
        lax.all_gather(rights[2], "shard", axis=0, tiled=True),
        lax.all_gather(rights[3], "shard", axis=0, tiled=True),
        lax.all_gather(rights[4], "shard", axis=0, tiled=True),
        lax.all_gather(rights[5], "shard", axis=0, tiled=True),
        lax.all_gather(rights[6], "shard", axis=0, tiled=True),
    )
    dealt = (
        lax.all_to_all(
            deal_columns(normed, ctx_count, shard_count),
            "shard",
            split_axis=1,
            concat_axis=0,
            tiled=True,
        ),
        lax.all_to_all(
            deal_columns(attended, ctx_count, shard_count),
            "shard",
            split_axis=1,
            concat_axis=0,
            tiled=True,
        ),
        lax.all_to_all(
            deal_columns(normed_two, ctx_count, shard_count),
            "shard",
            split_axis=1,
            concat_axis=0,
            tiled=True,
        ),
        lax.all_to_all(
            deal_columns(act, ctx_count, shard_count),
            "shard",
            split_axis=1,
            concat_axis=0,
            tiled=True,
        ),
    )
    group_lefts = tuple((part.reshape(part.shape[0], -1) for part in dealt))
    gain_pair = lax.psum(jnp.stack([attn_gain_term, mlp_gain_term]), "shard")
    gain_mine = lax.dynamic_index_in_dim(
        gain_pair.reshape(2, ctx_count, shard_count, own_share),
        lax.axis_index("shard"),
        2,
        keepdims=False,
    ).reshape(2, ctx_count * own_share)
    gain_block = jnp.concatenate(
        [gain_mine.T, jnp.zeros((ctx_count * own_share, 126), jnp.float32)], axis=1
    )
    summed = lax.psum_scatter(
        term_rows(group_lefts, group_rights, gain_block, own_share * lax.axis_size("ctx")).astype(
            jnp.bfloat16
        ),
        "ctx",
        scatter_dimension=0,
        tiled=True,
    ).astype(jnp.float32)
    edge_one = HQ * HD
    edge_two = edge_one + HK * HD
    edge_three = edge_two + HK * HD
    edge_four = edge_three + model_width
    edge_five = edge_four + hidden_width
    edge_six = edge_five + hidden_width
    edge_seven = edge_six + ratio * model_width
    grad_query = summed[:, :edge_one]
    grad_key = summed[:, edge_one:edge_two]
    grad_value = summed[:, edge_two:edge_three]
    grad_out = summed[:, edge_three:edge_four]
    grad_gate = summed[:, edge_four:edge_five]
    grad_up = summed[:, edge_five:edge_six]
    grad_down = summed[:, edge_six:edge_seven].reshape(own_share * ratio, model_width)
    grad_attn_gain = summed[:, edge_seven]
    grad_mlp_gain = summed[:, edge_seven + 1]
    return (
        output,
        grad_input,
        grad_query,
        grad_key,
        grad_value,
        grad_out,
        grad_gate,
        grad_up,
        grad_down,
        grad_attn_gain,
        grad_mlp_gain,
    )


def solution(mesh):
    placed = (
        P("shard", "ctx", None),
        P(None, "shard"),
        P(None, "shard"),
        P(None, "shard"),
        P(None, "shard"),
        P(None, "shard"),
        P(None, "shard"),
        P(None, "shard"),
        P(),
        P(),
        P("shard", None),
        P("shard", None),
        P("shard", "ctx", None),
    )
    return jax.shard_map(
        on_device,
        mesh=mesh,
        in_specs=placed,
        out_specs=(
            P("shard", "ctx", None),
            P("shard", "ctx", None),
            P(("ctx", "shard"), None),
            P(("ctx", "shard"), None),
            P(("ctx", "shard"), None),
            P(("ctx", "shard"), None),
            P(("ctx", "shard"), None),
            P(("ctx", "shard"), None),
            P(("ctx", "shard"), None),
            P(("ctx", "shard")),
            P(("ctx", "shard")),
        ),
        check_vma=False,
    )
```

profile of v0, /device:TPU:0, one launch (start us, length us, event | category | flops | bytes accessed | tf_op | source)
XLA Modules:
  0.0 3169.7 jit_solution(1593208876885877455)
XLA Ops:
  12.4 5.2 fusion.115
  18.6 282.2 %all-gather.17.cloned.1.call-done = bf16[2048,4096]{1,0:T(8,128)(2,1)} async-done(((bf16[2048,1024]{1,0:T(8,128)(2,1)}), bf16[2048,4096]{1,0:T(8,128)(2,1)}) %all-gather.17.cloned.1.call-update) | async-done | bytes 16777232 | tf_op jit(solution)/shard_map/all_gather | solution.py:152
  300.8 22.5 copy.42
  323.3 11.5 fusion.104
  337.4 13.9 pad_maximum_fusion
  365.6 4.4 copy.51
  370.0 23.0 all-gather.21.cloned.1.call-done
  398.3 29.0 while.54
  398.9 5.0 compare_select_fusion.28
  413.5 5.0 compare_select_fusion.28
  428.6 115.5 %all-gather.23.cloned.1.call-done = bf16[2048,2048]{1,0:T(8,128)(2,1)} async-done(((bf16[2048,512]{1,0:T(8,128)(2,1)}), bf16[2048,2048]{1,0:T(8,128)(2,1)}) %all-gather.23.cloned.1.call-update) | async-done | bytes 8388624 | tf_op jit(solution)/shard_map/all_gather | solution.py:205
  544.1 4.8 multiply_reduce_fusion.3
  549.1 1105.3 %all-gather.25.cloned.1.call-done = bf16[2048,16384]{1,0:T(8,128)(2,1)} async-done(((bf16[2048,4096]{1,0:T(8,128)(2,1)}), bf16[2048,16384]{1,0:T(8,128)(2,1)}) %all-gather.25.cloned.1.call-update) | async-done | bytes 67108880 | tf_op jit(solution)/shard_map/all_gather | solution.py:209
  1654.4 33.9 %fusion.124 = f32[128,16384]{1,0:T(8,128)} fusion(bf16[128,2048]{1,0:T(8,128)(2,1)S(1)} %multiply_convert_fusion.5, bf16[2048,16384]{1,0:T(8,128)(2,1)} %all-gather.25.cloned.1.call-done), kind=kOutput, calls=%fused_computation.267 | convolution fusion | flops 8589934592 | bytes 76021760 | tf_op jit(solution)/shard_map/dot_general | solution.py:65
  1688.3 11.2 reshape.596
  1699.5 5.4 fusion.119
  1704.9 5.3 copy.94
  1710.2 5.3 copy.93
  1715.5 499.9 %all-gather.27.cloned.1.call-done = bf16[8192,2048]{1,0:T(8,128)(2,1)} async-done(((bf16[8192,512]{1,0:T(8,128)(2,1)}), bf16[8192,2048]{1,0:T(8,128)(2,1)}) %all-gather.27.cloned.1.call-update) | async-done | bytes 33554448 | tf_op jit(solution)/shard_map/all_gather | solution.py:216
  2215.4 19.2 multiply_convert_fusion.1
  2237.7 4.6 reshape.601
  2242.3 4.1 pad_maximum_fusion.2
  2246.4 4.8 copy.95
  2251.2 30.1 multiply_reduce_fusion
  2282.8 7.3 convolution_convert_fusion.5
  2292.7 6.6 copy.56
  2302.1 29.1 while.55
  2305.2 5.1 compare_select_fusion.29
  2319.6 5.1 compare_select_fusion.29
  2327.2 4.0 fusion.199
  2333.8 8.9 all_gather.64
  2342.7 7.8 reshape.605
  2350.5 8.8 all_gather.66
  2359.4 8.2 reshape.606
  2367.7 58.9 %while.56 = (s32[]{:T(128)}, f32[128,4,256]{0,2,1:T(8,128)}, f32[128,4,256]{0,2,1:T(8,128)S(1)}, bf16[2,512,4,2,256]{4,3,2,1,0:T(2,128)(2,1)}, s32[8]{0:T(128)S(...) while((s32[]{:T(128)}, f32[128,4,256]{0,2,1:T(8,128)}, ...), condition=%wide.region_11.14_spmd.clone, body=%wide.region_10.13_spmd.clone.sunk | while | flops 1078360576 | bytes 38530400 | solution.py:321
  2367.7 6.4 constant_dynamic-slice_fusion.6
  2374.9 5.1 compare_select_fusion.30
  2384.6 4.7 copy.137
  2389.4 5.3 fusion.208
  2397.1 6.4 constant_dynamic-slice_fusion.6
  2404.3 5.1 compare_select_fusion.30
  2414.1 4.7 copy.137
  2418.8 5.4 fusion.208
  2436.8 29.0 all-to-all-done
  2470.9 6.6 reshape.618
  2477.5 6.6 reshape.617
  2484.1 4.2 all-to-all-done.1
  2492.7 5.5 fusion.90
  2500.6 18.3 all-to-all-done.2
  2527.7 60.6 %all-to-all-done.3 = bf16[128,4,2048]{2,0,1:T(8,128)(2,1)S(1)} async-done(((bf16[128,4,2048]{2,0,1:T(8,128)(2,1)}), bf16[128,4,2048]{2,0,1:T(8,128)(2,1)S(1)}, u32[]{:S(2)}, u32[]{:S(2)}) %all-to-all-start.3) | async-done | bytes 2097184 | tf_op jit(solution)/shard_map/all_to_all | solution.py:385
  2588.3 8.5 convolution_convert_fusion.2
  2596.8 14.9 reshape.621
  2611.6 4.3 convolution_convert_fusion.4
  2616.0 4.3 convolution_convert_fusion.3
  2620.3 12.5 fusion.99
  2632.9 18.3 psum.7
  2657.3 80.9 %all-gather.41.cloned.1.call-done = bf16[512,8192]{1,0:T(8,128)(2,1)} async-done(((bf16[128,8192]{1,0:T(8,128)(2,1)}), bf16[512,8192]{1,0:T(8,128)(2,1)}) %all-gather.41.cloned.1.call-update) | async-done | bytes 8388624 | tf_op jit(solution)/shard_map/all_gather | solution.py:359
  2738.3 10.1 convolution_convert_fusion.1
  2748.3 139.3 %all-gather.43.cloned.1.call-done = bf16[512,8192]{1,0:T(8,128)(2,1)} async-done(((bf16[128,8192]{1,0:T(8,128)(2,1)}), bf16[512,8192]{1,0:T(8,128)(2,1)}) %all-gather.43.cloned.1.call-update) | async-done | bytes 8388624 | tf_op jit(solution)/shard_map/all_gather | solution.py:360
  2887.6 10.1 convolution_convert_fusion
  2897.7 45.8 %concatenate.48 = bf16[512,30848]{1,0:T(8,128)(2,1)} concatenate(bf16[512,2048]{1,0:T(8,128)(2,1)S(1)} %copy-done.30, bf16[512,1024]{1,0:T(8,128)(2,1)} %convolution_convert_fusion.7, bf16[512,1024]{1,0:T(8,128)(2,1)} %convolution_convert_fusion.6, bf16[512,2048]{1,0:T(8,128)(2,1)} %convolution_convert_fusion.3, bf16[512,8192]{1,0:T(8,128)(2,1)} %convolution_convert_fusion.1, ...), dimensions={1} | concatenate | bytes 63176704 | tf_op jit(solution)/shard_map/concatenate | solution.py:91
  2944.8 23.3 fusion.88
  2970.5 179.0 %reduce-scatter.2.cloned.1.call-done = bf16[64,30848]{1,0:T(8,128)(2,1)} async-done(((bf16[512,30848]{1,0:T(8,128)(2,1)}), bf16[64,30848]{1,0:T(8,128)(2,1)}) %reduce-scatter.2.cloned.1.call-update) | async-done | bytes 3948560 | tf_op jit(solution)/shard_map/reduce_scatter | solution.py:404
  3149.5 4.6 fusion.120
  (295 shorter events, 140.5 us)
Async XLA Ops:
  7.2 293.6 %all-gather.17.cloned.1.call-start = ((), (), s32[]{:S(2)}) async-start(), calls=%async_computation.5 | async-start | bytes 20971520 | tf_op jit(solution)/shard_map/all_gather | solution.py:152
  11.1 6.5 copy-start.8
  11.1 351.2 %all-gather.19.cloned.1.call-start = ((), (), s32[]{:S(2)}) async-start(), calls=%async_computation.6 | async-start | bytes 2359296 | tf_op jit(solution)/shard_map/all_gather | solution.py:174
  18.3 305.1 %copy-start.51 = (f32[128]{0:T(128)}, f32[128]{0:T(128)S(1)}, u32[]{:S(2)}) copy-start(f32[128]{0:T(128)S(1)} %get-tuple-element.1212) | copy-start | bytes 1540
  18.6 333.4 %copy-start.38 = (f32[128,128]{1,0:T(8,128)}, f32[128,128]{1,0:T(8,128)S(1)}, u32[]{:S(2)}) copy-start(f32[128,128]{1,0:T(8,128)S(1)} %get-tuple-element.1210) | copy-start | bytes 196612
  18.6 333.5 %copy-start.36 = (f32[128,128]{1,0:T(8,128)}, f32[128,128]{1,0:T(8,128)S(1)}, u32[]{:S(2)}) copy-start(f32[128,128]{1,0:T(8,128)S(1)} %get-tuple-element.1209) | copy-start | bytes 196612
  300.8 22.5 copy-start.48
  335.8 57.2 %all-gather.21.cloned.1.call-start = ((), (), s32[]{:S(2)}) async-start(), calls=%async_computation.7 | async-start | bytes 2359296 | tf_op jit(solution)/shard_map/all_gather | solution.py:175
  335.9 15.4 copy-start.26
  336.8 207.3 %all-gather.23.cloned.1.call-start = ((), (), s32[]{:S(2)}) async-start(), calls=%async_computation.8 | async-start | bytes 10485760 | tf_op jit(solution)/shard_map/all_gather | solution.py:205
  337.4 1317.0 %all-gather.25.cloned.1.call-start = ((), (), s32[]{:S(2)}) async-start(), calls=%async_computation.9 | async-start | bytes 83886080 | tf_op jit(solution)/shard_map/all_gather | solution.py:209
  351.4 1864.1 %all-gather.27.cloned.1.call-start = ((), (), s32[]{:S(2)}) async-start(), calls=%async_computation.10 | async-start | bytes 41943040 | tf_op jit(solution)/shard_map/all_gather | solution.py:216
  351.9 1990.8 %all-gather.29.cloned.1.call-start = ((), (), s32[]{:S(2)}) async-start(), calls=%async_computation.11 | async-start | bytes 4718592 | tf_op jit(solution)/shard_map/all_gather | solution.py:326
  352.1 3.8 copy-start.42
  352.2 3.7 copy-start.44
  360.8 1998.6 %all-gather.31.cloned.1.call-start = ((), (), s32[]{:S(2)}) async-start(), calls=%async_computation.12 | async-start | bytes 4718592 | tf_op jit(solution)/shard_map/all_gather | solution.py:327
  365.6 4.4 copy-start.5
  396.3 1.9 copy-start.7
  428.6 120.2 %copy-start.15 = (bf16[128,4,2,256]{0,3,2,1:T(8,128)(2,1)}, bf16[128,4,2,256]{0,3,2,1:T(8,128)(2,1)S(1)}, u32[]{:S(2)}) copy-start(bf16[128,4,2,256]{0,3,2,1:T(8,128)(2,1)S(1)} %fusion.110) | copy-start | bytes 1572868
  544.1 4.8 copy-start.50
  548.9 1732.5 %copy-start.10 = (f32[128,2048]{1,0:T(8,128)}, f32[128,2048]{1,0:T(8,128)S(1)}, u32[]{:S(2)}) copy-start(f32[128,2048]{1,0:T(8,128)S(1)} %get-tuple-element.1224) | copy-start | bytes 3145732
  549.1 1139.2 %copy-start.17 = (bf16[128,2048]{1,0:T(8,128)(2,1)}, bf16[128,2048]{1,0:T(8,128)(2,1)S(1)}, u32[]{:S(2)}) copy-start(bf16[128,2048]{1,0:T(8,128)(2,1)S(1)} %multiply_convert_fusion.5) | copy-start | bytes 1572868
  1704.9 5.3 copy-start.3
  1704.9 5.3 copy-start.2
  2234.6 3.0 copy-start.13
  2237.7 4.6 copy-start.14
  2251.2 30.2 copy-start.31
  2282.8 7.3 copy-start.19
  2282.8 8.2 copy-start.6
  2290.2 237.5 %all-gather.45.cloned.1.call-start = ((), (), s32[]{:S(2)}) async-start(), calls=%async_computation.20 | async-start | bytes 2621440 | tf_op jit(solution)/shard_map/all_gather | solution.py:361
  2290.9 320.7 %all-gather.33.cloned.1.call-start = ((), (), s32[]{:S(2)}) async-start(), calls=%async_computation.13 | async-start | bytes 2621440 | tf_op jit(solution)/shard_map/all_gather | solution.py:355
  2292.7 6.6 copy-start.20
  2299.3 2.6 copy-start.25
  2302.1 2.1 copy-start.4
  2316.4 2.1 copy-start.4
  2331.1 1.4 copy-start.43
  2331.1 1.4 copy-start.45
  2333.5 282.4 %all-gather.39.cloned.1.call-start = ((), (), s32[]{:S(2)}) async-start(), calls=%async_computation.16 | async-start | bytes 2621440 | tf_op jit(solution)/shard_map/all_gather | solution.py:358
  2359.4 8.3 copy-start.41
  2359.4 292.0 %all-gather.35.cloned.1.call-start = ((), (), s32[]{:S(2)}) async-start(), calls=%async_computation.14 | async-start | bytes 1310720 | tf_op jit(solution)/shard_map/all_gather | solution.py:356
  2374.1 10.5 copy-start.1
  2403.5 10.5 copy-start.1
  2426.6 1.4 copy-start.37
  2426.6 1.4 copy-start.39
  2429.0 225.3 %all-gather.37.cloned.1.call-start = ((), (), s32[]{:S(2)}) async-start(), calls=%async_computation.15 | async-start | bytes 1310720 | tf_op jit(solution)/shard_map/all_gather | solution.py:357
  2429.8 308.4 %all-gather.41.cloned.1.call-start = ((), (), s32[]{:S(2)}) async-start(), calls=%async_computation.17 | async-start | bytes 10485760 | tf_op jit(solution)/shard_map/all_gather | solution.py:359
  2430.4 457.2 %all-gather.43.cloned.1.call-start = ((), (), s32[]{:S(2)}) async-start(), calls=%async_computation.18 | async-start | bytes 10485760 | tf_op jit(solution)/shard_map/all_gather | solution.py:360
  2431.2 4.8 copy-start.16
  2431.7 38.1 %copy-start.18 = (bf16[128,2048]{1,0:T(8,128)(2,1)S(1)}, bf16[128,2048]{1,0:T(8,128)(2,1)}, u32[]{:S(2)}) copy-start(bf16[128,2048]{1,0:T(8,128)(2,1)} %copy-done.17) | copy-start | bytes 1572868
  2432.5 33.3 %all-to-all-start = ((bf16[128,4,512]{0,2,1:T(8,128)(2,1)}), bf16[128,4,512]{0,2,1:T(8,128)(2,1)S(1)}, u32[]{:S(2)}, u32[]{:S(2)}) async-start(bf16[128,4,512]{0,2,1:T(8,128)(2,1)} %bitcast.34), calls=%async_computation | async-start | bytes 1048576 | tf_op jit(solution)/shard_map/all_to_all | solution.py:364
  2465.8 11.6 copy-start.32
  2465.8 22.4 all-to-all-start.1
  2489.1 29.8 all-to-all-start.2
  2500.6 22.8 copy-start.33
  2519.7 68.6 %all-to-all-start.3 = ((bf16[128,4,2048]{2,0,1:T(8,128)(2,1)}), bf16[128,4,2048]{2,0,1:T(8,128)(2,1)S(1)}, u32[]{:S(2)}, u32[]{:S(2)}) async-start(bf16[128,4,2048]{2,0,1:T(8,128)(2,1)} %reshape.619), calls=%async_computation.3 | async-start | bytes 4194304 | tf_op jit(solution)/shard_map/all_to_all | solution.py:385
  2523.3 626.2 %reduce-scatter.2.cloned.1.call-start = ((), (), s32[]{:S(2)}) async-start(), calls=%async_computation.19 | async-start | bytes 35536896 | tf_op jit(solution)/shard_map/reduce_scatter | solution.py:404
  2596.8 14.9 copy-start.46
  2611.6 4.3 copy-start.47
  2615.9 4.3 copy-start.21
  2615.9 4.3 copy-start.28
  2615.9 4.3 copy-start.29
  2748.3 149.4 %copy-start.30 = (bf16[512,2048]{1,0:T(8,128)(2,1)S(1)}, bf16[512,2048]{1,0:T(8,128)(2,1)}, u32[]{:S(2)}) copy-start(bf16[512,2048]{1,0:T(8,128)(2,1)} %convolution_convert_fusion.4) | copy-start | bytes 6291460
  2944.8 23.3 copy-start.22
  2944.8 23.3 copy-start.53
  (14 other events, 13.8 us)
Sparse Core Ops, SparseCore 0:
  11.2 289.5 all-gather.16
  335.9 26.3 all-gather.18
  364.8 28.1 all-gather.20
  394.4 149.6 all-gather.22
  545.5 1108.8 all-gather.24
  1655.8 559.5 all-gather.26
  2217.9 34.8 all-gather.28
  2290.3 35.6 all-gather.30
  2327.6 45.9 all-gather.44
  2375.5 44.9 all-gather.32
  2422.1 64.4 all-gather.38
  2488.6 50.7 all-gather.34
  2541.5 44.3 all-gather.36
  2588.0 150.2 all-gather.40
  2739.7 147.8 all-gather.42
  2943.7 205.7 reduce-scatter.1
where the time goes:
time: 3180 us; the launch traced here: 3170 us
  waiting for transfers between devices  2540 us (80%)
  local copies, waits for them, and re-layouts  257 us (8%)
  matrix products  225 us (7%)
  other arithmetic  79.6 us (3%)
  blocking collectives  36 us (1%)
    all_gather x1, waiting for transfers between devices, on_device(): lax.all_gather(stack_mlp, 'shard', axis=1, tiled=True)  1110 us
    all_gather x1, waiting for transfers between devices, on_device(): lax.all_gather(w_down, 'shard', axis=1, tiled=True)  500 us
    all_gather x1, waiting for transfers between devices, on_device(): lax.all_gather(stack_qkv, 'shard', axis=1, tiled=True)  282 us
    reduce_scatter x1, waiting for transfers between devices, on_device(): lax.psum_scatter(term_rows(group_lefts, group_rights, gain_block, own_sha...  179 us
    all_gather x1, waiting for transfers between devices, on_device(): lax.all_gather(rights[5], 'shard', axis=0, tiled=True)  139 us
    all_gather x1, waiting for transfers between devices, on_device(): lax.all_gather(w_out, 'shard', axis=1, tiled=True)  115 us
    all_gather x1, waiting for transfers between devices, on_device(): lax.all_gather(rights[4], 'shard', axis=0, tiled=True)  80.9 us
    dot_general x4, matrix products, write_columns(): made = jnp.dot(left, piece, preferred_element_type=jnp.float32)  73.4 us
  transfers between devices with their start and end apart: 20, of which 13 were waited for; matrix products, arithmetic and copies ran while one was open for 14% of the time, Pallas kernels for 0%

commit v1 on v0

--- a/solution.py
+++ b/solution.py
@@ -1,8 +1,11 @@
+import functools
 import math
 
 import jax
 import jax.numpy as jnp
 from jax import lax
+from jax.experimental import pallas as pl
+from jax.experimental.pallas import tpu as pltpu
 from jax.sharding import PartitionSpec as P
 
 HQ = 8
@@ -440,6 +443,439 @@
     )
 
 
+BF16 = jnp.bfloat16
+F32 = jnp.float32
+VISIBLE_ROWS = 256
+
+
+def dot_nn(a, b):
+    return jnp.dot(a, b, preferred_element_type=F32)
+
+
+def dot_nt(a, b):
+    return lax.dot_general(a, b, (((1,), (1,)), ((), ())), preferred_element_type=F32)
+
+
+def dot_tn(a, b):
+    return lax.dot_general(a, b, (((0,), (0,)), ((), ())), preferred_element_type=F32)
+
+
+def scores_of(query, key, code, low_code, key_code):
+    scores = dot_nt(query, key) * SCORE_SCALE
+    mask = (key_code <= code) & (key_code >= low_code)
+    return jnp.where(mask, scores, MASKED)
+
+
+def attend_kernel(query, key, value, code, low_code, key_code, attended, log_total):
+    scores = scores_of(query[...], key[...], code[...], low_code[...], key_code[...])
+    top = jnp.max(scores, axis=-1, keepdims=True)
+    weights = jnp.exp(scores - top)
+    total = jnp.sum(weights, axis=-1, keepdims=True)
+    mixed = dot_nn(weights.astype(BF16), value[...])
+    attended[...] = (mixed / total).astype(BF16)
+    log_total[...] = top + jnp.log(total)
+
+
+def attend(query, key, value, code, low_code, key_code):
+    rows, head = query.shape
+    step = math.gcd(rows, VISIBLE_ROWS)
+    by_row = lambda width: pl.BlockSpec((step, width), lambda i: (i, 0))
+    whole = lambda shape: pl.BlockSpec(shape, lambda i: (0, 0))
+    return pl.pallas_call(
+        attend_kernel,
+        grid=(rows // step,),
+        in_specs=[
+            by_row(head),
+            whole(key.shape),
+            whole(value.shape),
+            by_row(1),
+            by_row(1),
+            whole(key_code.shape),
+        ],
+        out_specs=[by_row(head), by_row(1)],
+        out_shape=[
+            jax.ShapeDtypeStruct((rows, head), BF16),
+            jax.ShapeDtypeStruct((rows, 1), F32),
+        ],
+        compiler_params=pltpu.CompilerParams(vmem_limit_bytes=32 << 20),
+        cost_estimate=pl.CostEstimate(
+            flops=4 * rows * key.shape[0] * head,
+            bytes_accessed=8 * rows * head,
+            transcendentals=rows * key.shape[0],
+        ),
+    )(query, key, value, code, low_code, key_code)
+
+
+def attend_back_kernel(
+    query, outgrad, key, value, log_total, code, low_code, key_code, d_query, d_key, d_value
+):
+    @pl.when(pl.program_id(0) == 0)
+    def _():
+        d_key[...] = jnp.zeros_like(d_key)
+        d_value[...] = jnp.zeros_like(d_value)
+
+    scores = scores_of(query[...], key[...], code[...], low_code[...], key_code[...])
+    probs = jnp.exp(scores - log_total[...])
+    prob_grad = dot_nt(outgrad[...], value[...])
+    delta = jnp.sum(probs * prob_grad, axis=-1, keepdims=True)
+    score_grad = (probs * (prob_grad - delta)).astype(BF16)
+    d_query[...] = dot_nn(score_grad, key[...]) * SCORE_SCALE
+    d_key[...] += dot_tn(score_grad, query[...]) * SCORE_SCALE
+    d_value[...] += dot_tn(probs.astype(BF16), outgrad[...])
+
+
+def attend_back(query, outgrad, key, value, log_total, code, low_code, key_code):
+    rows, head = query.shape
+    step = math.gcd(rows, VISIBLE_ROWS)
+    by_row = lambda width: pl.BlockSpec((step, width), lambda i: (i, 0))
+    whole = lambda shape: pl.BlockSpec(shape, lambda i: (0, 0))
+    return pl.pallas_call(
+        attend_back_kernel,
+        grid=(rows // step,),
+        in_specs=[
+            by_row(head),
+            by_row(head),
+            whole(key.shape),
+            whole(value.shape),
+            by_row(1),
+            by_row(1),
+            by_row(1),
+            whole(key_code.shape),
+        ],
+        out_specs=[by_row(head), whole(key.shape), whole(value.shape)],
+        out_shape=[
+            jax.ShapeDtypeStruct((rows, head), F32),
+            jax.ShapeDtypeStruct(key.shape, F32),
+            jax.ShapeDtypeStruct(value.shape, F32),
+        ],
+        compiler_params=pltpu.CompilerParams(vmem_limit_bytes=40 << 20),
+        cost_estimate=pl.CostEstimate(
+            flops=10 * rows * key.shape[0] * head,
+            bytes_accessed=20 * rows * head,
+            transcendentals=rows * key.shape[0],
+        ),
+    )(query, outgrad, key, value, log_total, code, low_code, key_code)
+
+
+def rotate_head(values, cosine, sine):
+    half = values.shape[-1] // 2
+    first, second = values[:, :half], values[:, half:]
+    return jnp.concatenate([first * cosine - second * sine, second * cosine + first * sine], axis=1)
+
+
+def swap_halves(values):
+    half = values.shape[0] // 2
+    return jnp.concatenate([values[half:], values[:half]], axis=0)
+
+
+def index_of(stacked, i):
+    return lax.dynamic_index_in_dim(stacked, i, 0, keepdims=False)
+
+
+def cut(values, starts, sizes):
+    return lax.dynamic_slice(values, starts, sizes)
+
+
+def on_device_by_head(
+    layer_input,
+    w_query,
+    w_key,
+    w_value,
+    w_out,
+    w_gate,
+    w_up,
+    w_down,
+    attn_gain,
+    mlp_gain,
+    block_pairs,
+    doc_ids,
+    cotangent,
+):
+    tok_rows, width = layer_input.shape[1:]
+    planes = lax.axis_size("shard")
+    ctx_count = lax.axis_size("ctx")
+    chips = ctx_count // 2
+    ctx, plane = lax.axis_index("ctx"), lax.axis_index("shard")
+    chip, core = ctx // 2, ctx % 2
+    first_core = core == 0
+    seq_rows = tok_rows * ctx_count
+    half_seq = seq_rows // 2
+    group_rows = tok_rows * planes
+    shard_width = w_down.shape[1]
+    hidden_plane = w_gate.shape[1]
+    hidden = hidden_plane // 2
+    own_share = width // (planes * ctx_count)
+
+    def over_z(values, d):
+        return lax.ppermute(values, "shard", [(i, i ^ d) for i in range(planes)])
+
+    def over_chips(values, d):
+        return lax.ppermute(values, "ctx", [(i, i ^ (2 * d)) for i in range(ctx_count)])
+
+    def sibling(values):
+        return lax.ppermute(values, "ctx", [(i, i ^ 1) for i in range(ctx_count)])
+
+    z_steps = range(1, planes)
+    chip_steps = range(1, chips)
+
+    def gather_z(values):
+        return [values] + [over_z(values, d) for d in z_steps]
+
+    def gather_chips(values):
+        return [values] + [over_chips(values, d) for d in chip_steps]
+
+    def gather_seq(values):
+        mine = jnp.concatenate(gather_chips(values), axis=0)
+        return jnp.concatenate([mine, sibling(mine)], axis=0)
+
+    def gather_group(values):
+        mine = jnp.concatenate(gather_z(values), axis=0)
+        return jnp.concatenate([mine, sibling(mine)], axis=0)
+
+    def sum_chips(block_of):
+        total = block_of(0)
+        for d in chip_steps:
+            total = total + over_chips(block_of(d).astype(BF16), d).astype(F32)
+        return total
+
+    def sum_z(block_of):
+        total = block_of(0)
+        for d in z_steps:
+            total = total + over_z(block_of(d).astype(BF16), d).astype(F32)
+        return total
+
+    quarter = width // chips
+    head_block = jnp.concatenate(
+        [
+            cut(w_query, (quarter * chip, HD * core), (quarter, HD)),
+            jnp.where(
+                first_core,
+                cut(w_key, (quarter * chip, 0), (quarter, HD)),
+                cut(w_value, (quarter * chip, 0), (quarter, HD)),
+            ),
+        ],
+        axis=1,
+    )
+    head_parts = jnp.stack(gather_z(head_block))
+    w_head = jnp.zeros((width, 2 * HD), BF16)
+    for d in range(chips):
+        part = index_of(head_parts, plane ^ chip ^ d)
+        if d:
+            part = over_chips(part, d)
+        w_head = lax.dynamic_update_slice(w_head, part, (quarter * (chip ^ d), 0))
+
+    inputs_low = layer_input[0]
+    inputs = inputs_low.astype(F32)
+    all_inputs = gather_seq(inputs_low).astype(F32)
+    pairs, documents = block_pairs[0], doc_ids[0]
+    order = jnp.stack([(chip ^ d) * 2 + (core ^ e) for e in range(2) for d in range(chips)])
+    rows = (order[:, None] * tok_rows + jnp.arange(tok_rows, dtype=jnp.int32)[None, :]).reshape(-1)
+    positions = position_of(rows, pairs, tok_rows, 2 * ctx_count).astype(jnp.int32)
+    span = 2 * seq_rows
+    doc_first = jnp.take(documents, positions).astype(jnp.int32) * span
+    code = doc_first + positions
+    low_code = jnp.maximum(doc_first, code - (WINDOW - 1))
+    code_column, low_column, code_row = code[:, None], low_code[:, None], code[None, :]
+    cosine, sine = rope_tables(positions, HD)
+
+    factor_all = lax.rsqrt(jnp.mean(all_inputs * all_inputs, axis=-1, keepdims=True) + EPSILON)
+    normed_all = (all_inputs * factor_all * attn_gain).astype(BF16)
+    projected = dot_nn(normed_all, w_head)
+    query = rotate_head(projected[:, :HD], cosine, sine).astype(BF16)
+    key_cosine = jnp.where(first_core, cosine, 1.0)
+    key_sine = jnp.where(first_core, sine, 0.0)
+    mine_kv = rotate_head(projected[:, HD:], key_cosine, key_sine).astype(BF16)
+    other_kv = swap_halves(sibling(mine_kv))
+    key = jnp.where(first_core, mine_kv, other_kv)
+    value = jnp.where(first_core, other_kv, mine_kv)
+    attended, log_total = attend(query, key, value, code_column, low_column, code_row)
+
+    out_rows = jnp.zeros((HD, width), BF16)
+    for d, part in enumerate(gather_z(cut(w_out, (HD * ctx, 0), (HD, shard_width)))):
+        out_rows = lax.dynamic_update_slice(out_rows, part, (0, shard_width * (plane ^ d)))
+    out_pair = jnp.concatenate([out_rows, sibling(out_rows)], axis=0)
+    attended_pair = jnp.concatenate([attended[:half_seq], sibling(attended[half_seq:])], axis=1)
+    branch_parts = dot_nn(attended_pair, out_pair).reshape(chips, tok_rows, width)
+    mid = inputs + sum_chips(lambda d: branch_parts[d])
+    factor_two = lax.rsqrt(jnp.mean(mid * mid, axis=-1, keepdims=True) + EPSILON)
+    normed_two = (mid * factor_two * mlp_gain).astype(BF16)
+    normed_group = gather_group(normed_two)
+
+    quarter_hidden = hidden // chips
+    down_block = jnp.zeros((quarter_hidden, width), BF16)
+    for d in range(planes):
+        start = hidden_plane * (plane ^ d) + hidden * core + quarter_hidden * chip
+        part = cut(w_down, (start, 0), (quarter_hidden, shard_width))
+        if d:
+            part = over_z(part, d)
+        down_block = lax.dynamic_update_slice(down_block, part, (0, shard_width * (plane ^ d)))
+    down_rows = jnp.zeros((hidden, width), BF16)
+    for d, part in enumerate(gather_chips(down_block)):
+        down_rows = lax.dynamic_update_slice(down_rows, part, (quarter_hidden * (chip ^ d), 0))
+
+    upstream_low = cotangent[0]
+    upstream = upstream_low.astype(F32)
+    upstream_group = gather_group(upstream_low)
+    act_grad = dot_nt(upstream_group, down_rows)
+    gate_cols = cut(w_gate, (0, hidden * core), (width, hidden))
+    up_cols = cut(w_up, (0, hidden * core), (width, hidden))
+    gate = dot_nn(normed_group, gate_cols)
+    up_lin = dot_nn(normed_group, up_cols)
+    sigma = jax.nn.sigmoid(gate)
+    swish = gate * sigma
+    act = (swish * up_lin).astype(BF16)
+    gate_grad = (act_grad * up_lin * (sigma * (1.0 + gate * (1.0 - sigma)))).astype(BF16)
+    up_grad = (act_grad * swish).astype(BF16)
+
+    def back_to_tokens(partial):
+        low = partial.astype(BF16)
+        pair = partial[:group_rows] + sibling(low[group_rows:]).astype(F32)
+        blocks = pair.reshape(planes, tok_rows, width)
+        return sum_z(lambda d: blocks[d])
+
+    norm_two_grad = back_to_tokens(dot_nt(gate_grad, gate_cols) + dot_nt(up_grad, up_cols))
+    mlp_gain_term = jnp.sum(norm_two_grad * mid * factor_two, axis=0)
+    scaled_two = norm_two_grad * mlp_gain
+    mid_grad = (
+        upstream
+        + factor_two * scaled_two
+        - mid * factor_two**3 * jnp.mean(scaled_two * mid, axis=-1, keepdims=True)
+    )
+    branch_grad_all = gather_seq(mid_grad.astype(BF16))
+    output = (mid + back_to_tokens(dot_nn(act, down_rows))).astype(BF16)[None]
+
+    attended_grad = dot_nt(branch_grad_all, out_rows).astype(BF16)
+    d_query, d_key, d_value = attend_back(
+        query, attended_grad, key, value, log_total, code_column, low_column, code_row
+    )
+    keep = jnp.where(first_core, d_key, d_value)
+    give = jnp.where(first_core, d_value, d_key)
+    d_kv = keep + swap_halves(sibling(give))
+    d_head = jnp.concatenate(
+        [rotate_head(d_query, cosine, -sine), rotate_head(d_kv, key_cosine, -key_sine)], axis=1
+    ).astype(BF16)
+    d_head_pair = jnp.concatenate([d_head[:half_seq], sibling(d_head[half_seq:])], axis=1)
+    w_head_pair = jnp.concatenate([w_head, sibling(w_head)], axis=1)
+    normed_parts = dot_nt(d_head_pair, w_head_pair).reshape(chips, tok_rows, width)
+    normed_grad = sum_chips(lambda d: normed_parts[d])
+    factor_one = factor_all[:tok_rows]
+    attn_gain_term = jnp.sum(normed_grad * inputs * factor_one, axis=0)
+    scaled_one = normed_grad * attn_gain
+    grad_input = (
+        mid_grad
+        + factor_one * scaled_one
+        - inputs * factor_one**3 * jnp.mean(scaled_one * inputs, axis=-1, keepdims=True)
+    ).astype(BF16)[None]
+
+    mlp_grads = jnp.concatenate([gate_grad, up_grad], axis=1)
+
+    def mlp_rows(d):
+        left = cut(normed_group, (0, quarter * (chip ^ d)), (2 * group_rows, quarter))
+        return dot_tn(left, mlp_grads)
+
+    mlp_sum = sum_chips(mlp_rows).astype(BF16).reshape(2, quarter // 2, 2 * hidden)
+    mlp_mine = index_of(mlp_sum, core)
+    mlp_other = sibling(index_of(mlp_sum, 1 - core))
+    left_half = jnp.where(first_core, mlp_mine, mlp_other)
+    right_half = jnp.where(first_core, mlp_other, mlp_mine)
+    mlp_rows_all = jnp.concatenate(
+        [left_half[:, :hidden], right_half[:, :hidden], left_half[:, hidden:], right_half[:, hidden:]],
+        axis=1,
+    ).reshape(planes, own_share, 2 * hidden_plane)
+    grad_gate = jnp.zeros((own_share, planes * hidden_plane), F32)
+    grad_up = jnp.zeros((own_share, planes * hidden_plane), F32)
+    for d in range(planes):
+        part = index_of(mlp_rows_all, plane ^ d)
+        if d:
+            part = over_z(part, d)
+        part = part.astype(F32)
+        at = (0, hidden_plane * (plane ^ d))
+        grad_gate = lax.dynamic_update_slice(grad_gate, part[:, :hidden_plane], at)
+        grad_up = lax.dynamic_update_slice(grad_up, part[:, hidden_plane:], at)
+
+    down_terms = dot_tn(act, upstream_group).reshape(planes, chips, -1, width)
+    down_sum = sum_chips(
+        lambda d: lax.dynamic_index_in_dim(down_terms, chip ^ d, 1, keepdims=False)
+    ).astype(BF16)
+    down_parts = []
+    for d in range(planes):
+        part = index_of(down_sum, plane ^ d)
+        down_parts.append(over_z(part, d) if d else part)
+    down_parts = jnp.stack(down_parts)
+    share = down_parts.shape[1]
+    grad_down = jnp.zeros((chips * share, width), F32)
+    for d in range(chips):
+        part = index_of(down_parts, plane ^ chip ^ d)
+        if d:
+            part = over_chips(part, d)
+        grad_down = lax.dynamic_update_slice(grad_down, part.astype(F32), (share * (chip ^ d), 0))
+
+    out_terms = dot_tn(attended, branch_grad_all).reshape(planes, own_share, width)
+    grad_out = sum_z(lambda d: index_of(out_terms, plane ^ d))
+
+    head_terms = dot_tn(normed_all, d_head).reshape(ctx_count, planes, own_share, 2 * HD)
+    head_sum = sum_z(
+        lambda d: lax.dynamic_index_in_dim(head_terms, plane ^ d, 1, keepdims=False)
+    ).astype(BF16)
+    head_sum = head_sum.reshape(chips, 2, own_share, 2 * HD)
+    head_mine = lax.dynamic_index_in_dim(head_sum, core, 1, keepdims=False)
+    head_other = sibling(lax.dynamic_index_in_dim(head_sum, 1 - core, 1, keepdims=False))
+    left_half = jnp.where(first_core, head_mine, head_other)
+    right_half = jnp.where(first_core, head_other, head_mine)
+    head_rows = jnp.concatenate(
+        [left_half[..., :HD], right_half[..., :HD], left_half[..., HD:], right_half[..., HD:]], axis=2
+    )
+    grad_query = jnp.zeros((own_share, HQ * HD), F32)
+    grad_key = jnp.zeros((own_share, HK * HD), F32)
+    grad_value = jnp.zeros((own_share, HK * HD), F32)
+    for d in range(chips):
+        part = index_of(head_rows, chip ^ d)
+        if d:
+            part = over_chips(part, d)
+        part = part.astype(F32)
+        grad_query = lax.dynamic_update_slice(grad_query, part[:, : 2 * HD], (0, 2 * HD * (chip ^ d)))
+        grad_key = lax.dynamic_update_slice(grad_key, part[:, 2 * HD : 3 * HD], (0, HD * (chip ^ d)))
+        grad_value = lax.dynamic_update_slice(grad_value, part[:, 3 * HD :], (0, HD * (chip ^ d)))
+
+    gains = jnp.stack([attn_gain_term, mlp_gain_term]).reshape(2, ctx_count, planes, own_share)
+
+    def gain_block(d):
+        return lax.dynamic_index_in_dim(gains, plane ^ d, 2, keepdims=False)
+
+    gain_sum = gain_block(0)
+    for d in z_steps:
+        gain_sum = gain_sum + over_z(gain_block(d), d)
+    gain_sum = gain_sum.reshape(2, chips, 2, own_share)
+    gain_sum = lax.dynamic_index_in_dim(gain_sum, core, 2, keepdims=False) + sibling(
+        lax.dynamic_index_in_dim(gain_sum, 1 - core, 2, keepdims=False)
+    )
+    gain_mine = lax.dynamic_index_in_dim(gain_sum, chip, 1, keepdims=False)
+    for d in chip_steps:
+        gain_mine = gain_mine + over_chips(
+            lax.dynamic_index_in_dim(gain_sum, chip ^ d, 1, keepdims=False), d
+        )
+    return (
+        output,
+        grad_input,
+        grad_query,
+        grad_key,
+        grad_value,
+        grad_out,
+        grad_gate,
+        grad_up,
+        grad_down,
+        gain_mine[0],
+        gain_mine[1],
+    )
+
+
+def plan_of(mesh):
+    chips, planes = mesh.shape["ctx"] // 2, mesh.shape["shard"]
+    if mesh.shape["ctx"] == HQ and HQ == 2 * HK and chips == planes == HK:
+        return on_device_by_head
+    return on_device
+
+
 def solution(mesh):
     placed = (
         P("shard", "ctx", None),
@@ -457,7 +893,7 @@
         P("shard", "ctx", None),
     )
     return jax.shard_map(
-        on_device,
+        plan_of(mesh),
         mesh=mesh,
         in_specs=placed,
         out_specs=(

time: 3180 us -> 764 us (0.24)
  waiting for transfers between devices: 2540 us -> 368 us
  local copies, waits for them, and re-layouts: 257 us -> 59.2 us
  starting transfers between devices: 15.5 us -> 161 us
  matrix products: 225 us -> 104 us
  blocking collectives: 36 us -> 0 us
    all_gather x15 -> x0, waiting for transfers between devices: 2250 us -> none  [the longest x1 1110 us: on_device(): lax.all_gather(stack_mlp, 'shard', axis=1, tiled=True)]
    ppermute x0 -> x84, waiting for transfers between devices: none -> 368 us  [the longest x36 201 us: over_z(): return lax.ppermute(values, 'shard', [(i, i ^ d) for i in range(planes)])]
    reduce_scatter x1 -> x0, waiting for transfers between devices: 179 us -> none  [on_device(): lax.psum_scatter(term_rows(group_lefts, group_rights, gain_block, own_sha...]
    ppermute x0 -> x84, starting transfers between devices: none -> 161 us  [the longest x36 118 us: over_z(): return lax.ppermute(values, 'shard', [(i, i ^ d) for i in range(planes)])]
    dot_general x29 -> x17, matrix products: 225 us -> 104 us  [the longest x5 36.7 us: dot_nt(): lax.dot_general(a, b, (((1,), (1,)), ((), ())), preferred_element_type=F32)]
    all_to_all x4 -> x0, waiting for transfers between devices: 112 us -> none  [the longest x1 60.6 us: on_device(): lax.all_to_all(deal_columns(act, ctx_count, shard_count), 'shard', split_...]
    reshape x15 -> x0, local copies, waits for them, and re-layouts: 76.2 us -> none  [the longest x1 14.9 us: term_rows(): down_part = outer_sum(act_all, upstream_g).reshape(count, -1)]
    concatenate x3 -> x4, local copies, waits for them, and re-layouts: 46.2 us -> 3.64 us  [the longest x2 1.87 us: gather_seq(): return jnp.concatenate([mine, sibling(mine)], axis=0)]
  transfers between devices with their start and end apart: 20 -> 84, of which waited for: 13 -> 30; matrix products, arithmetic and copies ran while one was open for 14% -> 21% of each run, Pallas kernels for 0% -> 1%
where the time goes in v1:
time: 764 us; the launch traced here: 754 us
  waiting for transfers between devices  368 us (48%)
  starting transfers between devices  161 us (21%)
  matrix products  104 us (14%)
  local copies, waits for them, and re-layouts  59.2 us (8%)
  other arithmetic  49.7 us (7%)
  Pallas kernels  9.78 us (1%)
    ppermute x36, waiting for transfers between devices, over_z(): return lax.ppermute(values, 'shard', [(i, i ^ d) for i in range(planes)])  201 us
    ppermute x33, waiting for transfers between devices, over_chips(): lax.ppermute(values, 'ctx', [(i, i ^ 2 * d) for i in range(ctx_count)])  166 us
    ppermute x36, starting transfers between devices, over_z(): return lax.ppermute(values, 'shard', [(i, i ^ d) for i in range(planes)])  118 us
    ppermute x33, starting transfers between devices, over_chips(): lax.ppermute(values, 'ctx', [(i, i ^ 2 * d) for i in range(ctx_count)])  41.9 us
    dot_general x5, matrix products, dot_nt(): lax.dot_general(a, b, (((1,), (1,)), ((), ())), preferred_element_type=F32)  36.7 us
    dot_general x7, matrix products, dot_tn(): lax.dot_general(a, b, (((0,), (0,)), ((), ())), preferred_element_type=F32)  33.7 us
    dot_general x5, matrix products, dot_nn(): return jnp.dot(a, b, preferred_element_type=F32)  33.6 us
    unnamed x89, local copies, waits for them, and re-layouts  17.9 us
  transfers between devices with their start and end apart: 84, of which 30 were waited for; matrix products, arithmetic and copies ran while one was open for 21% of the time, Pallas kernels for 1%

profile of v1, /device:TPU:0, one launch (start us, length us, event | category | flops | bytes accessed | tf_op | source)
XLA Modules:
  0.0 754.5 jit_solution(8377739944097656420)
XLA Ops:
  3.6 3.0 collective-permute-start.4
  6.7 2.6 collective-permute-start.5
  15.2 5.2 select_reduce_fusion
  22.2 4.5 gather_fusion
  30.2 4.9 collective-permute-done.1
  35.6 3.0 pad_maximum_fusion.1
  38.7 8.3 %collective-permute-done.6 = bf16[512,512]{1,0:T(8,128)(2,1)S(1)} collective-permute-done((bf16[512,512]{1,0:T(8,128)(2,1)}, bf16[512,512]{1,0:T(8,128)(2,1)S(1)}, u32[]{:S(2)}, u32[]{:S(2)}) %collective-permute-start.6) | collective-permute-done | bytes 524320 | tf_op jit(solution)/shard_map/ppermute | solution.py:610
  57.7 5.5 collective-permute-done.7
  63.2 9.9 %collective-permute-start.13 = (bf16[256,512]{1,0:T(8,128)(2,1)}, bf16[256,512]{1,0:T(8,128)(2,1)S(1)}, u32[]{:S(2)}, u32[]{:S(2)}) collective-permute-start(bf16[256,512]{1,0:T(8,128)(2,1)} %get-tuple-element.43), channel_id=1, source_target_pairs={{0,2},{1,3},{2,0},{3,1},{4,6},{5,7},{6,4},{7,5},{8,10},{9,11},{10,... | collective-permute-start | bytes 786440 | tf_op jit(solution)/shard_map/ppermute | solution.py:610
  79.5 4.5 fusion.24
  84.1 2.5 fusion.85
  90.7 4.3 shard_map.212
  99.0 8.5 %collective-permute-start.23 = (bf16[256,512]{1,0:T(8,128)(2,1)S(1)}, bf16[256,512]{1,0:T(8,128)(2,1)}, u32[]{:S(2)}, u32[]{:S(2)}) collective-permute-start(bf16[256,512]{1,0:T(8,128)(2,1)S(1)} %get-tuple-element.51), channel_id=1, source_target_pairs={{0,1},{1,0},{2,3},{3,2},{4,5},{5,4},{6,7},{7,6},{8,9},{9,8},{10,11... | collective-permute-start | bytes 786440 | tf_op jit(solution)/shard_map/ppermute | solution.py:610
  109.9 5.0 fusion.143
  123.0 6.1 collective-permute-done.24
  130.8 3.9 collective-permute-start.34
  139.8 3.3 collective-permute-start.26
  143.1 2.3 multiply_reduce_fusion.2
  148.6 21.6 %collective-permute-done.34 = bf16[128,2048]{1,0:T(8,128)(2,1)S(1)} collective-permute-done((bf16[128,2048]{1,0:T(8,128)(2,1)}, bf16[128,2048]{1,0:T(8,128)(2,1)S(1)}, u32[]{:S(2)}, u32[]{:S(2)}) %collective-permute-start.34) | collective-permute-done | bytes 524320 | tf_op jit(solution)/shard_map/ppermute | solution.py:610
  170.6 2.3 collective-permute-start.21
  177.2 38.0 %collective-permute-done.20 = bf16[128,2048]{1,0:T(8,128)(2,1)S(1)} collective-permute-done((bf16[128,2048]{1,0:T(8,128)(2,1)S(1)}, bf16[128,2048]{1,0:T(8,128)(2,1)S(1)}, u32[]{:S(2)}, u32[]{:S(2)}) %collective-permute-start.20) | collective-permute-done | bytes 524320 | tf_op jit(solution)/shard_map/ppermute | solution.py:610
  217.4 21.3 %collective-permute-done.28 = bf16[256,2048]{1,0:T(8,128)(2,1)S(1)} collective-permute-done((bf16[256,2048]{1,0:T(8,128)(2,1)S(1)}, bf16[256,2048]{1,0:T(8,128)(2,1)S(1)}, u32[]{:S(2)}, u32[]{:S(2)}) %collective-permute-start.28) | collective-permute-done | bytes 1048608 | tf_op jit(solution)/shard_map/ppermute | solution.py:613
  243.8 10.6 %fusion.9 = f32[1024,1024]{0,1:T(8,128)} fusion(bf16[1024,2048]{1,0:T(8,128)(2,1)} %constant_dynamic-update-slice_fusion.5, bf16[2048,2048]{1,0:T(8,128)(2,1)} %param.19, s32[]{:T(128)S(6)} %select_n.573), kind=kOutput, calls=%fused_computation.23 | convolution fusion | flops 4294967296 | bytes 12582916 | tf_op jit(solution)/shard_map/dot_general | solution.py:452
  254.4 9.0 %fusion.13 = f32[1024,1024]{0,1:T(8,128)} fusion(bf16[1024,2048]{1,0:T(8,128)(2,1)} %constant_dynamic-update-slice_fusion.5, bf16[2048,2048]{1,0:T(8,128)(2,1)S(1)} %bitcast.281, s32[]{:T(128)S(6)} %select_n.573), kind=kOutput, calls=%fused_computation.27 | convolution fusion | flops 4294967296 | bytes 12582916 | tf_op jit(solution)/shard_map/dot_general | solution.py:452
  263.4 9.7 %multiply_convert_fusion = (bf16[1024,1024]{0,1:T(8,128)(2,1)}, bf16[1024,1024]{0,1:T(8,128)(2,1)}, bf16[1024,1024]{0,1:T(8,128)(2,1)S(1)}) fusion(f32[1024,1024]{0,1:T(8,128)} %fusion.13, f32[1024,1024]{0,1:T(8,128)} %fusion.9, bf16[1024,2048]{1,0:T(8,128)(2,1)S(1)} %copy-done.29, bf16[1024,2048]{1,0:T(8,128)(2,1)S(1)} %constant_dynamic-update-slice_fusion.22), kind=kOutput, calls=%fused_computation.16 | convolution fusion | flops 4310695936 | bytes 23068672 | tf_op jit(solution)/shard_map/dot_general | solution.py:456
  273.1 4.6 fusion.145
  277.7 4.5 fusion.147
  285.3 10.3 %fusion.11 = f32[1024,2048]{1,0:T(8,128)} fusion(bf16[1024,1024]{0,1:T(8,128)(2,1)S(1)} %copy-done.33, bf16[2048,2048]{1,0:T(8,128)(2,1)} %param.18, s32[]{:T(128)S(6)} %select_n.573), kind=kOutput, calls=%fused_computation.25 | convolution fusion | flops 4294967296 | bytes 14680068 | tf_op jit(solution)/shard_map/dot_general | solution.py:456
  300.9 9.8 %convolution_add_fusion = f32[1024,2048]{1,0:T(8,128)S(1)} fusion(f32[1024,2048]{1,0:T(8,128)} %fusion.11, bf16[1024,1024]{0,1:T(8,128)(2,1)} %get-tuple-element.47, bf16[2048,2048]{1,0:T(8,128)(2,1)} %param.19, s32[]{:T(128)S(6)} %select_n.573), kind=kOutput, calls=%fused_computation.21 | convolution fusion | flops 4297064448 | bytes 23068676 | tf_op jit(solution)/shard_map/dot_general | solution.py:456
  310.8 9.3 %convolution_convert_fusion.2 = bf16[512,2048]{1,0:T(8,128)(2,1)} fusion(bf16[1024,2048]{1,0:T(8,128)(2,1)} %constant_dynamic-update-slice_fusion.5, s32[]{:T(128)S(6)} %select_n.538, bf16[1024,1024]{0,1:T(8,128)(2,1)} %get-tuple-element.47, bf16[1024,1024]{0,1:T(8,128)(2,1)} %get-tuple-element.48), kind=kOutput, calls=%fused_computation.31 | convolution fusion | flops 2156920832 | bytes 7340036 | tf_op jit(solution)/shard_map/dot_general | solution.py:460
  320.1 5.0 convolution_convert_fusion.1
  325.1 17.4 %collective-permute-done.69 = bf16[4,64,2048]{2,1,0:T(8,128)(2,1)S(1)} collective-permute-done((bf16[4,64,2048]{2,1,0:T(8,128)(2,1)}, bf16[4,64,2048]{2,1,0:T(8,128)(2,1)S(1)}, u32[]{:S(2)}, u32[]{:S(2)}) %collective-permute-start.69) | collective-permute-done | bytes 1048608 | tf_op jit(solution)/shard_map/ppermute | solution.py:613
  344.1 2.7 fusion.21
  347.0 17.6 %collective-permute-start.71 = (bf16[64,2048]{1,0:T(8,128)(2,1)S(1)}, bf16[64,2048]{1,0:T(8,128)(2,1)S(1)}, u32[]{:S(2)}, u32[]{:S(2)}) collective-permute-start(bf16[64,2048]{1,0:T(8,128)(2,1)S(1)} %get-tuple-element.95), channel_id=1, source_target_pairs={{0,1},{1,0},{2,3},{3,2},{4,5},{5,4},{6,7},{7,6},{8,9},{9,8},{10,11... | collective-permute-start | bytes 786440 | tf_op jit(solution)/shard_map/ppermute | solution.py:610
  367.1 5.3 convolution_convert_fusion
  373.4 12.2 %collective-permute-done.72 = bf16[64,2048]{1,0:T(8,128)(2,1)S(1)} collective-permute-done((bf16[64,2048]{1,0:T(8,128)(2,1)S(1)}, bf16[64,2048]{1,0:T(8,128)(2,1)S(1)}, u32[]{:S(2)}, u32[]{:S(2)}) %collective-permute-start.72) | collective-permute-done | bytes 262176 | tf_op jit(solution)/shard_map/ppermute | solution.py:610
  386.4 5.7 fusion.54
  396.5 51.1 %collective-permute-done.75 = bf16[64,2048]{1,0:T(8,128)(2,1)S(1)} collective-permute-done((bf16[64,2048]{1,0:T(8,128)(2,1)S(1)}, bf16[64,2048]{1,0:T(8,128)(2,1)S(1)}, u32[]{:S(2)}, u32[]{:S(2)}) %collective-permute-start.75) | collective-permute-done | bytes 262176 | tf_op jit(solution)/shard_map/ppermute | solution.py:613
  448.6 7.4 collective-permute-done.76
  458.4 2.7 fusion.129
  461.2 3.8 collective-permute-start.30
  466.5 3.8 fusion.128
  471.3 2.3 collective-permute-start.32
  474.6 28.5 %collective-permute-done.63 = bf16[512,2048]{1,0:T(8,128)(2,1)} collective-permute-done((bf16[512,2048]{1,0:T(8,128)(2,1)}, bf16[512,2048]{1,0:T(8,128)(2,1)}, u32[]{:S(2)}, u32[]{:S(2)}) %collective-permute-start.63) | collective-permute-done | bytes 2097184 | tf_op jit(solution)/shard_map/ppermute | solution.py:613
  503.2 3.9 collective-permute-start.39
  509.3 3.7 add_convert_fusion
  514.8 34.8 %collective-permute-done.39 = bf16[128,2048]{1,0:T(8,128)(2,1)S(1)} collective-permute-done((bf16[128,2048]{1,0:T(8,128)(2,1)S(1)}, bf16[128,2048]{1,0:T(8,128)(2,1)S(1)}, u32[]{:S(2)}, u32[]{:S(2)}) %collective-permute-start.39) | collective-permute-done | bytes 524320 | tf_op jit(solution)/shard_map/ppermute | solution.py:610
  558.8 8.7 %collective-permute-start.65 = (bf16[64,4096]{1,0:T(8,128)(2,1)S(1)}, bf16[64,4096]{1,0:T(8,128)(2,1)S(1)}, u32[]{:S(2)}, u32[]{:S(2)}) collective-permute-start(bf16[64,4096]{1,0:T(8,128)(2,1)S(1)} %get-tuple-element.65), channel_id=1, source_target_pairs={{0,1},{1,0},{2,3},{3,2},{4,5},{5,4},{6,7},{7,6},{8,9},{9,8},{10,11... | collective-permute-start | bytes 1572872 | tf_op jit(solution)/shard_map/ppermute | solution.py:610
  567.7 9.1 %collective-permute-start.66 = (bf16[64,4096]{1,0:T(8,128)(2,1)S(1)}, bf16[64,4096]{1,0:T(8,128)(2,1)S(1)}, u32[]{:S(2)}, u32[]{:S(2)}) collective-permute-start(bf16[64,4096]{1,0:T(8,128)(2,1)S(1)} %get-tuple-element.64), channel_id=1, source_target_pairs={{0,2},{1,3},{2,0},{3,1},{4,6},{5,7},{6,4},{7,5},{8,10},{9,11},{10,... | collective-permute-start | bytes 1572872 | tf_op jit(solution)/shard_map/ppermute | solution.py:610
  584.5 24.5 %collective-permute-done.66 = bf16[64,4096]{1,0:T(8,128)(2,1)S(1)} collective-permute-done((bf16[64,4096]{1,0:T(8,128)(2,1)S(1)}, bf16[64,4096]{1,0:T(8,128)(2,1)S(1)}, u32[]{:S(2)}, u32[]{:S(2)}) %collective-permute-start.66) | collective-permute-done | bytes 524320 | tf_op jit(solution)/shard_map/ppermute | solution.py:610
  609.9 2.6 convolution_convert_fusion.3.outgrad
  612.5 5.5 shard_map.213
  620.4 5.7 collective-permute-start.58
  628.8 2.6 fusion.81
  631.3 2.7 fusion.22
  635.6 2.7 collective-permute-done.58
  638.3 9.1 %collective-permute-done.59 = bf16[64,2048]{1,0:T(8,128)(2,1)S(1)} collective-permute-done((bf16[64,2048]{1,0:T(8,128)(2,1)S(1)}, bf16[64,2048]{1,0:T(8,128)(2,1)S(1)}, u32[]{:S(2)}, u32[]{:S(2)}) %collective-permute-start.59) | collective-permute-done | bytes 262176 | tf_op jit(solution)/shard_map/ppermute | solution.py:610
  650.8 10.0 %collective-permute-done.51 = bf16[8,64,512]{2,1,0:T(8,128)(2,1)S(1)} collective-permute-done((bf16[8,64,512]{2,1,0:T(8,128)(2,1)S(1)}, bf16[8,64,512]{2,1,0:T(8,128)(2,1)S(1)}, u32[]{:S(2)}, u32[]{:S(2)}) %collective-permute-start.51) | collective-permute-done | bytes 524320 | tf_op jit(solution)/shard_map/ppermute | solution.py:610
  660.8 26.0 %collective-permute-done.52 = bf16[8,64,512]{2,1,0:T(8,128)(2,1)S(1)} collective-permute-done((bf16[8,64,512]{2,1,0:T(8,128)(2,1)S(1)}, bf16[8,64,512]{2,1,0:T(8,128)(2,1)S(1)}, u32[]{:S(2)}, u32[]{:S(2)}) %collective-permute-start.52) | collective-permute-done | bytes 524320 | tf_op jit(solution)/shard_map/ppermute | solution.py:610
  687.3 4.3 fusion.144
  698.3 21.9 %collective-permute-done.55 = bf16[64,1024]{1,0:T(8,128)(2,1)S(1)} collective-permute-done((bf16[64,1024]{1,0:T(8,128)(2,1)S(1)}, bf16[64,1024]{1,0:T(8,128)(2,1)S(1)}, u32[]{:S(2)}, u32[]{:S(2)}) %collective-permute-start.55) | collective-permute-done | bytes 131104 | tf_op jit(solution)/shard_map/ppermute | solution.py:613
  722.3 3.9 collective-permute-done.57
  728.0 11.1 %collective-permute-start.77 = (f32[2,8,64]{2,1,0:T(8,128)S(1)}, f32[2,8,64]{2,1,0:T(8,128)S(1)}, u32[]{:S(2)}, u32[]{:S(2)}) collective-permute-start(f32[2,8,64]{2,1,0:T(8,128)S(1)} %bitcast.274), channel_id=1, source_target_pairs={{0,1},{1,0},{2,3},{3,2},{4,5},{5,4},{6,7},{7,6},{8,9},{9,8},{10,11... | collective-permute-start | bytes 12296 | tf_op jit(solution)/shard_map/ppermute | solution.py:610
  751.4 2.4 collective-permute-done.83
  (355 shorter events, 152.9 us)
Async XLA Ops:
  3.6 35.0 %collective-permute-start.4 = (bf16[512,512]{1,0:T(8,128)(2,1)}, bf16[512,512]{1,0:T(8,128)(2,1)}, u32[]{:S(2)}, u32[]{:S(2)}) collective-permute-start(bf16[512,512]{1,0:T(8,128)(2,1)} %get-tuple-element.126), channel_id=1, source_target_pairs={{0,1},{1,0},{2,3},{3,2},{4,5},{5,4},{6,7},{7,6},{8,9},{9,8},{10,11... | collective-permute-start | bytes 1572872 | tf_op jit(solution)/shard_map/ppermute | solution.py:610
  6.7 32.0 %collective-permute-start.5 = (bf16[512,512]{1,0:T(8,128)(2,1)}, bf16[512,512]{1,0:T(8,128)(2,1)}, u32[]{:S(2)}, u32[]{:S(2)}) collective-permute-start(bf16[512,512]{1,0:T(8,128)(2,1)} %get-tuple-element.126), channel_id=1, source_target_pairs={{0,2},{1,3},{2,0},{3,1},{4,6},{5,7},{6,4},{7,5},{8,10},{9,11},{10,... | collective-permute-start | bytes 1572872 | tf_op jit(solution)/shard_map/ppermute | solution.py:610
  9.2 20.8 %collective-permute-start = (bf16[128,2048]{1,0:T(8,128)(2,1)}, bf16[128,2048]{1,0:T(8,128)(2,1)}, u32[]{:S(2)}, u32[]{:S(2)}) collective-permute-start(bf16[128,2048]{1,0:T(8,128)(2,1)} %bitcast.240), channel_id=1, source_target_pairs={{0,8},{4,12},{8,0},{12,4},{16,24},{20,28},{24,16},{28,20},{1,9},{5... | collective-permute-start | bytes 1572872 | tf_op jit(solution)/shard_map/ppermute | solution.py:613
  10.7 24.4 %collective-permute-start.1 = (bf16[128,2048]{1,0:T(8,128)(2,1)}, bf16[128,2048]{1,0:T(8,128)(2,1)}, u32[]{:S(2)}, u32[]{:S(2)}) collective-permute-start(bf16[128,2048]{1,0:T(8,128)(2,1)} %bitcast.241), channel_id=1, source_target_pairs={{0,16},{4,20},{8,24},{12,28},{16,0},{20,4},{24,8},{28,12},{1,17},{... | collective-permute-start | bytes 1572872 | tf_op jit(solution)/shard_map/ppermute | solution.py:613
  12.3 23.3 %collective-permute-start.2 = (bf16[128,2048]{1,0:T(8,128)(2,1)}, bf16[128,2048]{1,0:T(8,128)(2,1)}, u32[]{:S(2)}, u32[]{:S(2)}) collective-permute-start(bf16[128,2048]{1,0:T(8,128)(2,1)} %bitcast.242), channel_id=1, source_target_pairs={{0,24},{4,28},{8,16},{12,20},{16,8},{20,12},{24,0},{28,4},{1,25},{... | collective-permute-start | bytes 1572872 | tf_op jit(solution)/shard_map/ppermute | solution.py:613
  35.1 52.4 %collective-permute-start.12 = (bf16[256,512]{1,0:T(8,128)(2,1)}, bf16[256,512]{1,0:T(8,128)(2,1)S(1)}, u32[]{:S(2)}, u32[]{:S(2)}) collective-permute-start(bf16[256,512]{1,0:T(8,128)(2,1)} %get-tuple-element.43), channel_id=1, source_target_pairs={{0,1},{1,0},{2,3},{3,2},{4,5},{5,4},{6,7},{7,6},{8,9},{9,8},{10,11... | collective-permute-start | bytes 786440 | tf_op jit(solution)/shard_map/ppermute | solution.py:610
  38.6 38.3 %collective-permute-start.3 = (bf16[512,2048]{1,0:T(8,128)(2,1)}, bf16[512,2048]{1,0:T(8,128)(2,1)}, u32[]{:S(2)}, u32[]{:S(2)}) collective-permute-start(bf16[512,2048]{1,0:T(8,128)(2,1)} %pad_maximum_fusion.1), channel_id=1, source_target_pairs={{0,4},{4,0},{8,12},{12,8},{16,20},{20,16},{24,28},{28,24},{1,5},{5... | collective-permute-start | bytes 6291464 | tf_op jit(solution)/shard_map/ppermute | solution.py:616
  50.2 23.7 %collective-permute-start.8 = (bf16[512,512]{1,0:T(8,128)(2,1)S(1)}, bf16[512,512]{1,0:T(8,128)(2,1)S(1)}, u32[]{:S(2)}, u32[]{:S(2)}) collective-permute-start(bf16[512,512]{1,0:T(8,128)(2,1)S(1)} %get-tuple-element.83), channel_id=1, source_target_pairs={{0,16},{4,20},{8,24},{12,28},{16,0},{20,4},{24,8},{28,12},{1,17},{... | collective-permute-start | bytes 1572872 | tf_op jit(solution)/shard_map/ppermute | solution.py:613
  51.7 24.3 %collective-permute-start.9 = (bf16[512,512]{1,0:T(8,128)(2,1)S(1)}, bf16[512,512]{1,0:T(8,128)(2,1)S(1)}, u32[]{:S(2)}, u32[]{:S(2)}) collective-permute-start(bf16[512,512]{1,0:T(8,128)(2,1)S(1)} %get-tuple-element.82), channel_id=1, source_target_pairs={{0,24},{4,28},{8,16},{12,20},{16,8},{20,12},{24,0},{28,4},{1,25},{... | collective-permute-start | bytes 1572872 | tf_op jit(solution)/shard_map/ppermute | solution.py:613
  63.2 25.4 %collective-permute-start.13 = (bf16[256,512]{1,0:T(8,128)(2,1)}, bf16[256,512]{1,0:T(8,128)(2,1)S(1)}, u32[]{:S(2)}, u32[]{:S(2)}) collective-permute-start(bf16[256,512]{1,0:T(8,128)(2,1)} %get-tuple-element.43), channel_id=1, source_target_pairs={{0,2},{1,3},{2,0},{3,1},{4,6},{5,7},{6,4},{7,5},{8,10},{9,11},{10,... | collective-permute-start | bytes 786440 | tf_op jit(solution)/shard_map/ppermute | solution.py:610
  90.1 19.8 %collective-permute-start.15 = (bf16[256,2048]{1,0:T(8,128)(2,1)}, bf16[256,2048]{1,0:T(8,128)(2,1)}, u32[]{:S(2)}, u32[]{:S(2)}) collective-permute-start(bf16[256,2048]{1,0:T(8,128)(2,1)} %constant_dynamic-update-slice_fusion.29), channel_id=1, source_target_pairs={{0,4},{4,0},{8,12},{12,8},{16,20},{20,16},{24,28},{28,24},{1,5},{5... | collective-permute-start | bytes 3145736 | tf_op jit(solution)/shard_map/ppermute | solution.py:616
  99.0 19.9 %collective-permute-start.23 = (bf16[256,512]{1,0:T(8,128)(2,1)S(1)}, bf16[256,512]{1,0:T(8,128)(2,1)}, u32[]{:S(2)}, u32[]{:S(2)}) collective-permute-start(bf16[256,512]{1,0:T(8,128)(2,1)S(1)} %get-tuple-element.51), channel_id=1, source_target_pairs={{0,1},{1,0},{2,3},{3,2},{4,5},{5,4},{6,7},{7,6},{8,9},{9,8},{10,11... | collective-permute-start | bytes 786440 | tf_op jit(solution)/shard_map/ppermute | solution.py:610
  107.5 21.6 %collective-permute-start.24 = (bf16[256,512]{1,0:T(8,128)(2,1)}, bf16[256,512]{1,0:T(8,128)(2,1)}, u32[]{:S(2)}, u32[]{:S(2)}) collective-permute-start(bf16[256,512]{1,0:T(8,128)(2,1)} %get-tuple-element.53), channel_id=1, source_target_pairs={{0,2},{1,3},{2,0},{3,1},{4,6},{5,7},{6,4},{7,5},{8,10},{9,11},{10,... | collective-permute-start | bytes 786440 | tf_op jit(solution)/shard_map/ppermute | solution.py:610
  107.6 23.2 %collective-permute-start.25 = (bf16[256,512]{1,0:T(8,128)(2,1)}, bf16[256,512]{1,0:T(8,128)(2,1)}, u32[]{:S(2)}, u32[]{:S(2)}) collective-permute-start(bf16[256,512]{1,0:T(8,128)(2,1)} %get-tuple-element.50), channel_id=1, source_target_pairs={{0,3},{1,2},{2,1},{3,0},{4,7},{5,6},{6,5},{7,4},{8,11},{9,10},{10,... | collective-permute-start | bytes 786440 | tf_op jit(solution)/shard_map/ppermute | solution.py:610
  116.1 20.3 %collective-permute-start.16 = (bf16[128,2048]{1,0:T(8,128)(2,1)}, bf16[128,2048]{1,0:T(8,128)(2,1)}, u32[]{:S(2)}, u32[]{:S(2)}) collective-permute-start(bf16[128,2048]{1,0:T(8,128)(2,1)} %get-tuple-element.79), channel_id=1, source_target_pairs={{0,8},{4,12},{8,0},{12,4},{16,24},{20,28},{24,16},{28,20},{1,9},{5... | collective-permute-start | bytes 1572872 | tf_op jit(solution)/shard_map/ppermute | solution.py:613
  116.1 23.7 %collective-permute-start.17 = (bf16[128,2048]{1,0:T(8,128)(2,1)}, bf16[128,2048]{1,0:T(8,128)(2,1)}, u32[]{:S(2)}, u32[]{:S(2)}) collective-permute-start(bf16[128,2048]{1,0:T(8,128)(2,1)} %get-tuple-element.81), channel_id=1, source_target_pairs={{0,16},{4,20},{8,24},{12,28},{16,0},{20,4},{24,8},{28,12},{1,17},{... | collective-permute-start | bytes 1572872 | tf_op jit(solution)/shard_map/ppermute | solution.py:613
  118.9 24.2 %collective-permute-start.18 = (bf16[128,2048]{1,0:T(8,128)(2,1)}, bf16[128,2048]{1,0:T(8,128)(2,1)}, u32[]{:S(2)}, u32[]{:S(2)}) collective-permute-start(bf16[128,2048]{1,0:T(8,128)(2,1)} %get-tuple-element.80), channel_id=1, source_target_pairs={{0,24},{4,28},{8,16},{12,20},{16,8},{20,12},{24,0},{28,4},{1,25},{... | collective-permute-start | bytes 1572872 | tf_op jit(solution)/shard_map/ppermute | solution.py:613
  130.8 39.4 %collective-permute-start.34 = (bf16[128,2048]{1,0:T(8,128)(2,1)}, bf16[128,2048]{1,0:T(8,128)(2,1)S(1)}, u32[]{:S(2)}, u32[]{:S(2)}) collective-permute-start(bf16[128,2048]{1,0:T(8,128)(2,1)} %bitcast.248), channel_id=1, source_target_pairs={{0,2},{1,3},{2,0},{3,1},{4,6},{5,7},{6,4},{7,5},{8,10},{9,11},{10,... | collective-permute-start | bytes 1572872 | tf_op jit(solution)/shard_map/ppermute | solution.py:610
  136.4 33.9 %collective-permute-start.35 = (bf16[128,2048]{1,0:T(8,128)(2,1)}, bf16[128,2048]{1,0:T(8,128)(2,1)S(1)}, u32[]{:S(2)}, u32[]{:S(2)}) collective-permute-start(bf16[128,2048]{1,0:T(8,128)(2,1)} %bitcast.249), channel_id=1, source_target_pairs={{0,3},{1,2},{2,1},{3,0},{4,7},{5,6},{6,5},{7,4},{8,11},{9,10},{10,... | collective-permute-start | bytes 1572872 | tf_op jit(solution)/shard_map/ppermute | solution.py:610
  139.8 77.3 %collective-permute-start.26 = (bf16[256,2048]{1,0:T(8,128)(2,1)}, bf16[256,2048]{1,0:T(8,128)(2,1)S(1)}, u32[]{:S(2)}, u32[]{:S(2)}) collective-permute-start(bf16[256,2048]{1,0:T(8,128)(2,1)} %constant_dynamic-update-slice_fusion.26), channel_id=1, source_target_pairs={{0,8},{4,12},{8,0},{12,4},{16,24},{20,28},{24,16},{28,20},{1,9},{5... | collective-permute-start | bytes 3145736 | tf_op jit(solution)/shard_map/ppermute | solution.py:613
  146.5 29.1 %collective-permute-start.19 = (bf16[128,2048]{1,0:T(8,128)(2,1)S(1)}, bf16[128,2048]{1,0:T(8,128)(2,1)S(1)}, u32[]{:S(2)}, u32[]{:S(2)}) collective-permute-start(bf16[128,2048]{1,0:T(8,128)(2,1)S(1)} %get-tuple-element.35), channel_id=1, source_target_pairs={{0,1},{1,0},{2,3},{3,2},{4,5},{5,4},{6,7},{7,6},{8,9},{9,8},{10,11... | collective-permute-start | bytes 1572872 | tf_op jit(solution)/shard_map/ppermute | solution.py:610
  147.9 67.3 %collective-permute-start.20 = (bf16[128,2048]{1,0:T(8,128)(2,1)S(1)}, bf16[128,2048]{1,0:T(8,128)(2,1)S(1)}, u32[]{:S(2)}, u32[]{:S(2)}) collective-permute-start(bf16[128,2048]{1,0:T(8,128)(2,1)S(1)} %get-tuple-element.35), channel_id=1, source_target_pairs={{0,2},{1,3},{2,0},{3,1},{4,6},{5,7},{6,4},{7,5},{8,10},{9,11},{10,... | collective-permute-start | bytes 1572872 | tf_op jit(solution)/shard_map/ppermute | solution.py:610
  170.5 68.4 %collective-permute-start.36 = (bf16[512,2048]{1,0:T(8,128)(2,1)S(1)}, bf16[512,2048]{1,0:T(8,128)(2,1)S(1)}, u32[]{:S(2)}, u32[]{:S(2)}) collective-permute-start(bf16[512,2048]{1,0:T(8,128)(2,1)S(1)} %pad_maximum_fusion.4), channel_id=1, source_target_pairs={{0,4},{4,0},{8,12},{12,8},{16,20},{20,16},{24,28},{28,24},{1,5},{5... | collective-permute-start | bytes 6291464 | tf_op jit(solution)/shard_map/ppermute | solution.py:616
  170.6 46.2 %collective-permute-start.21 = (bf16[128,2048]{1,0:T(8,128)(2,1)S(1)}, bf16[128,2048]{1,0:T(8,128)(2,1)S(1)}, u32[]{:S(2)}, u32[]{:S(2)}) collective-permute-start(bf16[128,2048]{1,0:T(8,128)(2,1)S(1)} %get-tuple-element.35), channel_id=1, source_target_pairs={{0,3},{1,2},{2,1},{3,0},{4,7},{5,6},{6,5},{7,4},{8,11},{9,10},{10,... | collective-permute-start | bytes 1572872 | tf_op jit(solution)/shard_map/ppermute | solution.py:610
  175.6 41.7 %collective-permute-start.27 = (bf16[256,2048]{1,0:T(8,128)(2,1)S(1)}, bf16[256,2048]{1,0:T(8,128)(2,1)S(1)}, u32[]{:S(2)}, u32[]{:S(2)}) collective-permute-start(bf16[256,2048]{1,0:T(8,128)(2,1)S(1)} %copy-done.14), channel_id=1, source_target_pairs={{0,16},{4,20},{8,24},{12,28},{16,0},{20,4},{24,8},{28,12},{1,17},{... | collective-permute-start | bytes 3145736 | tf_op jit(solution)/shard_map/ppermute | solution.py:613
  215.2 23.5 %collective-permute-start.28 = (bf16[256,2048]{1,0:T(8,128)(2,1)S(1)}, bf16[256,2048]{1,0:T(8,128)(2,1)S(1)}, u32[]{:S(2)}, u32[]{:S(2)}) collective-permute-start(bf16[256,2048]{1,0:T(8,128)(2,1)S(1)} %copy-done.14), channel_id=1, source_target_pairs={{0,24},{4,28},{8,16},{12,20},{16,8},{20,12},{24,0},{28,4},{1,25},{... | collective-permute-start | bytes 3145736 | tf_op jit(solution)/shard_map/ppermute | solution.py:613
  217.0 25.2 %collective-permute-start.22 = (bf16[512,2048]{1,0:T(8,128)(2,1)S(1)}, bf16[512,2048]{1,0:T(8,128)(2,1)S(1)}, u32[]{:S(2)}, u32[]{:S(2)}) collective-permute-start(bf16[512,2048]{1,0:T(8,128)(2,1)S(1)} %pad_maximum_fusion.3), channel_id=1, source_target_pairs={{0,4},{4,0},{8,12},{12,8},{16,20},{20,16},{24,28},{28,24},{1,5},{5... | collective-permute-start | bytes 6291464 | tf_op jit(solution)/shard_map/ppermute | solution.py:616
  283.8 174.6 %collective-permute-start.29 = (bf16[512,2048]{1,0:T(8,128)(2,1)}, bf16[512,2048]{1,0:T(8,128)(2,1)}, u32[]{:S(2)}, u32[]{:S(2)}) collective-permute-start(bf16[512,2048]{1,0:T(8,128)(2,1)} %slice.458), channel_id=1, source_target_pairs={{0,4},{4,0},{8,12},{12,8},{16,20},{20,16},{24,28},{28,24},{1,5},{5... | collective-permute-start | bytes 6291464 | tf_op jit(solution)/shard_map/ppermute | solution.py:616
  297.4 27.7 %collective-permute-start.68 = (bf16[4,64,2048]{2,1,0:T(8,128)(2,1)}, bf16[4,64,2048]{2,1,0:T(8,128)(2,1)S(1)}, u32[]{:S(2)}, u32[]{:S(2)}) collective-permute-start(bf16[4,64,2048]{2,1,0:T(8,128)(2,1)} %get-tuple-element.44), channel_id=1, source_target_pairs={{0,8},{4,12},{8,0},{12,4},{16,24},{20,28},{24,16},{28,20},{1,9},{5... | collective-permute-start | bytes 3145736 | tf_op jit(solution)/shard_map/ppermute | solution.py:613
  297.8 44.7 %collective-permute-start.69 = (bf16[4,64,2048]{2,1,0:T(8,128)(2,1)}, bf16[4,64,2048]{2,1,0:T(8,128)(2,1)S(1)}, u32[]{:S(2)}, u32[]{:S(2)}) collective-permute-start(bf16[4,64,2048]{2,1,0:T(8,128)(2,1)} %get-tuple-element.45), channel_id=1, source_target_pairs={{0,16},{4,20},{8,24},{12,28},{16,0},{20,4},{24,8},{28,12},{1,17},{... | collective-permute-start | bytes 3145736 | tf_op jit(solution)/shard_map/ppermute | solution.py:613
  299.5 44.6 %collective-permute-start.70 = (bf16[4,64,2048]{2,1,0:T(8,128)(2,1)}, bf16[4,64,2048]{2,1,0:T(8,128)(2,1)}, u32[]{:S(2)}, u32[]{:S(2)}) collective-permute-start(bf16[4,64,2048]{2,1,0:T(8,128)(2,1)} %get-tuple-element.46), channel_id=1, source_target_pairs={{0,24},{4,28},{8,16},{12,20},{16,8},{20,12},{24,0},{28,4},{1,25},{... | collective-permute-start | bytes 3145736 | tf_op jit(solution)/shard_map/ppermute | solution.py:613
  347.0 26.4 %collective-permute-start.71 = (bf16[64,2048]{1,0:T(8,128)(2,1)S(1)}, bf16[64,2048]{1,0:T(8,128)(2,1)S(1)}, u32[]{:S(2)}, u32[]{:S(2)}) collective-permute-start(bf16[64,2048]{1,0:T(8,128)(2,1)S(1)} %get-tuple-element.95), channel_id=1, source_target_pairs={{0,1},{1,0},{2,3},{3,2},{4,5},{5,4},{6,7},{7,6},{8,9},{9,8},{10,11... | collective-permute-start | bytes 786440 | tf_op jit(solution)/shard_map/ppermute | solution.py:610
  364.6 20.9 %collective-permute-start.72 = (bf16[64,2048]{1,0:T(8,128)(2,1)S(1)}, bf16[64,2048]{1,0:T(8,128)(2,1)S(1)}, u32[]{:S(2)}, u32[]{:S(2)}) collective-permute-start(bf16[64,2048]{1,0:T(8,128)(2,1)S(1)} %get-tuple-element.94), channel_id=1, source_target_pairs={{0,2},{1,3},{2,0},{3,1},{4,6},{5,7},{6,4},{7,5},{8,10},{9,11},{10,... | collective-permute-start | bytes 786440 | tf_op jit(solution)/shard_map/ppermute | solution.py:610
  364.8 20.7 %collective-permute-start.73 = (bf16[64,2048]{1,0:T(8,128)(2,1)S(1)}, bf16[64,2048]{1,0:T(8,128)(2,1)S(1)}, u32[]{:S(2)}, u32[]{:S(2)}) collective-permute-start(bf16[64,2048]{1,0:T(8,128)(2,1)S(1)} %get-tuple-element.93), channel_id=1, source_target_pairs={{0,3},{1,2},{2,1},{3,0},{4,7},{5,6},{6,5},{7,4},{8,11},{9,10},{10,... | collective-permute-start | bytes 786440 | tf_op jit(solution)/shard_map/ppermute | solution.py:610
  392.4 72.6 %collective-permute-start.37 = (bf16[512,2048]{1,0:T(8,128)(2,1)S(1)}, bf16[512,2048]{1,0:T(8,128)(2,1)S(1)}, u32[]{:S(2)}, u32[]{:S(2)}) collective-permute-start(bf16[512,2048]{1,0:T(8,128)(2,1)S(1)} %slice.457), channel_id=1, source_target_pairs={{0,4},{4,0},{8,12},{12,8},{16,20},{20,16},{24,28},{28,24},{1,5},{5... | collective-permute-start | bytes 6291464 | tf_op jit(solution)/shard_map/ppermute | solution.py:616
  392.5 78.8 %collective-permute-start.61 = (bf16[512,2048]{1,0:T(8,128)(2,1)}, bf16[512,2048]{1,0:T(8,128)(2,1)S(1)}, u32[]{:S(2)}, u32[]{:S(2)}) collective-permute-start(bf16[512,2048]{1,0:T(8,128)(2,1)} %convolution_convert_fusion.2), channel_id=1, source_target_pairs={{0,8},{4,12},{8,0},{12,4},{16,24},{20,28},{24,16},{28,20},{1,9},{5... | collective-permute-start | bytes 6291464 | tf_op jit(solution)/shard_map/ppermute | solution.py:613
  394.1 79.5 %collective-permute-start.62 = (bf16[512,2048]{1,0:T(8,128)(2,1)}, bf16[512,2048]{1,0:T(8,128)(2,1)S(1)}, u32[]{:S(2)}, u32[]{:S(2)}) collective-permute-start(bf16[512,2048]{1,0:T(8,128)(2,1)} %convolution_convert_fusion.1), channel_id=1, source_target_pairs={{0,16},{4,20},{8,24},{12,28},{16,0},{20,4},{24,8},{28,12},{1,17},{... | collective-permute-start | bytes 6291464 | tf_op jit(solution)/shard_map/ppermute | solution.py:613
  394.9 52.7 %collective-permute-start.75 = (bf16[64,2048]{1,0:T(8,128)(2,1)S(1)}, bf16[64,2048]{1,0:T(8,128)(2,1)S(1)}, u32[]{:S(2)}, u32[]{:S(2)}) collective-permute-start(bf16[64,2048]{1,0:T(8,128)(2,1)S(1)} %get-tuple-element.90), channel_id=1, source_target_pairs={{0,16},{4,20},{8,24},{12,28},{16,0},{20,4},{24,8},{28,12},{1,17},{... | collective-permute-start | bytes 786440 | tf_op jit(solution)/shard_map/ppermute | solution.py:613
  456.0 47.2 %collective-permute-start.63 = (bf16[512,2048]{1,0:T(8,128)(2,1)}, bf16[512,2048]{1,0:T(8,128)(2,1)}, u32[]{:S(2)}, u32[]{:S(2)}) collective-permute-start(bf16[512,2048]{1,0:T(8,128)(2,1)} %convolution_convert_fusion), channel_id=1, source_target_pairs={{0,24},{4,28},{8,16},{12,20},{16,8},{20,12},{24,0},{28,4},{1,25},{... | collective-permute-start | bytes 6291464 | tf_op jit(solution)/shard_map/ppermute | solution.py:613
  461.2 45.9 %collective-permute-start.30 = (bf16[128,2048]{1,0:T(8,128)(2,1)S(1)}, bf16[128,2048]{1,0:T(8,128)(2,1)S(1)}, u32[]{:S(2)}, u32[]{:S(2)}) collective-permute-start(bf16[128,2048]{1,0:T(8,128)(2,1)S(1)} %get-tuple-element.76), channel_id=1, source_target_pairs={{0,1},{1,0},{2,3},{3,2},{4,5},{5,4},{6,7},{7,6},{8,9},{9,8},{10,11... | collective-permute-start | bytes 1572872 | tf_op jit(solution)/shard_map/ppermute | solution.py:610
  466.4 47.9 %collective-permute-start.31 = (bf16[128,2048]{1,0:T(8,128)(2,1)S(1)}, bf16[128,2048]{1,0:T(8,128)(2,1)S(1)}, u32[]{:S(2)}, u32[]{:S(2)}) collective-permute-start(bf16[128,2048]{1,0:T(8,128)(2,1)S(1)} %get-tuple-element.78), channel_id=1, source_target_pairs={{0,2},{1,3},{2,0},{3,1},{4,6},{5,7},{6,4},{7,5},{8,10},{9,11},{10,... | collective-permute-start | bytes 1572872 | tf_op jit(solution)/shard_map/ppermute | solution.py:610
  471.3 43.0 %collective-permute-start.32 = (bf16[128,2048]{1,0:T(8,128)(2,1)S(1)}, bf16[128,2048]{1,0:T(8,128)(2,1)S(1)}, u32[]{:S(2)}, u32[]{:S(2)}) collective-permute-start(bf16[128,2048]{1,0:T(8,128)(2,1)S(1)} %get-tuple-element.77), channel_id=1, source_target_pairs={{0,3},{1,2},{2,1},{3,0},{4,7},{5,6},{6,5},{7,4},{8,11},{9,10},{10,... | collective-permute-start | bytes 1572872 | tf_op jit(solution)/shard_map/ppermute | solution.py:610
  473.5 41.2 %collective-permute-start.38 = (bf16[128,2048]{1,0:T(8,128)(2,1)}, bf16[128,2048]{1,0:T(8,128)(2,1)S(1)}, u32[]{:S(2)}, u32[]{:S(2)}) collective-permute-start(bf16[128,2048]{1,0:T(8,128)(2,1)} %get-tuple-element.73), channel_id=1, source_target_pairs={{0,1},{1,0},{2,3},{3,2},{4,5},{5,4},{6,7},{7,6},{8,9},{9,8},{10,11... | collective-permute-start | bytes 1572872 | tf_op jit(solution)/shard_map/ppermute | solution.py:610
  503.2 46.4 %collective-permute-start.39 = (bf16[128,2048]{1,0:T(8,128)(2,1)S(1)}, bf16[128,2048]{1,0:T(8,128)(2,1)S(1)}, u32[]{:S(2)}, u32[]{:S(2)}) collective-permute-start(bf16[128,2048]{1,0:T(8,128)(2,1)S(1)} %get-tuple-element.75), channel_id=1, source_target_pairs={{0,2},{1,3},{2,0},{3,1},{4,6},{5,7},{6,4},{7,5},{8,10},{9,11},{10,... | collective-permute-start | bytes 1572872 | tf_op jit(solution)/shard_map/ppermute | solution.py:610
  507.1 42.5 %collective-permute-start.40 = (bf16[128,2048]{1,0:T(8,128)(2,1)S(1)}, bf16[128,2048]{1,0:T(8,128)(2,1)S(1)}, u32[]{:S(2)}, u32[]{:S(2)}) collective-permute-start(bf16[128,2048]{1,0:T(8,128)(2,1)S(1)} %get-tuple-element.74), channel_id=1, source_target_pairs={{0,3},{1,2},{2,1},{3,0},{4,7},{5,6},{6,5},{7,4},{8,11},{9,10},{10,... | collective-permute-start | bytes 1572872 | tf_op jit(solution)/shard_map/ppermute | solution.py:610
  514.2 173.0 %collective-permute-start.47 = (bf16[2048,512]{1,0:T(8,128)(2,1)}, bf16[2048,512]{1,0:T(8,128)(2,1)}, u32[]{:S(2)}, u32[]{:S(2)}) collective-permute-start(bf16[2048,512]{1,0:T(8,128)(2,1)} %constant_dynamic-update-slice_fusion.33), channel_id=1, source_target_pairs={{0,4},{4,0},{8,12},{12,8},{16,20},{20,16},{24,28},{28,24},{1,5},{5... | collective-permute-start | bytes 6291464 | tf_op jit(solution)/shard_map/ppermute | solution.py:616
  514.2 42.2 %collective-permute-start.64 = (bf16[256,2048]{1,0:T(8,128)(2,1)}, bf16[256,2048]{1,0:T(8,128)(2,1)}, u32[]{:S(2)}, u32[]{:S(2)}) collective-permute-start(bf16[256,2048]{1,0:T(8,128)(2,1)} %dynamic-slice_bitcast_fusion), channel_id=1, source_target_pairs={{0,4},{4,0},{8,12},{12,8},{16,20},{20,16},{24,28},{28,24},{1,5},{5... | collective-permute-start | bytes 3145736 | tf_op jit(solution)/shard_map/ppermute | solution.py:616
  553.9 22.9 %collective-permute-start.42 = (bf16[128,2048]{1,0:T(8,128)(2,1)}, bf16[128,2048]{1,0:T(8,128)(2,1)}, u32[]{:S(2)}, u32[]{:S(2)}) collective-permute-start(bf16[128,2048]{1,0:T(8,128)(2,1)} %get-tuple-element.27), channel_id=1, source_target_pairs={{0,16},{4,20},{8,24},{12,28},{16,0},{20,4},{24,8},{28,12},{1,17},{... | collective-permute-start | bytes 1572872 | tf_op jit(solution)/shard_map/ppermute | solution.py:613
  555.4 23.7 %collective-permute-start.43 = (bf16[128,2048]{1,0:T(8,128)(2,1)}, bf16[128,2048]{1,0:T(8,128)(2,1)}, u32[]{:S(2)}, u32[]{:S(2)}) collective-permute-start(bf16[128,2048]{1,0:T(8,128)(2,1)} %get-tuple-element.27), channel_id=1, source_target_pairs={{0,24},{4,28},{8,16},{12,20},{16,8},{20,12},{24,0},{28,4},{1,25},{... | collective-permute-start | bytes 1572872 | tf_op jit(solution)/shard_map/ppermute | solution.py:613
  558.8 25.6 %collective-permute-start.65 = (bf16[64,4096]{1,0:T(8,128)(2,1)S(1)}, bf16[64,4096]{1,0:T(8,128)(2,1)S(1)}, u32[]{:S(2)}, u32[]{:S(2)}) collective-permute-start(bf16[64,4096]{1,0:T(8,128)(2,1)S(1)} %get-tuple-element.65), channel_id=1, source_target_pairs={{0,1},{1,0},{2,3},{3,2},{4,5},{5,4},{6,7},{7,6},{8,9},{9,8},{10,11... | collective-permute-start | bytes 1572872 | tf_op jit(solution)/shard_map/ppermute | solution.py:610
  567.7 41.3 %collective-permute-start.66 = (bf16[64,4096]{1,0:T(8,128)(2,1)S(1)}, bf16[64,4096]{1,0:T(8,128)(2,1)S(1)}, u32[]{:S(2)}, u32[]{:S(2)}) collective-permute-start(bf16[64,4096]{1,0:T(8,128)(2,1)S(1)} %get-tuple-element.64), channel_id=1, source_target_pairs={{0,2},{1,3},{2,0},{3,1},{4,6},{5,7},{6,4},{7,5},{8,10},{9,11},{10,... | collective-permute-start | bytes 1572872 | tf_op jit(solution)/shard_map/ppermute | solution.py:610
  576.8 32.7 %collective-permute-start.67 = (bf16[64,4096]{1,0:T(8,128)(2,1)S(1)}, bf16[64,4096]{1,0:T(8,128)(2,1)S(1)}, u32[]{:S(2)}, u32[]{:S(2)}) collective-permute-start(bf16[64,4096]{1,0:T(8,128)(2,1)S(1)} %get-tuple-element.63), channel_id=1, source_target_pairs={{0,3},{1,2},{2,1},{3,0},{4,7},{5,6},{6,5},{7,4},{8,11},{9,10},{10,... | collective-permute-start | bytes 1572872 | tf_op jit(solution)/shard_map/ppermute | solution.py:610
  580.9 28.9 %collective-permute-start.44 = (bf16[512,2048]{1,0:T(8,128)(2,1)S(1)}, bf16[512,2048]{1,0:T(8,128)(2,1)S(1)}, u32[]{:S(2)}, u32[]{:S(2)}) collective-permute-start(bf16[512,2048]{1,0:T(8,128)(2,1)S(1)} %pad_maximum_fusion.5), channel_id=1, source_target_pairs={{0,4},{4,0},{8,12},{12,8},{16,20},{20,16},{24,28},{28,24},{1,5},{5... | collective-permute-start | bytes 6291464 | tf_op jit(solution)/shard_map/ppermute | solution.py:616
  626.1 21.4 %collective-permute-start.59 = (bf16[64,2048]{1,0:T(8,128)(2,1)S(1)}, bf16[64,2048]{1,0:T(8,128)(2,1)S(1)}, u32[]{:S(2)}, u32[]{:S(2)}) collective-permute-start(bf16[64,2048]{1,0:T(8,128)(2,1)S(1)} %get-tuple-element.69), channel_id=1, source_target_pairs={{0,2},{1,3},{2,0},{3,1},{4,6},{5,7},{6,4},{7,5},{8,10},{9,11},{10,... | collective-permute-start | bytes 786440 | tf_op jit(solution)/shard_map/ppermute | solution.py:610
  626.9 22.9 %collective-permute-start.60 = (bf16[64,2048]{1,0:T(8,128)(2,1)S(1)}, bf16[64,2048]{1,0:T(8,128)(2,1)S(1)}, u32[]{:S(2)}, u32[]{:S(2)}) collective-permute-start(bf16[64,2048]{1,0:T(8,128)(2,1)S(1)} %get-tuple-element.68), channel_id=1, source_target_pairs={{0,3},{1,2},{2,1},{3,0},{4,7},{5,6},{6,5},{7,4},{8,11},{9,10},{10,... | collective-permute-start | bytes 786440 | tf_op jit(solution)/shard_map/ppermute | solution.py:610
  634.3 26.5 %collective-permute-start.51 = (bf16[8,64,512]{2,1,0:T(8,128)(2,1)S(1)}, bf16[8,64,512]{2,1,0:T(8,128)(2,1)S(1)}, u32[]{:S(2)}, u32[]{:S(2)}) collective-permute-start(bf16[8,64,512]{2,1,0:T(8,128)(2,1)S(1)} %get-tuple-element.54), channel_id=1, source_target_pairs={{0,1},{1,0},{2,3},{3,2},{4,5},{5,4},{6,7},{7,6},{8,9},{9,8},{10,11... | collective-permute-start | bytes 1572872 | tf_op jit(solution)/shard_map/ppermute | solution.py:610
  638.3 48.5 %collective-permute-start.52 = (bf16[8,64,512]{2,1,0:T(8,128)(2,1)S(1)}, bf16[8,64,512]{2,1,0:T(8,128)(2,1)S(1)}, u32[]{:S(2)}, u32[]{:S(2)}) collective-permute-start(bf16[8,64,512]{2,1,0:T(8,128)(2,1)S(1)} %get-tuple-element.56), channel_id=1, source_target_pairs={{0,2},{1,3},{2,0},{3,1},{4,6},{5,7},{6,4},{7,5},{8,10},{9,11},{10,... | collective-permute-start | bytes 1572872 | tf_op jit(solution)/shard_map/ppermute | solution.py:610
  647.5 39.4 %collective-permute-start.53 = (bf16[8,64,512]{2,1,0:T(8,128)(2,1)S(1)}, bf16[8,64,512]{2,1,0:T(8,128)(2,1)S(1)}, u32[]{:S(2)}, u32[]{:S(2)}) collective-permute-start(bf16[8,64,512]{2,1,0:T(8,128)(2,1)S(1)} %get-tuple-element.55), channel_id=1, source_target_pairs={{0,3},{1,2},{2,1},{3,0},{4,7},{5,6},{6,5},{7,4},{8,11},{9,10},{10,... | collective-permute-start | bytes 1572872 | tf_op jit(solution)/shard_map/ppermute | solution.py:610
  649.8 37.5 %collective-permute-start.46 = (bf16[512,512]{1,0:T(8,128)(2,1)S(1)}, bf16[512,512]{1,0:T(8,128)(2,1)S(1)}, u32[]{:S(2)}, u32[]{:S(2)}) collective-permute-start(bf16[512,512]{1,0:T(8,128)(2,1)S(1)} %get-tuple-element.107), channel_id=1, source_target_pairs={{0,4},{4,0},{8,12},{12,8},{16,20},{20,16},{24,28},{28,24},{1,5},{5... | collective-permute-start | bytes 1572872 | tf_op jit(solution)/shard_map/ppermute | solution.py:616
  691.7 34.6 %collective-permute-start.48 = (bf16[128,2048]{1,0:T(8,128)(2,1)S(1)}, bf16[128,2048]{1,0:T(8,128)(2,1)S(1)}, u32[]{:S(2)}, u32[]{:S(2)}) collective-permute-start(bf16[128,2048]{1,0:T(8,128)(2,1)S(1)} %get-tuple-element.70), channel_id=1, source_target_pairs={{0,8},{4,12},{8,0},{12,4},{16,24},{20,28},{24,16},{28,20},{1,9},{5... | collective-permute-start | bytes 1572872 | tf_op jit(solution)/shard_map/ppermute | solution.py:613
  692.8 33.5 %collective-permute-start.49 = (bf16[128,2048]{1,0:T(8,128)(2,1)S(1)}, bf16[128,2048]{1,0:T(8,128)(2,1)S(1)}, u32[]{:S(2)}, u32[]{:S(2)}) collective-permute-start(bf16[128,2048]{1,0:T(8,128)(2,1)S(1)} %get-tuple-element.72), channel_id=1, source_target_pairs={{0,16},{4,20},{8,24},{12,28},{16,0},{20,4},{24,8},{28,12},{1,17},{... | collective-permute-start | bytes 1572872 | tf_op jit(solution)/shard_map/ppermute | solution.py:613
  694.3 32.0 %collective-permute-start.50 = (bf16[128,2048]{1,0:T(8,128)(2,1)S(1)}, bf16[128,2048]{1,0:T(8,128)(2,1)S(1)}, u32[]{:S(2)}, u32[]{:S(2)}) collective-permute-start(bf16[128,2048]{1,0:T(8,128)(2,1)S(1)} %get-tuple-element.71), channel_id=1, source_target_pairs={{0,24},{4,28},{8,16},{12,20},{16,8},{20,12},{24,0},{28,4},{1,25},{... | collective-permute-start | bytes 1572872 | tf_op jit(solution)/shard_map/ppermute | solution.py:613
  695.5 24.7 %collective-permute-start.55 = (bf16[64,1024]{1,0:T(8,128)(2,1)S(1)}, bf16[64,1024]{1,0:T(8,128)(2,1)S(1)}, u32[]{:S(2)}, u32[]{:S(2)}) collective-permute-start(bf16[64,1024]{1,0:T(8,128)(2,1)S(1)} %get-tuple-element.119), channel_id=1, source_target_pairs={{0,8},{4,12},{8,0},{12,4},{16,24},{20,28},{24,16},{28,20},{1,9},{5... | collective-permute-start | bytes 393224 | tf_op jit(solution)/shard_map/ppermute | solution.py:613
  696.6 25.7 %collective-permute-start.56 = (bf16[64,1024]{1,0:T(8,128)(2,1)S(1)}, bf16[64,1024]{1,0:T(8,128)(2,1)S(1)}, u32[]{:S(2)}, u32[]{:S(2)}) collective-permute-start(bf16[64,1024]{1,0:T(8,128)(2,1)S(1)} %get-tuple-element.118), channel_id=1, source_target_pairs={{0,16},{4,20},{8,24},{12,28},{16,0},{20,4},{24,8},{28,12},{1,17},{... | collective-permute-start | bytes 393224 | tf_op jit(solution)/shard_map/ppermute | solution.py:613
  (57 other events, 793.8 us)

commit v2 on v1

--- a/solution.py
+++ b/solution.py
@@ -557,6 +557,310 @@
     )(query, outgrad, key, value, log_total, code, low_code, key_code)
 
 
+MESH = pl.DeviceIdType.MESH
+TILE = 256
+
+
+def flip(i, d):
+    return (i, i + 1 - 2 * (i % 2), (i + 2) % 4, 3 - i)[d]
+
+
+def mlp_kernel(
+    second_ref,
+    mid_ref,
+    upstream_ref,
+    gain_ref,
+    upstream_hbm,
+    gate_hbm,
+    up_hbm,
+    down_hbm,
+    output_ref,
+    mid_grad_ref,
+    gain_grad_ref,
+    branch_all,
+    gate_up_terms,
+    down_terms,
+    gate_w,
+    up_w,
+    down_w,
+    upstream_all,
+    second_all,
+    act,
+    gate_grad,
+    up_grad,
+    held,
+    own_sum,
+    pair_send,
+    pair_recv,
+    z_send,
+    z_recv,
+    branch_low,
+    staged,
+    local_sem,
+    staged_sem,
+    send_sem,
+    recv_sem,
+):
+    tok = second_ref.shape[0]
+    pair = 2 * tok
+    hidden = gate_w.shape[1]
+    width = second_ref.shape[1]
+    ctx, plane = lax.axis_index("ctx"), lax.axis_index("shard")
+    chip, core = ctx // 2, ctx % 2
+    sibling = (ctx + 1 - 2 * core, plane)
+    over_z = [(ctx, flip(plane, d)) for d in range(4)]
+    over_chips = [(2 * flip(chip, d) + core, plane) for d in range(4)]
+
+    half = pl.ds(pl.multiple_of(core * hidden, hidden), hidden)
+    loads = [
+        pltpu.make_async_copy(upstream_hbm, upstream_all, local_sem.at[0]),
+        pltpu.make_async_copy(down_hbm, down_w, local_sem.at[1]),
+        pltpu.make_async_copy(gate_hbm.at[:, half], gate_w, local_sem.at[2]),
+        pltpu.make_async_copy(up_hbm.at[:, half], up_w, local_sem.at[3]),
+        pltpu.make_async_copy(second_ref, second_all.at[0, 0], local_sem.at[4]),
+    ]
+    for load in loads:
+        load.start()
+
+    barrier = pltpu.get_barrier_semaphore()
+    partners = [sibling] + over_z[1:] + over_chips[1:]
+    for partner in partners:
+        pl.semaphore_signal(barrier, inc=1, device_id=partner, device_id_type=MESH)
+    pl.semaphore_wait(barrier, len(partners))
+
+    def send(slot, source, target, device):
+        copy = pltpu.make_async_remote_copy(
+            src_ref=source,
+            dst_ref=target,
+            send_sem=send_sem.at[slot],
+            recv_sem=recv_sem.at[slot],
+            device_id=device,
+            device_id_type=MESH,
+        )
+        copy.start()
+        return copy
+
+    gather_z = {d: send(d, second_ref, second_all.at[d, 0], over_z[d]) for d in (1, 2, 3)}
+    gather_pair = {0: send(0, second_ref, second_all.at[0, 1], sibling)}
+    for load in loads:
+        load.wait()
+
+    def rows_of(d):
+        return pl.ds(d * pair, pair)
+
+    def forward(d):
+        rows = rows_of(d)
+        second = lambda: second_all[d].reshape(pair, width)
+
+        def step(t, carry):
+            at = pl.ds(pl.multiple_of(t * TILE, TILE), TILE)
+            act_grad = dot_nt(upstream_all[rows, :], down_w[at, :])
+            gate = dot_nn(second(), gate_w[:, at])
+            up_lin = dot_nn(second(), up_w[:, at])
+            sigma = 1.0 / (1.0 + jnp.exp(-gate))
+            swish = gate * sigma
+            act[rows, at] = (swish * up_lin).astype(BF16)
+            gate_grad[rows, at] = (
+                act_grad * up_lin * (sigma * (1.0 + gate * (1.0 - sigma)))
+            ).astype(BF16)
+            up_grad[rows, at] = (act_grad * swish).astype(BF16)
+            return carry
+
+        lax.fori_loop(0, hidden // TILE, step, 0)
+
+    def give_pair(d, base, product):
+        which = 0 if base == 7 else 1
+
+        def step(t, carry):
+            at = pl.ds(pl.multiple_of(t * TILE, TILE), TILE)
+            terms = product(at)
+            held[d % 2, :, at] = terms[:tok]
+            pair_send[which, d, :, at] = terms[tok:].astype(BF16)
+            return carry
+
+        lax.fori_loop(0, width // TILE, step, 0)
+        return send(base + d, pair_send.at[which, d], pair_recv.at[which, d], sibling)
+
+    def give_plane(d, base, copy):
+        which = 0 if base == 7 else 1
+        copy.wait_recv()
+        total = held[d % 2] + pair_recv[which, d].astype(F32)
+        if d == 0:
+            own_sum[which] = total
+            return None
+        z_send[which, d - 1] = total.astype(BF16)
+        return send(base + 3 + d, z_send.at[which, d - 1], z_recv.at[which, d - 1], over_z[d])
+
+    def back(d):
+        rows = rows_of(d)
+        return lambda at: dot_nt(gate_grad[rows, :], gate_w[at, :]) + dot_nt(
+            up_grad[rows, :], up_w[at, :]
+        )
+
+    def onward(d):
+        rows = rows_of(d)
+        return lambda at: dot_nn(act[rows, :], down_w[:, at])
+
+    pairs, planes = {}, {}
+    for d in range(4):
+        if d:
+            gather_z[d].wait_recv()
+            gather_pair[d] = send(
+                3 + d, second_all.at[d, 0], second_all.at[d, 1], sibling
+            )
+        gather_pair[d].wait_recv()
+        forward(d)
+        pairs[d] = give_pair(d, 7, back(d))
+        if d:
+            planes[d - 1] = give_plane(d - 1, 7, pairs[d - 1])
+    planes[3] = give_plane(3, 7, pairs[3])
+
+    out_pairs, out_planes = {}, {}
+    for d in range(4):
+        out_pairs[d] = give_pair(d, 14, onward(d))
+        if d:
+            out_planes[d - 1] = give_plane(d - 1, 14, out_pairs[d - 1])
+    out_planes[3] = give_plane(3, 14, out_pairs[3])
+
+    second_rows = second_all.reshape(8 * tok, width)
+
+    def to_hbm(slot, target):
+        return pltpu.make_async_copy(staged.at[slot], target, staged_sem.at[slot])
+
+    def gate_up_step(d):
+        for h in range(2):
+            first = flip(chip, d) * (2 * TILE) + h * TILE
+            left = second_rows[:, pl.ds(pl.multiple_of(first, TILE), TILE)]
+            target = gate_up_terms.at[d, pl.ds(h * TILE, TILE)]
+            if d:
+                to_hbm(h, target).wait()
+            staged[h, :, :hidden] = dot_tn(left, gate_grad[...]).astype(BF16)
+            staged[h, :, hidden:] = dot_tn(left, up_grad[...]).astype(BF16)
+            to_hbm(h, target).start()
+
+    for d in range(4):
+        gate_up_step(d)
+
+    for d in (1, 2, 3):
+        planes[d].wait_recv()
+    chunk = 32
+    gain = gain_ref[...]
+
+    def mid_step(i, carry):
+        at = pl.ds(pl.multiple_of(i * chunk, chunk), chunk)
+        grad = own_sum[0, at, :]
+        for d in range(3):
+            grad = grad + z_recv[0, d, at, :].astype(F32)
+        mid = mid_ref[at, :]
+        factor = lax.rsqrt(jnp.mean(mid * mid, axis=-1, keepdims=True) + EPSILON)
+        scaled = grad * gain
+        mid_grad = (
+            upstream_ref[at, :].astype(F32)
+            + factor * scaled
+            - mid * (factor * factor * factor * jnp.mean(scaled * mid, axis=-1, keepdims=True))
+        )
+        mid_grad_ref[at, :] = mid_grad
+        branch_low[at, :] = mid_grad.astype(BF16)
+        return carry + jnp.sum(grad * mid * factor, axis=0, keepdims=True)
+
+    gain_grad_ref[...] = lax.fori_loop(0, tok // chunk, mid_step, jnp.zeros((1, width), F32))
+    branch_chips = {
+        d: send(20 + d, branch_low, branch_all.at[0, d], over_chips[d]) for d in (1, 2, 3)
+    }
+    branch_pairs = {0: send(24, branch_low, branch_all.at[1, 0], sibling)}
+    keep = pltpu.make_async_copy(branch_low, branch_all.at[0, 0], local_sem.at[0])
+    keep.start()
+
+    def down_step(t):
+        slot = t % 2
+        target = down_terms.at[pl.ds(t * TILE, TILE)]
+        to_hbm(slot, target).wait()
+        left = act[:, pl.ds(t * TILE, TILE)]
+        staged[slot] = dot_tn(left, upstream_all[...]).astype(BF16)
+        to_hbm(slot, target).start()
+
+    for t in range(hidden // TILE):
+        down_step(t)
+    for d in (1, 2, 3):
+        branch_chips[d].wait_recv()
+        branch_pairs[d] = send(24 + d, branch_all.at[0, d], branch_all.at[1, d], sibling)
+
+    for d in (1, 2, 3):
+        out_planes[d].wait_recv()
+
+    def out_step(i, carry):
+        at = pl.ds(pl.multiple_of(i * chunk, chunk), chunk)
+        total = mid_ref[at, :] + own_sum[1, at, :]
+        for d in range(3):
+            total = total + z_recv[1, d, at, :].astype(F32)
+        output_ref[at, :] = total.astype(BF16)
+        return carry
+
+    lax.fori_loop(0, tok // chunk, out_step, 0)
+
+    for d in range(4):
+        branch_pairs[d].wait_recv()
+        for copy in (gather_pair[d], pairs[d], out_pairs[d], branch_pairs[d]):
+            copy.wait_send()
+    for d in (1, 2, 3):
+        for copy in (gather_z[d], planes[d], out_planes[d], branch_chips[d]):
+            copy.wait_send()
+    keep.wait()
+    for slot in range(2):
+        to_hbm(slot, down_terms.at[pl.ds(0, TILE)]).wait()
+
+
+def mlp_of(normed_two, mid, upstream, gain, upstream_group, w_gate, w_up, down_rows):
+    tok, width = mid.shape
+    hidden = down_rows.shape[0]
+    rows = upstream_group.shape[0]
+    vmem = pl.BlockSpec(memory_space=pltpu.VMEM)
+    hbm = pl.BlockSpec(memory_space=pl.ANY)
+    return pl.pallas_call(
+        mlp_kernel,
+        in_specs=[vmem] * 4 + [hbm] * 4,
+        out_specs=[vmem] * 3 + [hbm] * 3,
+        out_shape=[
+            jax.ShapeDtypeStruct((tok, width), BF16),
+            jax.ShapeDtypeStruct((tok, width), F32),
+            jax.ShapeDtypeStruct((1, width), F32),
+            jax.ShapeDtypeStruct((2, 4, tok, width), BF16),
+            jax.ShapeDtypeStruct((4, 2 * TILE, 2 * hidden), BF16),
+            jax.ShapeDtypeStruct((hidden, width), BF16),
+        ],
+        scratch_shapes=[
+            pltpu.VMEM((width, hidden), BF16),
+            pltpu.VMEM((width, hidden), BF16),
+            pltpu.VMEM((hidden, width), BF16),
+            pltpu.VMEM((rows, width), BF16),
+            pltpu.VMEM((4, 2, tok, width), BF16),
+            pltpu.VMEM((rows, hidden), BF16),
+            pltpu.VMEM((rows, hidden), BF16),
+            pltpu.VMEM((rows, hidden), BF16),
+            pltpu.VMEM((2, tok, width), F32),
+            pltpu.VMEM((2, tok, width), F32),
+            pltpu.VMEM((2, 4, tok, width), BF16),
+            pltpu.VMEM((2, 4, tok, width), BF16),
+            pltpu.VMEM((2, 3, tok, width), BF16),
+            pltpu.VMEM((2, 3, tok, width), BF16),
+            pltpu.VMEM((tok, width), BF16),
+            pltpu.VMEM((2, TILE, width), BF16),
+            pltpu.SemaphoreType.DMA((5,)),
+            pltpu.SemaphoreType.DMA((2,)),
+            pltpu.SemaphoreType.DMA((28,)),
+            pltpu.SemaphoreType.DMA((28,)),
+        ],
+        compiler_params=pltpu.CompilerParams(
+            collective_id=1, has_side_effects=True, vmem_limit_bytes=60 << 20
+        ),
+        cost_estimate=pl.CostEstimate(
+            flops=18 * rows * width * hidden,
+            bytes_accessed=2 * (5 * width * hidden + 4 * rows * width),
+            transcendentals=rows * hidden,
+        ),
+    )(normed_two, mid, upstream, gain, upstream_group, w_gate, w_up, down_rows)
+
+
 def rotate_head(values, cosine, sine):
     half = values.shape[-1] // 2
     first, second = values[:, :half], values[:, half:]
@@ -600,7 +904,6 @@
     first_core = core == 0
     seq_rows = tok_rows * ctx_count
     half_seq = seq_rows // 2
-    group_rows = tok_rows * planes
     shard_width = w_down.shape[1]
     hidden_plane = w_gate.shape[1]
     hidden = hidden_plane // 2
@@ -629,8 +932,8 @@
         return jnp.concatenate([mine, sibling(mine)], axis=0)
 
     def gather_group(values):
-        mine = jnp.concatenate(gather_z(values), axis=0)
-        return jnp.concatenate([mine, sibling(mine)], axis=0)
+        mine = jnp.stack(gather_z(values))
+        return jnp.stack([mine, sibling(mine)], axis=1).reshape(-1, width)
 
     def sum_chips(block_of):
         total = block_of(0)
@@ -699,7 +1002,6 @@
     mid = inputs + sum_chips(lambda d: branch_parts[d])
     factor_two = lax.rsqrt(jnp.mean(mid * mid, axis=-1, keepdims=True) + EPSILON)
     normed_two = (mid * factor_two * mlp_gain).astype(BF16)
-    normed_group = gather_group(normed_two)
 
     quarter_hidden = hidden // chips
     down_block = jnp.zeros((quarter_hidden, width), BF16)
@@ -714,35 +1016,13 @@
         down_rows = lax.dynamic_update_slice(down_rows, part, (quarter_hidden * (chip ^ d), 0))
 
     upstream_low = cotangent[0]
-    upstream = upstream_low.astype(F32)
     upstream_group = gather_group(upstream_low)
-    act_grad = dot_nt(upstream_group, down_rows)
-    gate_cols = cut(w_gate, (0, hidden * core), (width, hidden))
-    up_cols = cut(w_up, (0, hidden * core), (width, hidden))
-    gate = dot_nn(normed_group, gate_cols)
-    up_lin = dot_nn(normed_group, up_cols)
-    sigma = jax.nn.sigmoid(gate)
-    swish = gate * sigma
-    act = (swish * up_lin).astype(BF16)
-    gate_grad = (act_grad * up_lin * (sigma * (1.0 + gate * (1.0 - sigma)))).astype(BF16)
-    up_grad = (act_grad * swish).astype(BF16)
-
-    def back_to_tokens(partial):
-        low = partial.astype(BF16)
-        pair = partial[:group_rows] + sibling(low[group_rows:]).astype(F32)
-        blocks = pair.reshape(planes, tok_rows, width)
-        return sum_z(lambda d: blocks[d])
-
-    norm_two_grad = back_to_tokens(dot_nt(gate_grad, gate_cols) + dot_nt(up_grad, up_cols))
-    mlp_gain_term = jnp.sum(norm_two_grad * mid * factor_two, axis=0)
-    scaled_two = norm_two_grad * mlp_gain
-    mid_grad = (
-        upstream
-        + factor_two * scaled_two
-        - mid * factor_two**3 * jnp.mean(scaled_two * mid, axis=-1, keepdims=True)
-    )
-    branch_grad_all = gather_seq(mid_grad.astype(BF16))
-    output = (mid + back_to_tokens(dot_nn(act, down_rows))).astype(BF16)[None]
+    output, mid_grad, mlp_gain_term, branch_grad_all, gate_up_terms, down_terms = mlp_of(
+        normed_two, mid, upstream_low, mlp_gain[None], upstream_group, w_gate, w_up, down_rows
+    )
+    output = output[None]
+    mlp_gain_term = mlp_gain_term[0]
+    branch_grad_all = branch_grad_all.reshape(seq_rows, width)
 
     attended_grad = dot_nt(branch_grad_all, out_rows).astype(BF16)
     d_query, d_key, d_value = attend_back(
@@ -767,13 +1047,7 @@
         - inputs * factor_one**3 * jnp.mean(scaled_one * inputs, axis=-1, keepdims=True)
     ).astype(BF16)[None]
 
-    mlp_grads = jnp.concatenate([gate_grad, up_grad], axis=1)
-
-    def mlp_rows(d):
-        left = cut(normed_group, (0, quarter * (chip ^ d)), (2 * group_rows, quarter))
-        return dot_tn(left, mlp_grads)
-
-    mlp_sum = sum_chips(mlp_rows).astype(BF16).reshape(2, quarter // 2, 2 * hidden)
+    mlp_sum = sum_chips(lambda d: gate_up_terms[d].astype(F32)).astype(BF16).reshape(2, quarter // 2, 2 * hidden)
     mlp_mine = index_of(mlp_sum, core)
     mlp_other = sibling(index_of(mlp_sum, 1 - core))
     left_half = jnp.where(first_core, mlp_mine, mlp_other)
@@ -793,9 +1067,9 @@
         grad_gate = lax.dynamic_update_slice(grad_gate, part[:, :hidden_plane], at)
         grad_up = lax.dynamic_update_slice(grad_up, part[:, hidden_plane:], at)
 
-    down_terms = dot_tn(act, upstream_group).reshape(planes, chips, -1, width)
+    down_terms = down_terms.reshape(planes, chips, -1, width)
     down_sum = sum_chips(
-        lambda d: lax.dynamic_index_in_dim(down_terms, chip ^ d, 1, keepdims=False)
+        lambda d: lax.dynamic_index_in_dim(down_terms, chip ^ d, 1, keepdims=False).astype(F32)
     ).astype(BF16)
     down_parts = []
     for d in range(planes):

time: 764 us -> 679 us (0.89)
  Pallas kernels: 9.78 us -> 152 us
  matrix products: 104 us -> 17.4 us
  waiting for transfers between devices: 368 us -> 284 us
  starting transfers between devices: 161 us -> 127 us
  other arithmetic: 49.7 us -> 36 us
  local copies, waits for them, and re-layouts: 59.2 us -> 49.9 us
    pallas_call x0 -> x1, Pallas kernels: none -> 142 us  [mlp_of(): pl.pallas_call(mlp_kernel, in_specs=[vmem] * 4 + [hbm] * 4, out_specs=[vm...]
    ppermute x33 -> x30, waiting for transfers between devices: 166 us -> 121 us  [over_chips(): lax.ppermute(values, 'ctx', [(i, i ^ 2 * d) for i in range(ctx_count)])]
    ppermute x36 -> x27, waiting for transfers between devices: 201 us -> 158 us  [over_z(): return lax.ppermute(values, 'shard', [(i, i ^ d) for i in range(planes)])]
    ppermute x36 -> x27, starting transfers between devices: 118 us -> 85.9 us  [over_z(): return lax.ppermute(values, 'shard', [(i, i ^ d) for i in range(planes)])]
    dot_general x5 -> x2, matrix products: 36.7 us -> 5.73 us  [dot_nt(): lax.dot_general(a, b, (((1,), (1,)), ((), ())), preferred_element_type=F32)]
    dot_general x7 -> x2, matrix products: 33.7 us -> 3.98 us  [dot_tn(): lax.dot_general(a, b, (((0,), (0,)), ((), ())), preferred_element_type=F32)]
    dot_general x5 -> x2, matrix products: 33.6 us -> 7.64 us  [dot_nn(): return jnp.dot(a, b, preferred_element_type=F32)]
    squeeze x0 -> x2, local copies, waits for them, and re-layouts: none -> 9.58 us  [the longest x1 5.96 us: on_device_by_head(): gate_up_terms[d].astype(F32)]
  transfers between devices with their start and end apart: 84 -> 68, of which waited for: 30 -> 26; matrix products, arithmetic and copies ran while one was open for 21% -> 13% of each run, Pallas kernels for 1% -> 1%
where the time goes in v2:
time: 679 us; the launch traced here: 669 us
  waiting for transfers between devices  284 us (42%)
  Pallas kernels  152 us (22%)
  starting transfers between devices  127 us (19%)
  local copies, waits for them, and re-layouts  49.9 us (7%)
  other arithmetic  36 us (5%)
  matrix products  17.4 us (3%)
    ppermute x27, waiting for transfers between devices, over_z(): return lax.ppermute(values, 'shard', [(i, i ^ d) for i in range(planes)])  158 us
    pallas_call x1, Pallas kernels, mlp_of(): pl.pallas_call(mlp_kernel, in_specs=[vmem] * 4 + [hbm] * 4, out_specs=[vm...  142 us
    ppermute x30, waiting for transfers between devices, over_chips(): lax.ppermute(values, 'ctx', [(i, i ^ 2 * d) for i in range(ctx_count)])  121 us
    ppermute x27, starting transfers between devices, over_z(): return lax.ppermute(values, 'shard', [(i, i ^ d) for i in range(planes)])  85.9 us
    ppermute x30, starting transfers between devices, over_chips(): lax.ppermute(values, 'ctx', [(i, i ^ 2 * d) for i in range(ctx_count)])  38.9 us
  transfers between devices with their start and end apart: 68, of which 26 were waited for; matrix products, arithmetic and copies ran while one was open for 13% of the time, Pallas kernels for 1%

profile of v2, /device:TPU:0, one launch (start us, length us, event | category | flops | bytes accessed | tf_op | source)
XLA Modules:
  0.0 669.1 jit_solution(11431864859871402621)
XLA Ops:
  0.7 3.0 collective-permute-start
  6.3 2.2 constant_dynamic-slice_fusion.11
  8.5 2.0 collective-permute-start.23
  11.7 1.8 constant_dynamic-update-slice_fusion.10
  15.9 5.2 select_reduce_fusion
  22.9 4.8 gather_fusion
  30.4 3.1 collective-permute-start.24
  37.5 7.0 %collective-permute-done.24 = bf16[256,512]{1,0:T(8,128)(2,1)} collective-permute-done((bf16[256,512]{1,0:T(8,128)(2,1)}, bf16[256,512]{1,0:T(8,128)(2,1)}, u32[]{:S(2)}, u32[]{:S(2)}) %collective-permute-start.24) | collective-permute-done | bytes 262176 | tf_op jit(solution)/shard_map/ppermute | solution.py:913
  46.2 2.9 collective-permute-start.13
  49.1 3.5 collective-permute-start.14
  54.5 24.7 %collective-permute-done.25 = bf16[256,512]{1,0:T(8,128)(2,1)S(1)} collective-permute-done((bf16[256,512]{1,0:T(8,128)(2,1)}, bf16[256,512]{1,0:T(8,128)(2,1)S(1)}, u32[]{:S(2)}, u32[]{:S(2)}) %collective-permute-start.25) | collective-permute-done | bytes 262176 | tf_op jit(solution)/shard_map/ppermute | solution.py:913
  79.2 2.5 collective-permute-start.6
  81.7 23.5 %collective-permute-done.13 = bf16[256,512]{1,0:T(8,128)(2,1)S(1)} collective-permute-done((bf16[256,512]{1,0:T(8,128)(2,1)}, bf16[256,512]{1,0:T(8,128)(2,1)S(1)}, u32[]{:S(2)}, u32[]{:S(2)}) %collective-permute-start.13) | collective-permute-done | bytes 262176 | tf_op jit(solution)/shard_map/ppermute | solution.py:913
  106.6 13.2 %collective-permute-start.19 = (bf16[128,2048]{1,0:T(8,128)(2,1)S(1)}, bf16[128,2048]{1,0:T(8,128)(2,1)S(1)}, u32[]{:S(2)}, u32[]{:S(2)}) collective-permute-start(bf16[128,2048]{1,0:T(8,128)(2,1)S(1)} %bitcast.252), channel_id=1, source_target_pairs={{0,1},{1,0},{2,3},{3,2},{4,5},{5,4},{6,7},{7,6},{8,9},{9,8},{10,11... | collective-permute-start | bytes 1572872 | tf_op jit(solution)/shard_map/ppermute | solution.py:913
  128.8 8.8 %collective-permute-done.7 = bf16[512,512]{1,0:T(8,128)(2,1)S(1)} collective-permute-done((bf16[512,512]{1,0:T(8,128)(2,1)S(1)}, bf16[512,512]{1,0:T(8,128)(2,1)S(1)}, u32[]{:S(2)}, u32[]{:S(2)}) %collective-permute-start.7) | collective-permute-done | bytes 524320 | tf_op jit(solution)/shard_map/ppermute | solution.py:916
  137.7 8.8 %collective-permute-start.20 = (bf16[128,2048]{1,0:T(8,128)(2,1)S(1)}, bf16[128,2048]{1,0:T(8,128)(2,1)S(1)}, u32[]{:S(2)}, u32[]{:S(2)}) collective-permute-start(bf16[128,2048]{1,0:T(8,128)(2,1)S(1)} %bitcast.253), channel_id=1, source_target_pairs={{0,2},{1,3},{2,0},{3,1},{4,6},{5,7},{6,4},{7,5},{8,10},{9,11},{10,... | collective-permute-start | bytes 1572872 | tf_op jit(solution)/shard_map/ppermute | solution.py:913
  146.5 2.9 collective-permute-done.8
  150.7 1.9 collective-permute-start.27
  154.9 2.4 fusion.19
  157.3 2.5 fusion.66
  161.4 16.8 %collective-permute-done.20 = bf16[128,2048]{1,0:T(8,128)(2,1)S(1)} collective-permute-done((bf16[128,2048]{1,0:T(8,128)(2,1)S(1)}, bf16[128,2048]{1,0:T(8,128)(2,1)S(1)}, u32[]{:S(2)}, u32[]{:S(2)}) %collective-permute-start.20) | collective-permute-done | bytes 524320 | tf_op jit(solution)/shard_map/ppermute | solution.py:913
  179.3 1.9 collective-permute-done.10
  181.5 4.6 shard_map.212
  186.6 9.7 %collective-permute-done.27 = bf16[256,2048]{1,0:T(8,128)(2,1)S(1)} collective-permute-done((bf16[256,2048]{1,0:T(8,128)(2,1)}, bf16[256,2048]{1,0:T(8,128)(2,1)S(1)}, u32[]{:S(2)}, u32[]{:S(2)}) %collective-permute-start.27) | collective-permute-done | bytes 1048608 | tf_op jit(solution)/shard_map/ppermute | solution.py:916
  198.1 5.3 fusion.111
  208.4 2.6 copy.62
  212.0 7.6 %collective-permute-done.16 = bf16[128,2048]{1,0:T(8,128)(2,1)} collective-permute-done((bf16[128,2048]{1,0:T(8,128)(2,1)}, bf16[128,2048]{1,0:T(8,128)(2,1)}, u32[]{:S(2)}, u32[]{:S(2)}) %collective-permute-start.16) | collective-permute-done | bytes 524320 | tf_op jit(solution)/shard_map/ppermute | solution.py:916
  219.7 8.1 %collective-permute-done.17 = bf16[128,2048]{1,0:T(8,128)(2,1)} collective-permute-done((bf16[128,2048]{1,0:T(8,128)(2,1)}, bf16[128,2048]{1,0:T(8,128)(2,1)}, u32[]{:S(2)}, u32[]{:S(2)}) %collective-permute-start.17) | collective-permute-done | bytes 524320 | tf_op jit(solution)/shard_map/ppermute | solution.py:916
  227.8 2.3 multiply_reduce_fusion
  232.1 142.1 %shard_map.213 = (bf16[128,2048]{1,0:T(8,128)(2,1)}, f32[128,2048]{1,0:T(8,128)}, f32[1,2048]{1,0:T(1,128)}, bf16[2,4,128,2048]{3,2,1,0:T(8,128)(2,1)}, bf16[4,5...) custom-call(bf16[128,2048]{1,0:T(8,128)(2,1)} %multiply_convert_fusion.second_ref, f32[128,2048]{1,0:T(8,128)} %copy-done.11, ...), custom_call_target="tpu_custom_call" | custom-call | flops 38654705664 | bytes 37748736 | tf_op jit(solution)/shard_map/pallas_call | solution.py:819
  374.2 3.6 dynamic-slice_bitcast_fusion.2
  381.3 6.0 slice_bitcast_fusion.2
  389.6 18.2 %collective-permute-start.42 = (bf16[64,2048]{1,0:T(8,128)(2,1)}, bf16[64,2048]{1,0:T(8,128)(2,1)}, u32[]{:S(2)}, u32[]{:S(2)}) collective-permute-start(bf16[64,2048]{1,0:T(8,128)(2,1)} %get-tuple-element.67), channel_id=1, source_target_pairs={{0,1},{1,0},{2,3},{3,2},{4,5},{5,4},{6,7},{7,6},{8,9},{9,8},{10,11... | collective-permute-start | bytes 786440 | tf_op jit(solution)/shard_map/ppermute | solution.py:913
  407.8 3.4 convolution_convert_fusion.outgrad
  414.5 5.4 shard_map.214
  420.0 1.9 collective-permute-start.44
  422.0 10.5 %collective-permute-done.43 = bf16[64,2048]{1,0:T(8,128)(2,1)S(1)} collective-permute-done((bf16[64,2048]{1,0:T(8,128)(2,1)}, bf16[64,2048]{1,0:T(8,128)(2,1)S(1)}, u32[]{:S(2)}, u32[]{:S(2)}) %collective-permute-start.43) | collective-permute-done | bytes 262176 | tf_op jit(solution)/shard_map/ppermute | solution.py:913
  433.1 2.0 fusion.81
  435.8 2.9 fusion.16
  438.8 8.7 %collective-permute-start.55 = (bf16[64,2048]{1,0:T(8,128)(2,1)S(1)}, bf16[64,2048]{1,0:T(8,128)(2,1)S(1)}, u32[]{:S(2)}, u32[]{:S(2)}) collective-permute-start(bf16[64,2048]{1,0:T(8,128)(2,1)S(1)} %get-tuple-element.91), channel_id=1, source_target_pairs={{0,1},{1,0},{2,3},{3,2},{4,5},{5,4},{6,7},{7,6},{8,9},{9,8},{10,11... | collective-permute-start | bytes 786440 | tf_op jit(solution)/shard_map/ppermute | solution.py:913
  448.2 1.8 collective-permute-start.57
  450.3 2.8 fusion.62
  453.2 2.7 fusion.17
  456.5 2.1 collective-permute-start.46
  458.5 10.3 %collective-permute-done.56 = bf16[64,2048]{1,0:T(8,128)(2,1)S(1)} collective-permute-done((bf16[64,2048]{1,0:T(8,128)(2,1)S(1)}, bf16[64,2048]{1,0:T(8,128)(2,1)S(1)}, u32[]{:S(2)}, u32[]{:S(2)}) %collective-permute-start.56) | collective-permute-done | bytes 262176 | tf_op jit(solution)/shard_map/ppermute | solution.py:913
  468.8 3.6 collective-permute-start.35
  473.5 1.8 collective-permute-start.37
  475.3 2.4 fusion.112
  477.8 14.4 %collective-permute-done.35 = bf16[8,64,512]{2,1,0:T(8,128)(2,1)S(1)} collective-permute-done((bf16[8,64,512]{2,1,0:T(8,128)(2,1)S(1)}, bf16[8,64,512]{2,1,0:T(8,128)(2,1)S(1)}, u32[]{:S(2)}, u32[]{:S(2)}) %collective-permute-start.35) | collective-permute-done | bytes 524320 | tf_op jit(solution)/shard_map/ppermute | solution.py:913
  493.7 17.5 %collective-permute-done.36 = bf16[8,64,512]{2,1,0:T(8,128)(2,1)S(1)} collective-permute-done((bf16[8,64,512]{2,1,0:T(8,128)(2,1)S(1)}, bf16[8,64,512]{2,1,0:T(8,128)(2,1)S(1)}, u32[]{:S(2)}, u32[]{:S(2)}) %collective-permute-start.36) | collective-permute-done | bytes 524320 | tf_op jit(solution)/shard_map/ppermute | solution.py:913
  514.0 30.2 %collective-permute-done.58 = bf16[64,2048]{1,0:T(8,128)(2,1)S(1)} collective-permute-done((bf16[64,2048]{1,0:T(8,128)(2,1)S(1)}, bf16[64,2048]{1,0:T(8,128)(2,1)S(1)}, u32[]{:S(2)}, u32[]{:S(2)}) %collective-permute-start.58) | collective-permute-done | bytes 262176 | tf_op jit(solution)/shard_map/ppermute | solution.py:916
  546.0 12.7 %collective-permute-done.59 = bf16[64,2048]{1,0:T(8,128)(2,1)S(1)} collective-permute-done((bf16[64,2048]{1,0:T(8,128)(2,1)S(1)}, bf16[64,2048]{1,0:T(8,128)(2,1)S(1)}, u32[]{:S(2)}, u32[]{:S(2)}) %collective-permute-start.59) | collective-permute-done | bytes 262176 | tf_op jit(solution)/shard_map/ppermute | solution.py:916
  563.2 2.9 collective-permute-done.39
  569.4 13.8 %collective-permute-done.41 = bf16[64,1024]{1,0:T(8,128)(2,1)S(1)} collective-permute-done((bf16[64,1024]{1,0:T(8,128)(2,1)S(1)}, bf16[64,1024]{1,0:T(8,128)(2,1)S(1)}, u32[]{:S(2)}, u32[]{:S(2)}) %collective-permute-start.41) | collective-permute-done | bytes 131104 | tf_op jit(solution)/shard_map/ppermute | solution.py:916
  583.6 2.0 collective-permute-start.34
  585.7 20.7 %collective-permute-done.33 = bf16[128,2048]{1,0:T(8,128)(2,1)S(1)} collective-permute-done((bf16[128,2048]{1,0:T(8,128)(2,1)S(1)}, bf16[128,2048]{1,0:T(8,128)(2,1)S(1)}, u32[]{:S(2)}, u32[]{:S(2)}) %collective-permute-start.33) | collective-permute-done | bytes 524320 | tf_op jit(solution)/shard_map/ppermute | solution.py:916
  607.7 2.1 collective-permute-start.62
  609.9 1.9 collective-permute-start.63
  611.8 5.2 fusion.9
  617.8 2.0 collective-permute-done.64
  627.8 2.5 collective-permute-start.50
  630.6 1.9 collective-permute-start.51
  632.6 17.4 %collective-permute-done.49 = bf16[64,4096]{1,0:T(8,128)(2,1)S(1)} collective-permute-done((bf16[64,4096]{1,0:T(8,128)(2,1)S(1)}, bf16[64,4096]{1,0:T(8,128)(2,1)S(1)}, u32[]{:S(2)}, u32[]{:S(2)}) %collective-permute-start.49) | collective-permute-done | bytes 524320 | tf_op jit(solution)/shard_map/ppermute | solution.py:913
  650.2 15.9 %collective-permute-done.50 = bf16[64,4096]{1,0:T(8,128)(2,1)S(1)} collective-permute-done((bf16[64,4096]{1,0:T(8,128)(2,1)S(1)}, bf16[64,4096]{1,0:T(8,128)(2,1)S(1)}, u32[]{:S(2)}, u32[]{:S(2)}) %collective-permute-start.50) | collective-permute-done | bytes 524320 | tf_op jit(solution)/shard_map/ppermute | solution.py:913
  (281 shorter events, 85.7 us)
Async XLA Ops:
  0.7 45.5 %collective-permute-start = (bf16[128,2048]{1,0:T(8,128)(2,1)}, bf16[128,2048]{1,0:T(8,128)(2,1)}, u32[]{:S(2)}, u32[]{:S(2)}) collective-permute-start(bf16[128,2048]{1,0:T(8,128)(2,1)} %bitcast.233), channel_id=1, source_target_pairs={{0,8},{4,12},{8,0},{12,4},{16,24},{20,28},{24,16},{28,20},{1,9},{5... | collective-permute-start | bytes 1572872 | tf_op jit(solution)/shard_map/ppermute | solution.py:916
  3.7 45.4 %collective-permute-start.1 = (bf16[128,2048]{1,0:T(8,128)(2,1)}, bf16[128,2048]{1,0:T(8,128)(2,1)}, u32[]{:S(2)}, u32[]{:S(2)}) collective-permute-start(bf16[128,2048]{1,0:T(8,128)(2,1)} %bitcast.234), channel_id=1, source_target_pairs={{0,16},{4,20},{8,24},{12,28},{16,0},{20,4},{24,8},{28,12},{1,17},{... | collective-permute-start | bytes 1572872 | tf_op jit(solution)/shard_map/ppermute | solution.py:916
  5.2 47.5 %collective-permute-start.2 = (bf16[128,2048]{1,0:T(8,128)(2,1)}, bf16[128,2048]{1,0:T(8,128)(2,1)S(1)}, u32[]{:S(2)}, u32[]{:S(2)}) collective-permute-start(bf16[128,2048]{1,0:T(8,128)(2,1)} %bitcast.235), channel_id=1, source_target_pairs={{0,24},{4,28},{8,16},{12,20},{16,8},{20,12},{24,0},{28,4},{1,25},{... | collective-permute-start | bytes 1572872 | tf_op jit(solution)/shard_map/ppermute | solution.py:916
  8.5 21.9 %collective-permute-start.23 = (bf16[256,512]{1,0:T(8,128)(2,1)}, bf16[256,512]{1,0:T(8,128)(2,1)S(1)}, u32[]{:S(2)}, u32[]{:S(2)}) collective-permute-start(bf16[256,512]{1,0:T(8,128)(2,1)} %get-tuple-element.48), channel_id=1, source_target_pairs={{0,1},{1,0},{2,3},{3,2},{4,5},{5,4},{6,7},{7,6},{8,9},{9,8},{10,11... | collective-permute-start | bytes 786440 | tf_op jit(solution)/shard_map/ppermute | solution.py:913
  13.5 20.8 %collective-permute-start.12 = (bf16[256,512]{1,0:T(8,128)(2,1)}, bf16[256,512]{1,0:T(8,128)(2,1)}, u32[]{:S(2)}, u32[]{:S(2)}) collective-permute-start(bf16[256,512]{1,0:T(8,128)(2,1)} %get-tuple-element.43), channel_id=1, source_target_pairs={{0,1},{1,0},{2,3},{3,2},{4,5},{5,4},{6,7},{7,6},{8,9},{9,8},{10,11... | collective-permute-start | bytes 786440 | tf_op jit(solution)/shard_map/ppermute | solution.py:913
  30.4 14.1 %collective-permute-start.24 = (bf16[256,512]{1,0:T(8,128)(2,1)}, bf16[256,512]{1,0:T(8,128)(2,1)}, u32[]{:S(2)}, u32[]{:S(2)}) collective-permute-start(bf16[256,512]{1,0:T(8,128)(2,1)} %get-tuple-element.50), channel_id=1, source_target_pairs={{0,2},{1,3},{2,0},{3,1},{4,6},{5,7},{6,4},{7,5},{8,10},{9,11},{10,... | collective-permute-start | bytes 786440 | tf_op jit(solution)/shard_map/ppermute | solution.py:913
  34.3 88.2 %collective-permute-start.4 = (bf16[512,512]{1,0:T(8,128)(2,1)S(1)}, bf16[512,512]{1,0:T(8,128)(2,1)S(1)}, u32[]{:S(2)}, u32[]{:S(2)}) collective-permute-start(bf16[512,512]{1,0:T(8,128)(2,1)S(1)} %get-tuple-element.121), channel_id=1, source_target_pairs={{0,1},{1,0},{2,3},{3,2},{4,5},{5,4},{6,7},{7,6},{8,9},{9,8},{10,11... | collective-permute-start | bytes 1572872 | tf_op jit(solution)/shard_map/ppermute | solution.py:913
  44.5 78.0 %collective-permute-start.5 = (bf16[512,512]{1,0:T(8,128)(2,1)S(1)}, bf16[512,512]{1,0:T(8,128)(2,1)S(1)}, u32[]{:S(2)}, u32[]{:S(2)}) collective-permute-start(bf16[512,512]{1,0:T(8,128)(2,1)S(1)} %get-tuple-element.121), channel_id=1, source_target_pairs={{0,2},{1,3},{2,0},{3,1},{4,6},{5,7},{6,4},{7,5},{8,10},{9,11},{10,... | collective-permute-start | bytes 1572872 | tf_op jit(solution)/shard_map/ppermute | solution.py:913
  46.2 59.0 %collective-permute-start.13 = (bf16[256,512]{1,0:T(8,128)(2,1)}, bf16[256,512]{1,0:T(8,128)(2,1)S(1)}, u32[]{:S(2)}, u32[]{:S(2)}) collective-permute-start(bf16[256,512]{1,0:T(8,128)(2,1)} %get-tuple-element.43), channel_id=1, source_target_pairs={{0,2},{1,3},{2,0},{3,1},{4,6},{5,7},{6,4},{7,5},{8,10},{9,11},{10,... | collective-permute-start | bytes 786440 | tf_op jit(solution)/shard_map/ppermute | solution.py:913
  49.1 57.5 %collective-permute-start.14 = (bf16[256,512]{1,0:T(8,128)(2,1)}, bf16[256,512]{1,0:T(8,128)(2,1)S(1)}, u32[]{:S(2)}, u32[]{:S(2)}) collective-permute-start(bf16[256,512]{1,0:T(8,128)(2,1)} %get-tuple-element.43), channel_id=1, source_target_pairs={{0,3},{1,2},{2,1},{3,0},{4,7},{5,6},{6,5},{7,4},{8,11},{9,10},{10,... | collective-permute-start | bytes 786440 | tf_op jit(solution)/shard_map/ppermute | solution.py:913
  52.6 26.5 %collective-permute-start.25 = (bf16[256,512]{1,0:T(8,128)(2,1)}, bf16[256,512]{1,0:T(8,128)(2,1)S(1)}, u32[]{:S(2)}, u32[]{:S(2)}) collective-permute-start(bf16[256,512]{1,0:T(8,128)(2,1)} %get-tuple-element.47), channel_id=1, source_target_pairs={{0,3},{1,2},{2,1},{3,0},{4,7},{5,6},{6,5},{7,4},{8,11},{9,10},{10,... | collective-permute-start | bytes 786440 | tf_op jit(solution)/shard_map/ppermute | solution.py:913
  79.2 43.3 %collective-permute-start.6 = (bf16[512,512]{1,0:T(8,128)(2,1)S(1)}, bf16[512,512]{1,0:T(8,128)(2,1)S(1)}, u32[]{:S(2)}, u32[]{:S(2)}) collective-permute-start(bf16[512,512]{1,0:T(8,128)(2,1)S(1)} %get-tuple-element.121), channel_id=1, source_target_pairs={{0,3},{1,2},{2,1},{3,0},{4,7},{5,6},{6,5},{7,4},{8,11},{9,10},{10,... | collective-permute-start | bytes 1572872 | tf_op jit(solution)/shard_map/ppermute | solution.py:913
  105.2 45.6 %collective-permute-start.3 = (bf16[512,2048]{1,0:T(8,128)(2,1)S(1)}, bf16[512,2048]{1,0:T(8,128)(2,1)S(1)}, u32[]{:S(2)}, u32[]{:S(2)}) collective-permute-start(bf16[512,2048]{1,0:T(8,128)(2,1)S(1)} %pad_maximum_fusion.1), channel_id=1, source_target_pairs={{0,4},{4,0},{8,12},{12,8},{16,20},{20,16},{24,28},{28,24},{1,5},{5... | collective-permute-start | bytes 6291464 | tf_op jit(solution)/shard_map/ppermute | solution.py:919
  106.6 53.3 %collective-permute-start.19 = (bf16[128,2048]{1,0:T(8,128)(2,1)S(1)}, bf16[128,2048]{1,0:T(8,128)(2,1)S(1)}, u32[]{:S(2)}, u32[]{:S(2)}) collective-permute-start(bf16[128,2048]{1,0:T(8,128)(2,1)S(1)} %bitcast.252), channel_id=1, source_target_pairs={{0,1},{1,0},{2,3},{3,2},{4,5},{5,4},{6,7},{7,6},{8,9},{9,8},{10,11... | collective-permute-start | bytes 1572872 | tf_op jit(solution)/shard_map/ppermute | solution.py:913
  122.9 14.8 %collective-permute-start.7 = (bf16[512,512]{1,0:T(8,128)(2,1)S(1)}, bf16[512,512]{1,0:T(8,128)(2,1)S(1)}, u32[]{:S(2)}, u32[]{:S(2)}) collective-permute-start(bf16[512,512]{1,0:T(8,128)(2,1)S(1)} %get-tuple-element.80), channel_id=1, source_target_pairs={{0,8},{4,12},{8,0},{12,4},{16,24},{20,28},{24,16},{28,20},{1,9},{5... | collective-permute-start | bytes 1572872 | tf_op jit(solution)/shard_map/ppermute | solution.py:916
  124.4 25.0 %collective-permute-start.8 = (bf16[512,512]{1,0:T(8,128)(2,1)S(1)}, bf16[512,512]{1,0:T(8,128)(2,1)S(1)}, u32[]{:S(2)}, u32[]{:S(2)}) collective-permute-start(bf16[512,512]{1,0:T(8,128)(2,1)S(1)} %get-tuple-element.79), channel_id=1, source_target_pairs={{0,16},{4,20},{8,24},{12,28},{16,0},{20,4},{24,8},{28,12},{1,17},{... | collective-permute-start | bytes 1572872 | tf_op jit(solution)/shard_map/ppermute | solution.py:916
  125.9 24.4 %collective-permute-start.9 = (bf16[512,512]{1,0:T(8,128)(2,1)S(1)}, bf16[512,512]{1,0:T(8,128)(2,1)S(1)}, u32[]{:S(2)}, u32[]{:S(2)}) collective-permute-start(bf16[512,512]{1,0:T(8,128)(2,1)S(1)} %get-tuple-element.78), channel_id=1, source_target_pairs={{0,24},{4,28},{8,16},{12,20},{16,8},{20,12},{24,0},{28,4},{1,25},{... | collective-permute-start | bytes 1572872 | tf_op jit(solution)/shard_map/ppermute | solution.py:916
  137.7 40.5 %collective-permute-start.20 = (bf16[128,2048]{1,0:T(8,128)(2,1)S(1)}, bf16[128,2048]{1,0:T(8,128)(2,1)S(1)}, u32[]{:S(2)}, u32[]{:S(2)}) collective-permute-start(bf16[128,2048]{1,0:T(8,128)(2,1)S(1)} %bitcast.253), channel_id=1, source_target_pairs={{0,2},{1,3},{2,0},{3,1},{4,6},{5,7},{6,4},{7,5},{8,10},{9,11},{10,... | collective-permute-start | bytes 1572872 | tf_op jit(solution)/shard_map/ppermute | solution.py:913
  149.4 28.7 %collective-permute-start.21 = (bf16[128,2048]{1,0:T(8,128)(2,1)S(1)}, bf16[128,2048]{1,0:T(8,128)(2,1)S(1)}, u32[]{:S(2)}, u32[]{:S(2)}) collective-permute-start(bf16[128,2048]{1,0:T(8,128)(2,1)S(1)} %bitcast.254), channel_id=1, source_target_pairs={{0,3},{1,2},{2,1},{3,0},{4,7},{5,6},{6,5},{7,4},{8,11},{9,10},{10,... | collective-permute-start | bytes 1572872 | tf_op jit(solution)/shard_map/ppermute | solution.py:913
  150.3 28.7 %collective-permute-start.26 = (bf16[256,2048]{1,0:T(8,128)(2,1)}, bf16[256,2048]{1,0:T(8,128)(2,1)S(1)}, u32[]{:S(2)}, u32[]{:S(2)}) collective-permute-start(bf16[256,2048]{1,0:T(8,128)(2,1)} %constant_dynamic-update-slice_fusion.4), channel_id=1, source_target_pairs={{0,8},{4,12},{8,0},{12,4},{16,24},{20,28},{24,16},{28,20},{1,9},{5... | collective-permute-start | bytes 3145736 | tf_op jit(solution)/shard_map/ppermute | solution.py:916
  150.7 45.5 %collective-permute-start.27 = (bf16[256,2048]{1,0:T(8,128)(2,1)}, bf16[256,2048]{1,0:T(8,128)(2,1)S(1)}, u32[]{:S(2)}, u32[]{:S(2)}) collective-permute-start(bf16[256,2048]{1,0:T(8,128)(2,1)} %constant_dynamic-update-slice_fusion.4), channel_id=1, source_target_pairs={{0,16},{4,20},{8,24},{12,28},{16,0},{20,4},{24,8},{28,12},{1,17},{... | collective-permute-start | bytes 3145736 | tf_op jit(solution)/shard_map/ppermute | solution.py:916
  159.9 38.0 %collective-permute-start.28 = (bf16[256,2048]{1,0:T(8,128)(2,1)}, bf16[256,2048]{1,0:T(8,128)(2,1)S(1)}, u32[]{:S(2)}, u32[]{:S(2)}) collective-permute-start(bf16[256,2048]{1,0:T(8,128)(2,1)} %constant_dynamic-update-slice_fusion.4), channel_id=1, source_target_pairs={{0,24},{4,28},{8,16},{12,20},{16,8},{20,12},{24,0},{28,4},{1,25},{... | collective-permute-start | bytes 3145736 | tf_op jit(solution)/shard_map/ppermute | solution.py:916
  178.2 19.9 %collective-permute-start.15 = (bf16[256,2048]{1,0:T(8,128)(2,1)}, bf16[256,2048]{1,0:T(8,128)(2,1)S(1)}, u32[]{:S(2)}, u32[]{:S(2)}) collective-permute-start(bf16[256,2048]{1,0:T(8,128)(2,1)} %constant_dynamic-update-slice_fusion.7), channel_id=1, source_target_pairs={{0,4},{4,0},{8,12},{12,8},{16,20},{20,16},{24,28},{28,24},{1,5},{5... | collective-permute-start | bytes 3145736 | tf_op jit(solution)/shard_map/ppermute | solution.py:919
  179.0 29.0 %collective-permute-start.22 = (bf16[4,128,2048]{2,1,0:T(8,128)(2,1)S(1)}, bf16[4,128,2048]{2,1,0:T(8,128)(2,1)S(1)}, u32[]{:S(2)}, u32[]{:S(2)}) collective-permute-start(bf16[4,128,2048]{2,1,0:T(8,128)(2,1)S(1)} %get-tuple-element.74), channel_id=1, source_target_pairs={{0,4},{4,0},{8,12},{12,8},{16,20},{20,16},{24,28},{28,24},{1,5},{5... | collective-permute-start | bytes 6291464 | tf_op jit(solution)/shard_map/ppermute | solution.py:919
  186.1 12.0 %collective-permute-start.11 = (bf16[512,256]{1,0:T(8,128)(2,1)S(1)}, bf16[512,256]{1,0:T(8,128)(2,1)S(1)}, u32[]{:S(2)}, u32[]{:S(2)}) collective-permute-start(bf16[512,256]{1,0:T(8,128)(2,1)S(1)} %get-tuple-element.117), channel_id=1, source_target_pairs={{0,4},{4,0},{8,12},{12,8},{16,20},{20,16},{24,28},{28,24},{1,5},{5... | collective-permute-start | bytes 786440 | tf_op jit(solution)/shard_map/ppermute | solution.py:919
  204.5 15.2 %collective-permute-start.16 = (bf16[128,2048]{1,0:T(8,128)(2,1)}, bf16[128,2048]{1,0:T(8,128)(2,1)}, u32[]{:S(2)}, u32[]{:S(2)}) collective-permute-start(bf16[128,2048]{1,0:T(8,128)(2,1)} %get-tuple-element.75), channel_id=1, source_target_pairs={{0,8},{4,12},{8,0},{12,4},{16,24},{20,28},{24,16},{28,20},{1,9},{5... | collective-permute-start | bytes 1572872 | tf_op jit(solution)/shard_map/ppermute | solution.py:916
  205.4 22.4 %collective-permute-start.17 = (bf16[128,2048]{1,0:T(8,128)(2,1)}, bf16[128,2048]{1,0:T(8,128)(2,1)}, u32[]{:S(2)}, u32[]{:S(2)}) collective-permute-start(bf16[128,2048]{1,0:T(8,128)(2,1)} %get-tuple-element.77), channel_id=1, source_target_pairs={{0,16},{4,20},{8,24},{12,28},{16,0},{20,4},{24,8},{28,12},{1,17},{... | collective-permute-start | bytes 1572872 | tf_op jit(solution)/shard_map/ppermute | solution.py:916
  207.1 20.7 %collective-permute-start.18 = (bf16[128,2048]{1,0:T(8,128)(2,1)}, bf16[128,2048]{1,0:T(8,128)(2,1)}, u32[]{:S(2)}, u32[]{:S(2)}) collective-permute-start(bf16[128,2048]{1,0:T(8,128)(2,1)} %get-tuple-element.76), channel_id=1, source_target_pairs={{0,24},{4,28},{8,16},{12,20},{16,8},{20,12},{24,0},{28,4},{1,25},{... | collective-permute-start | bytes 1572872 | tf_op jit(solution)/shard_map/ppermute | solution.py:916
  377.8 57.3 %collective-permute-start.52 = (bf16[4,64,2048]{2,1,0:T(8,128)(2,1)}, bf16[4,64,2048]{2,1,0:T(8,128)(2,1)}, u32[]{:S(2)}, u32[]{:S(2)}) collective-permute-start(bf16[4,64,2048]{2,1,0:T(8,128)(2,1)} %get-tuple-element.51), channel_id=1, source_target_pairs={{0,8},{4,12},{8,0},{12,4},{16,24},{20,28},{24,16},{28,20},{1,9},{5... | collective-permute-start | bytes 3145736 | tf_op jit(solution)/shard_map/ppermute | solution.py:916
  379.3 56.5 %collective-permute-start.53 = (bf16[4,64,2048]{2,1,0:T(8,128)(2,1)}, bf16[4,64,2048]{2,1,0:T(8,128)(2,1)}, u32[]{:S(2)}, u32[]{:S(2)}) collective-permute-start(bf16[4,64,2048]{2,1,0:T(8,128)(2,1)} %get-tuple-element.53), channel_id=1, source_target_pairs={{0,16},{4,20},{8,24},{12,28},{16,0},{20,4},{24,8},{28,12},{1,17},{... | collective-permute-start | bytes 3145736 | tf_op jit(solution)/shard_map/ppermute | solution.py:916
  379.9 56.0 %collective-permute-start.54 = (bf16[4,64,2048]{2,1,0:T(8,128)(2,1)}, bf16[4,64,2048]{2,1,0:T(8,128)(2,1)}, u32[]{:S(2)}, u32[]{:S(2)}) collective-permute-start(bf16[4,64,2048]{2,1,0:T(8,128)(2,1)} %get-tuple-element.52), channel_id=1, source_target_pairs={{0,24},{4,28},{8,16},{12,20},{16,8},{20,12},{24,0},{28,4},{1,25},{... | collective-permute-start | bytes 3145736 | tf_op jit(solution)/shard_map/ppermute | solution.py:916
  389.6 30.4 %collective-permute-start.42 = (bf16[64,2048]{1,0:T(8,128)(2,1)}, bf16[64,2048]{1,0:T(8,128)(2,1)}, u32[]{:S(2)}, u32[]{:S(2)}) collective-permute-start(bf16[64,2048]{1,0:T(8,128)(2,1)} %get-tuple-element.67), channel_id=1, source_target_pairs={{0,1},{1,0},{2,3},{3,2},{4,5},{5,4},{6,7},{7,6},{8,9},{9,8},{10,11... | collective-permute-start | bytes 786440 | tf_op jit(solution)/shard_map/ppermute | solution.py:913
  412.5 20.1 %collective-permute-start.43 = (bf16[64,2048]{1,0:T(8,128)(2,1)}, bf16[64,2048]{1,0:T(8,128)(2,1)S(1)}, u32[]{:S(2)}, u32[]{:S(2)}) collective-permute-start(bf16[64,2048]{1,0:T(8,128)(2,1)} %get-tuple-element.69), channel_id=1, source_target_pairs={{0,2},{1,3},{2,0},{3,1},{4,6},{5,7},{6,4},{7,5},{8,10},{9,11},{10,... | collective-permute-start | bytes 786440 | tf_op jit(solution)/shard_map/ppermute | solution.py:913
  420.0 12.5 %collective-permute-start.44 = (bf16[64,2048]{1,0:T(8,128)(2,1)S(1)}, bf16[64,2048]{1,0:T(8,128)(2,1)S(1)}, u32[]{:S(2)}, u32[]{:S(2)}) collective-permute-start(bf16[64,2048]{1,0:T(8,128)(2,1)S(1)} %get-tuple-element.68), channel_id=1, source_target_pairs={{0,3},{1,2},{2,1},{3,0},{4,7},{5,6},{6,5},{7,4},{8,11},{9,10},{10,... | collective-permute-start | bytes 786440 | tf_op jit(solution)/shard_map/ppermute | solution.py:913
  432.5 40.4 %collective-permute-start.31 = (bf16[2048,512]{1,0:T(8,128)(2,1)S(1)}, bf16[2048,512]{1,0:T(8,128)(2,1)S(1)}, u32[]{:S(2)}, u32[]{:S(2)}) collective-permute-start(bf16[2048,512]{1,0:T(8,128)(2,1)S(1)} %copy-done.16), channel_id=1, source_target_pairs={{0,4},{4,0},{8,12},{12,8},{16,20},{20,16},{24,28},{28,24},{1,5},{5... | collective-permute-start | bytes 6291464 | tf_op jit(solution)/shard_map/ppermute | solution.py:919
  432.5 15.6 %collective-permute-start.29 = (f32[1024,256]{1,0:T(8,128)S(1)}, f32[1024,256]{1,0:T(8,128)S(1)}, u32[]{:S(2)}, u32[]{:S(2)}) collective-permute-start(f32[1024,256]{1,0:T(8,128)S(1)} %broadcast_select_fusion), channel_id=1, source_target_pairs={{0,4},{4,0},{8,12},{12,8},{16,20},{20,16},{24,28},{28,24},{1,5},{5... | collective-permute-start | bytes 3145736 | tf_op jit(solution)/shard_map/ppermute | solution.py:919
  435.1 174.8 %collective-permute-start.45 = (bf16[512,2048]{1,0:T(8,128)(2,1)}, bf16[512,2048]{1,0:T(8,128)(2,1)}, u32[]{:S(2)}, u32[]{:S(2)}) collective-permute-start(bf16[512,2048]{1,0:T(8,128)(2,1)} %get-tuple-element.44), channel_id=1, source_target_pairs={{0,8},{4,12},{8,0},{12,4},{16,24},{20,28},{24,16},{28,20},{1,9},{5... | collective-permute-start | bytes 6291464 | tf_op jit(solution)/shard_map/ppermute | solution.py:916
  438.8 17.6 %collective-permute-start.55 = (bf16[64,2048]{1,0:T(8,128)(2,1)S(1)}, bf16[64,2048]{1,0:T(8,128)(2,1)S(1)}, u32[]{:S(2)}, u32[]{:S(2)}) collective-permute-start(bf16[64,2048]{1,0:T(8,128)(2,1)S(1)} %get-tuple-element.91), channel_id=1, source_target_pairs={{0,1},{1,0},{2,3},{3,2},{4,5},{5,4},{6,7},{7,6},{8,9},{9,8},{10,11... | collective-permute-start | bytes 786440 | tf_op jit(solution)/shard_map/ppermute | solution.py:913
  447.5 21.3 %collective-permute-start.56 = (bf16[64,2048]{1,0:T(8,128)(2,1)S(1)}, bf16[64,2048]{1,0:T(8,128)(2,1)S(1)}, u32[]{:S(2)}, u32[]{:S(2)}) collective-permute-start(bf16[64,2048]{1,0:T(8,128)(2,1)S(1)} %get-tuple-element.90), channel_id=1, source_target_pairs={{0,2},{1,3},{2,0},{3,1},{4,6},{5,7},{6,4},{7,5},{8,10},{9,11},{10,... | collective-permute-start | bytes 786440 | tf_op jit(solution)/shard_map/ppermute | solution.py:913
  448.2 20.7 %collective-permute-start.57 = (bf16[64,2048]{1,0:T(8,128)(2,1)S(1)}, bf16[64,2048]{1,0:T(8,128)(2,1)S(1)}, u32[]{:S(2)}, u32[]{:S(2)}) collective-permute-start(bf16[64,2048]{1,0:T(8,128)(2,1)S(1)} %get-tuple-element.89), channel_id=1, source_target_pairs={{0,3},{1,2},{2,1},{3,0},{4,7},{5,6},{6,5},{7,4},{8,11},{9,10},{10,... | collective-permute-start | bytes 786440 | tf_op jit(solution)/shard_map/ppermute | solution.py:913
  456.5 155.3 %collective-permute-start.46 = (bf16[512,2048]{1,0:T(8,128)(2,1)}, bf16[512,2048]{1,0:T(8,128)(2,1)}, u32[]{:S(2)}, u32[]{:S(2)}) collective-permute-start(bf16[512,2048]{1,0:T(8,128)(2,1)} %get-tuple-element.46), channel_id=1, source_target_pairs={{0,16},{4,20},{8,24},{12,28},{16,0},{20,4},{24,8},{28,12},{1,17},{... | collective-permute-start | bytes 6291464 | tf_op jit(solution)/shard_map/ppermute | solution.py:916
  468.8 4.7 collective-permute-start.30
  468.8 23.3 %collective-permute-start.35 = (bf16[8,64,512]{2,1,0:T(8,128)(2,1)S(1)}, bf16[8,64,512]{2,1,0:T(8,128)(2,1)S(1)}, u32[]{:S(2)}, u32[]{:S(2)}) collective-permute-start(bf16[8,64,512]{2,1,0:T(8,128)(2,1)S(1)} %get-tuple-element.54), channel_id=1, source_target_pairs={{0,1},{1,0},{2,3},{3,2},{4,5},{5,4},{6,7},{7,6},{8,9},{9,8},{10,11... | collective-permute-start | bytes 1572872 | tf_op jit(solution)/shard_map/ppermute | solution.py:913
  472.9 38.3 %collective-permute-start.36 = (bf16[8,64,512]{2,1,0:T(8,128)(2,1)S(1)}, bf16[8,64,512]{2,1,0:T(8,128)(2,1)S(1)}, u32[]{:S(2)}, u32[]{:S(2)}) collective-permute-start(bf16[8,64,512]{2,1,0:T(8,128)(2,1)S(1)} %get-tuple-element.56), channel_id=1, source_target_pairs={{0,2},{1,3},{2,0},{3,1},{4,6},{5,7},{6,4},{7,5},{8,10},{9,11},{10,... | collective-permute-start | bytes 1572872 | tf_op jit(solution)/shard_map/ppermute | solution.py:913
  473.5 39.4 %collective-permute-start.37 = (bf16[8,64,512]{2,1,0:T(8,128)(2,1)S(1)}, bf16[8,64,512]{2,1,0:T(8,128)(2,1)S(1)}, u32[]{:S(2)}, u32[]{:S(2)}) collective-permute-start(bf16[8,64,512]{2,1,0:T(8,128)(2,1)S(1)} %get-tuple-element.55), channel_id=1, source_target_pairs={{0,3},{1,2},{2,1},{3,0},{4,7},{5,6},{6,5},{7,4},{8,11},{9,10},{10,... | collective-permute-start | bytes 1572872 | tf_op jit(solution)/shard_map/ppermute | solution.py:913
  492.2 119.6 %collective-permute-start.47 = (bf16[512,2048]{1,0:T(8,128)(2,1)}, bf16[512,2048]{1,0:T(8,128)(2,1)}, u32[]{:S(2)}, u32[]{:S(2)}) collective-permute-start(bf16[512,2048]{1,0:T(8,128)(2,1)} %get-tuple-element.45), channel_id=1, source_target_pairs={{0,24},{4,28},{8,16},{12,20},{16,8},{20,12},{24,0},{28,4},{1,25},{... | collective-permute-start | bytes 6291464 | tf_op jit(solution)/shard_map/ppermute | solution.py:916
  511.2 33.0 %collective-permute-start.58 = (bf16[64,2048]{1,0:T(8,128)(2,1)S(1)}, bf16[64,2048]{1,0:T(8,128)(2,1)S(1)}, u32[]{:S(2)}, u32[]{:S(2)}) collective-permute-start(bf16[64,2048]{1,0:T(8,128)(2,1)S(1)} %get-tuple-element.87), channel_id=1, source_target_pairs={{0,8},{4,12},{8,0},{12,4},{16,24},{20,28},{24,16},{28,20},{1,9},{5... | collective-permute-start | bytes 786440 | tf_op jit(solution)/shard_map/ppermute | solution.py:916
  512.9 45.8 %collective-permute-start.59 = (bf16[64,2048]{1,0:T(8,128)(2,1)S(1)}, bf16[64,2048]{1,0:T(8,128)(2,1)S(1)}, u32[]{:S(2)}, u32[]{:S(2)}) collective-permute-start(bf16[64,2048]{1,0:T(8,128)(2,1)S(1)} %get-tuple-element.86), channel_id=1, source_target_pairs={{0,16},{4,20},{8,24},{12,28},{16,0},{20,4},{24,8},{28,12},{1,17},{... | collective-permute-start | bytes 786440 | tf_op jit(solution)/shard_map/ppermute | solution.py:916
  544.2 14.6 %collective-permute-start.60 = (bf16[64,2048]{1,0:T(8,128)(2,1)S(1)}, bf16[64,2048]{1,0:T(8,128)(2,1)S(1)}, u32[]{:S(2)}, u32[]{:S(2)}) collective-permute-start(bf16[64,2048]{1,0:T(8,128)(2,1)S(1)} %get-tuple-element.85), channel_id=1, source_target_pairs={{0,24},{4,28},{8,16},{12,20},{16,8},{20,12},{24,0},{28,4},{1,25},{... | collective-permute-start | bytes 786440 | tf_op jit(solution)/shard_map/ppermute | solution.py:916
  560.5 5.6 collective-permute-start.39
  562.2 5.6 collective-permute-start.40
  566.1 17.5 %collective-permute-start.32 = (bf16[128,2048]{1,0:T(8,128)(2,1)S(1)}, bf16[128,2048]{1,0:T(8,128)(2,1)S(1)}, u32[]{:S(2)}, u32[]{:S(2)}) collective-permute-start(bf16[128,2048]{1,0:T(8,128)(2,1)S(1)} %get-tuple-element.70), channel_id=1, source_target_pairs={{0,8},{4,12},{8,0},{12,4},{16,24},{20,28},{24,16},{28,20},{1,9},{5... | collective-permute-start | bytes 1572872 | tf_op jit(solution)/shard_map/ppermute | solution.py:916
  567.7 15.5 %collective-permute-start.41 = (bf16[64,1024]{1,0:T(8,128)(2,1)S(1)}, bf16[64,1024]{1,0:T(8,128)(2,1)S(1)}, u32[]{:S(2)}, u32[]{:S(2)}) collective-permute-start(bf16[64,1024]{1,0:T(8,128)(2,1)S(1)} %get-tuple-element.112), channel_id=1, source_target_pairs={{0,24},{4,28},{8,16},{12,20},{16,8},{20,12},{24,0},{28,4},{1,25},{... | collective-permute-start | bytes 393224 | tf_op jit(solution)/shard_map/ppermute | solution.py:916
  583.2 23.2 %collective-permute-start.33 = (bf16[128,2048]{1,0:T(8,128)(2,1)S(1)}, bf16[128,2048]{1,0:T(8,128)(2,1)S(1)}, u32[]{:S(2)}, u32[]{:S(2)}) collective-permute-start(bf16[128,2048]{1,0:T(8,128)(2,1)S(1)} %get-tuple-element.72), channel_id=1, source_target_pairs={{0,16},{4,20},{8,24},{12,28},{16,0},{20,4},{24,8},{28,12},{1,17},{... | collective-permute-start | bytes 1572872 | tf_op jit(solution)/shard_map/ppermute | solution.py:916
  583.6 22.8 %collective-permute-start.34 = (bf16[128,2048]{1,0:T(8,128)(2,1)S(1)}, bf16[128,2048]{1,0:T(8,128)(2,1)S(1)}, u32[]{:S(2)}, u32[]{:S(2)}) collective-permute-start(bf16[128,2048]{1,0:T(8,128)(2,1)S(1)} %get-tuple-element.71), channel_id=1, source_target_pairs={{0,24},{4,28},{8,16},{12,20},{16,8},{20,12},{24,0},{28,4},{1,25},{... | collective-permute-start | bytes 1572872 | tf_op jit(solution)/shard_map/ppermute | solution.py:916
  607.3 9.9 %collective-permute-start.61 = (f32[2,8,64]{2,1,0:T(8,128)S(1)}, f32[2,8,64]{2,1,0:T(8,128)S(1)}, u32[]{:S(2)}, u32[]{:S(2)}) collective-permute-start(f32[2,8,64]{2,1,0:T(8,128)S(1)} %bitcast.277), channel_id=1, source_target_pairs={{0,1},{1,0},{2,3},{3,2},{4,5},{5,4},{6,7},{7,6},{8,9},{9,8},{10,11... | collective-permute-start | bytes 12296 | tf_op jit(solution)/shard_map/ppermute | solution.py:913
  607.7 9.5 %collective-permute-start.62 = (f32[2,8,64]{2,1,0:T(8,128)S(1)}, f32[2,8,64]{2,1,0:T(8,128)S(1)}, u32[]{:S(2)}, u32[]{:S(2)}) collective-permute-start(f32[2,8,64]{2,1,0:T(8,128)S(1)} %bitcast.276), channel_id=1, source_target_pairs={{0,2},{1,3},{2,0},{3,1},{4,6},{5,7},{6,4},{7,5},{8,10},{9,11},{10,... | collective-permute-start | bytes 12296 | tf_op jit(solution)/shard_map/ppermute | solution.py:913
  609.9 7.4 %collective-permute-start.63 = (f32[2,8,64]{2,1,0:T(8,128)S(1)}, f32[2,8,64]{2,1,0:T(8,128)S(1)}, u32[]{:S(2)}, u32[]{:S(2)}) collective-permute-start(f32[2,8,64]{2,1,0:T(8,128)S(1)} %bitcast.275), channel_id=1, source_target_pairs={{0,3},{1,2},{2,1},{3,0},{4,7},{5,6},{6,5},{7,4},{8,11},{9,10},{10,... | collective-permute-start | bytes 12296 | tf_op jit(solution)/shard_map/ppermute | solution.py:913
  617.1 9.7 %collective-permute-start.48 = (bf16[256,2048]{1,0:T(8,128)(2,1)S(1)}, bf16[256,2048]{1,0:T(8,128)(2,1)S(1)}, u32[]{:S(2)}, u32[]{:S(2)}) collective-permute-start(bf16[256,2048]{1,0:T(8,128)(2,1)S(1)} %dynamic-slice_bitcast_fusion.3), channel_id=1, source_target_pairs={{0,4},{4,0},{8,12},{12,8},{16,20},{20,16},{24,28},{28,24},{1,5},{5... | collective-permute-start | bytes 3145736 | tf_op jit(solution)/shard_map/ppermute | solution.py:919
  619.9 4.7 collective-permute-start.65
  621.9 4.5 collective-permute-start.67
  627.7 22.3 %collective-permute-start.49 = (bf16[64,4096]{1,0:T(8,128)(2,1)S(1)}, bf16[64,4096]{1,0:T(8,128)(2,1)S(1)}, u32[]{:S(2)}, u32[]{:S(2)}) collective-permute-start(bf16[64,4096]{1,0:T(8,128)(2,1)S(1)} %get-tuple-element.65), channel_id=1, source_target_pairs={{0,1},{1,0},{2,3},{3,2},{4,5},{5,4},{6,7},{7,6},{8,9},{9,8},{10,11... | collective-permute-start | bytes 1572872 | tf_op jit(solution)/shard_map/ppermute | solution.py:913
  627.8 38.3 %collective-permute-start.50 = (bf16[64,4096]{1,0:T(8,128)(2,1)S(1)}, bf16[64,4096]{1,0:T(8,128)(2,1)S(1)}, u32[]{:S(2)}, u32[]{:S(2)}) collective-permute-start(bf16[64,4096]{1,0:T(8,128)(2,1)S(1)} %get-tuple-element.64), channel_id=1, source_target_pairs={{0,2},{1,3},{2,0},{3,1},{4,6},{5,7},{6,4},{7,5},{8,10},{9,11},{10,... | collective-permute-start | bytes 1572872 | tf_op jit(solution)/shard_map/ppermute | solution.py:913
  630.6 35.6 %collective-permute-start.51 = (bf16[64,4096]{1,0:T(8,128)(2,1)S(1)}, bf16[64,4096]{1,0:T(8,128)(2,1)S(1)}, u32[]{:S(2)}, u32[]{:S(2)}) collective-permute-start(bf16[64,4096]{1,0:T(8,128)(2,1)S(1)} %get-tuple-element.63), channel_id=1, source_target_pairs={{0,3},{1,2},{2,1},{3,0},{4,7},{5,6},{6,5},{7,4},{8,11},{9,10},{10,... | collective-permute-start | bytes 1572872 | tf_op jit(solution)/shard_map/ppermute | solution.py:913
  (34 other events, 314.6 us)

commit v3 on v2

--- a/solution.py
+++ b/solution.py
@@ -861,6 +861,340 @@
     )(normed_two, mid, upstream, gain, upstream_group, w_gate, w_up, down_rows)
 
 
+def xor4(a, b):
+    return 2 * ((a // 2 + b // 2) % 2) + (a % 2 + b % 2) % 2
+
+
+def rotated(values, cosine, sine):
+    half = values.shape[1] // 2
+    first, second = values[:, :half], values[:, half:]
+    return jnp.concatenate([first * cosine - second * sine, second * cosine + first * sine], axis=1)
+
+
+def front_kernel(
+    input_ref,
+    attn_gain_ref,
+    mlp_gain_ref,
+    cosine_ref,
+    sine_ref,
+    code_ref,
+    low_code_ref,
+    key_code_ref,
+    query_hbm,
+    key_hbm,
+    value_hbm,
+    out_hbm,
+    down_hbm,
+    upstream_hbm,
+    second_ref,
+    mid_ref,
+    normed_ref,
+    query_ref,
+    kv_ref,
+    attended_ref,
+    log_total_ref,
+    w_head,
+    w_sibling,
+    out_pair,
+    down_rows,
+    upstream_all,
+    inputs_all,
+    w_parts,
+    attended_other,
+    own_sum,
+    chip_send,
+    chip_recv,
+    local_sem,
+    send_sem,
+    recv_sem,
+):
+    tok, width = input_ref.shape
+    quarter = width // 4
+    shard = out_hbm.shape[1]
+    hidden = down_rows.shape[0]
+    part = hidden // 4
+    seq = 8 * tok
+    half_seq = 4 * tok
+    ctx, plane = lax.axis_index("ctx"), lax.axis_index("shard")
+    chip, core = ctx // 2, ctx % 2
+    sibling = (ctx + 1 - 2 * core, plane)
+    over_z = [(ctx, flip(plane, d)) for d in range(4)]
+    over_chips = [(2 * flip(chip, d) + core, plane) for d in range(4)]
+    others = (1, 2, 3)
+
+    def at(i, size):
+        return pl.ds(pl.multiple_of(i * size, size), size)
+
+    def remote(slot, source, target, device):
+        return pltpu.make_async_remote_copy(
+            src_ref=source,
+            dst_ref=target,
+            send_sem=send_sem.at[slot],
+            recv_sem=recv_sem.at[slot],
+            device_id=device,
+            device_id_type=MESH,
+        )
+
+    def send(slot, source, target, device):
+        copy = remote(slot, source, target, device)
+        copy.start()
+        return copy
+
+    def local(slot, source, target):
+        return pltpu.make_async_copy(source, target, local_sem.at[slot])
+
+    rows = at(chip, quarter)
+    mine = w_parts.at[plane]
+    load_query = local(0, query_hbm.at[rows, at(core, HD)], mine.at[0])
+    load_key = local(1, key_hbm.at[rows], mine.at[1])
+    load_value = local(1, value_hbm.at[rows], mine.at[1])
+    load_query.start()
+
+    @pl.when(core == 0)
+    def _():
+        load_key.start()
+
+    @pl.when(core == 1)
+    def _():
+        load_value.start()
+
+    keep_input = local(2, input_ref, inputs_all.at[0, 0])
+    keep_input.start()
+    out_own = out_hbm.at[at(ctx, HD), :]
+    keep_out = local(3, out_own, out_pair.at[0, :, at(plane, shard)])
+    keep_out.start()
+
+    def down_block(to_plane):
+        first = to_plane * (2 * hidden) + core * hidden + chip * part
+        return down_hbm.at[pl.ds(pl.multiple_of(first, part), part), :]
+
+    down_place = down_rows.at[at(chip, part), at(plane, shard)]
+    keep_down = local(4, down_block(plane), down_place)
+    keep_down.start()
+    keep_upstream = local(5, upstream_hbm, upstream_all.at[0, 0])
+    keep_upstream.start()
+
+    barrier = pltpu.get_barrier_semaphore()
+    partners = [sibling] + over_z[1:] + over_chips[1:]
+    for partner in partners:
+        pl.semaphore_signal(barrier, inc=1, device_id=partner, device_id_type=MESH)
+    pl.semaphore_wait(barrier, len(partners))
+
+    input_chips = {
+        d: send(d - 1, input_ref, inputs_all.at[0, d], over_chips[d]) for d in others
+    }
+    input_pairs = {0: send(3, input_ref, inputs_all.at[1, 0], sibling)}
+    load_query.wait()
+    load_key.wait()
+    head_z = {d: send(6 + d, mine, w_parts.at[plane], over_z[d]) for d in others}
+
+    chunk = 32
+    attn_gain = attn_gain_ref[...]
+
+    def norm(e, d):
+        def step(i, carry):
+            block = inputs_all[e, d, at(i, chunk), :].astype(F32)
+            factor = lax.rsqrt(jnp.mean(block * block, axis=-1, keepdims=True) + EPSILON)
+            first = (4 * e + d) * tok + i * chunk
+            normed_ref[pl.ds(pl.multiple_of(first, chunk), chunk), :] = (
+                block * factor * attn_gain
+            ).astype(BF16)
+            return carry
+
+        lax.fori_loop(0, tok // chunk, step, 0)
+
+    keep_input.wait()
+    norm(0, 0)
+    for d in others:
+        input_chips[d].wait_recv()
+        input_pairs[d] = send(3 + d, inputs_all.at[0, d], inputs_all.at[1, d], sibling)
+        norm(0, d)
+    for d in range(4):
+        input_pairs[d].wait_recv()
+        norm(1, d)
+
+    head_rows = w_head.at[:, rows, :]
+    for d in range(4):
+        if d:
+            head_z[d].wait_recv()
+        source = flip(plane, d)
+        apart = xor4(chip, source)
+        block = w_parts.at[source]
+
+        @pl.when(apart == 0)
+        def _(block=block):
+            local(6, block, head_rows).start()
+
+        @pl.when(apart != 0)
+        def _(block=block, source=source, apart=apart):
+            remote(9 + apart, block, head_rows, (2 * source + core, plane)).start()
+
+    out_z = {
+        d: send(12 + d, out_own, out_pair.at[0, :, at(plane, shard)], over_z[d]) for d in others
+    }
+    local(6, mine, head_rows).wait()
+    for d in others:
+        remote(9 + d, mine, head_rows, over_chips[d]).wait_recv()
+    head_pair = send(16, w_head, w_sibling, sibling)
+    down_z = {d: send(16 + d, down_block(flip(plane, d)), down_place, over_z[d]) for d in others}
+
+    def project(which, target, flat):
+        def step(t, carry):
+            here = at(t, TILE)
+            made = dot_nn(normed_ref[here, :], w_head[which])
+            cosine, sine = cosine_ref[here, :], sine_ref[here, :]
+            if flat:
+                cosine = jnp.where(core == 0, cosine, 1.0)
+                sine = jnp.where(core == 0, sine, 0.0)
+            target[here, :] = rotated(made, cosine, sine).astype(BF16)
+            return carry
+
+        lax.fori_loop(0, seq // TILE, step, 0)
+
+    mine_kv = kv_ref.at[core]
+    project(1, mine_kv, True)
+    kv_pair = [
+        send(20 + e, mine_kv.at[pl.ds(e * half_seq, half_seq)],
+             mine_kv.at[pl.ds((1 - e) * half_seq, half_seq)], sibling)
+        for e in range(2)
+    ]
+    project(0, query_ref, False)
+    for copy in kv_pair:
+        copy.wait_recv()
+
+    def attend_step(t, carry):
+        here = at(t, TILE)
+        scores = scores_of(
+            query_ref[here, :], kv_ref[0], code_ref[here, :], low_code_ref[here, :], key_code_ref[...]
+        )
+        top = jnp.max(scores, axis=-1, keepdims=True)
+        weights = jnp.exp(scores - top)
+        total = jnp.sum(weights, axis=-1, keepdims=True)
+        mixed = dot_nn(weights.astype(BF16), kv_ref[1])
+        attended_ref[here, :] = (mixed / total).astype(BF16)
+        log_total_ref[here, :] = top + jnp.log(total)
+        return carry
+
+    lax.fori_loop(0, seq // TILE, attend_step, 0)
+    attended_pair = send(22, attended_ref.at[pl.ds(half_seq, half_seq)], attended_other, sibling)
+    keep_out.wait()
+    for d in others:
+        out_z[d].wait_recv()
+    out_sibling = send(23, out_pair.at[0], out_pair.at[1], sibling)
+    attended_pair.wait_recv()
+    out_sibling.wait_recv()
+
+    def out_step(t, carry):
+        here = at(t, TILE)
+        terms = dot_nn(attended_ref[:half_seq, :], out_pair[0, :, here]) + dot_nn(
+            attended_other[...], out_pair[1, :, here]
+        )
+        own_sum[:, here] = terms[:tok]
+        for d in others:
+            chip_send[d - 1, :, here] = terms[d * tok : (d + 1) * tok].astype(BF16)
+        return carry
+
+    lax.fori_loop(0, width // TILE, out_step, 0)
+    branch = {
+        d: send(23 + d, chip_send.at[d - 1], chip_recv.at[d - 1], over_chips[d]) for d in others
+    }
+
+    keep_down.wait()
+    for d in others:
+        down_z[d].wait_recv()
+    upstream_z = {
+        d: send(29 + d, upstream_hbm, upstream_all.at[d, 0], over_z[d]) for d in others
+    }
+    upstream_pair = {0: send(33, upstream_hbm, upstream_all.at[0, 1], sibling)}
+
+    for d in others:
+        branch[d].wait_recv()
+    down_mine = down_rows.at[at(chip, part), :]
+    down_chips = {d: send(26 + d, down_mine, down_mine, over_chips[d]) for d in others}
+    mlp_gain = mlp_gain_ref[...]
+
+    def mid_step(i, carry):
+        here = at(i, chunk)
+        mid = input_ref[here, :].astype(F32) + own_sum[here, :]
+        for d in range(3):
+            mid = mid + chip_recv[d, here, :].astype(F32)
+        factor = lax.rsqrt(jnp.mean(mid * mid, axis=-1, keepdims=True) + EPSILON)
+        mid_ref[here, :] = mid
+        second_ref[here, :] = (mid * factor * mlp_gain).astype(BF16)
+        return carry
+
+    lax.fori_loop(0, tok // chunk, mid_step, 0)
+
+    for d in others:
+        upstream_z[d].wait_recv()
+        upstream_pair[d] = send(33 + d, upstream_all.at[d, 0], upstream_all.at[d, 1], sibling)
+    keep_upstream.wait()
+    for d in range(4):
+        upstream_pair[d].wait_recv()
+        upstream_pair[d].wait_send()
+        input_pairs[d].wait_send()
+    head_pair.wait_recv()
+    for copy in (head_pair, attended_pair, out_sibling, *kv_pair):
+        copy.wait_send()
+    for d in others:
+        down_chips[d].wait_recv()
+        for copies in (input_chips, head_z, out_z, down_z, branch, down_chips, upstream_z):
+            copies[d].wait_send()
+        remote(9 + d, mine, head_rows, over_chips[d]).wait_send()
+
+
+def front_of(
+    inputs, attn_gain, mlp_gain, cosine, sine, code, low_code, key_code,
+    w_query, w_key, w_value, w_out, w_down, upstream,
+):
+    tok, width = inputs.shape
+    seq = 8 * tok
+    hidden = w_down.shape[0] // 8
+    vmem = pl.BlockSpec(memory_space=pltpu.VMEM)
+    hbm = pl.BlockSpec(memory_space=pl.ANY)
+    return pl.pallas_call(
+        front_kernel,
+        in_specs=[vmem] * 8 + [hbm] * 6,
+        out_specs=[vmem] * 8 + [hbm] + [vmem] + [hbm] * 2,
+        out_shape=[
+            jax.ShapeDtypeStruct((tok, width), BF16),
+            jax.ShapeDtypeStruct((tok, width), F32),
+            jax.ShapeDtypeStruct((seq, width), BF16),
+            jax.ShapeDtypeStruct((seq, HD), BF16),
+            jax.ShapeDtypeStruct((2, seq, HD), BF16),
+            jax.ShapeDtypeStruct((seq, HD), BF16),
+            jax.ShapeDtypeStruct((seq, 1), F32),
+            jax.ShapeDtypeStruct((2, width, HD), BF16),
+            jax.ShapeDtypeStruct((2, width, HD), BF16),
+            jax.ShapeDtypeStruct((2, HD, width), BF16),
+            jax.ShapeDtypeStruct((hidden, width), BF16),
+            jax.ShapeDtypeStruct((4, 2, tok, width), BF16),
+        ],
+        scratch_shapes=[
+            pltpu.VMEM((2, 4, tok, width), BF16),
+            pltpu.VMEM((4, 2, width // 4, HD), BF16),
+            pltpu.VMEM((4 * tok, HD), BF16),
+            pltpu.VMEM((tok, width), F32),
+            pltpu.VMEM((3, tok, width), BF16),
+            pltpu.VMEM((3, tok, width), BF16),
+            pltpu.SemaphoreType.DMA((7,)),
+            pltpu.SemaphoreType.DMA((37,)),
+            pltpu.SemaphoreType.DMA((37,)),
+        ],
+        compiler_params=pltpu.CompilerParams(
+            collective_id=2, has_side_effects=True, vmem_limit_bytes=56 << 20
+        ),
+        cost_estimate=pl.CostEstimate(
+            flops=2 * seq * width * 3 * HD + 4 * seq * seq * HD,
+            bytes_accessed=20 * seq * width,
+            transcendentals=seq * seq,
+        ),
+    )(
+        inputs, attn_gain, mlp_gain, cosine, sine, code, low_code, key_code,
+        w_query, w_key, w_value, w_out, w_down, upstream,
+    )
+
+
 def rotate_head(values, cosine, sine):
     half = values.shape[-1] // 2
     first, second = values[:, :half], values[:, half:]
@@ -948,28 +1282,8 @@
         return total
 
     quarter = width // chips
-    head_block = jnp.concatenate(
-        [
-            cut(w_query, (quarter * chip, HD * core), (quarter, HD)),
-            jnp.where(
-                first_core,
-                cut(w_key, (quarter * chip, 0), (quarter, HD)),
-                cut(w_value, (quarter * chip, 0), (quarter, HD)),
-            ),
-        ],
-        axis=1,
-    )
-    head_parts = jnp.stack(gather_z(head_block))
-    w_head = jnp.zeros((width, 2 * HD), BF16)
-    for d in range(chips):
-        part = index_of(head_parts, plane ^ chip ^ d)
-        if d:
-            part = over_chips(part, d)
-        w_head = lax.dynamic_update_slice(w_head, part, (quarter * (chip ^ d), 0))
-
     inputs_low = layer_input[0]
     inputs = inputs_low.astype(F32)
-    all_inputs = gather_seq(inputs_low).astype(F32)
     pairs, documents = block_pairs[0], doc_ids[0]
     order = jnp.stack([(chip ^ d) * 2 + (core ^ e) for e in range(2) for d in range(chips)])
     rows = (order[:, None] * tok_rows + jnp.arange(tok_rows, dtype=jnp.int32)[None, :]).reshape(-1)
@@ -981,42 +1295,42 @@
     code_column, low_column, code_row = code[:, None], low_code[:, None], code[None, :]
     cosine, sine = rope_tables(positions, HD)
 
-    factor_all = lax.rsqrt(jnp.mean(all_inputs * all_inputs, axis=-1, keepdims=True) + EPSILON)
-    normed_all = (all_inputs * factor_all * attn_gain).astype(BF16)
-    projected = dot_nn(normed_all, w_head)
-    query = rotate_head(projected[:, :HD], cosine, sine).astype(BF16)
+    upstream_low = cotangent[0]
+    (
+        normed_two,
+        mid,
+        normed_all,
+        query,
+        key_value,
+        attended,
+        log_total,
+        w_head,
+        w_sibling,
+        out_pair,
+        down_rows,
+        upstream_group,
+    ) = front_of(
+        inputs_low,
+        attn_gain[None],
+        mlp_gain[None],
+        cosine,
+        sine,
+        code_column,
+        low_column,
+        code_row,
+        w_query,
+        w_key,
+        w_value,
+        w_out,
+        w_down,
+        upstream_low,
+    )
+    key, value = key_value[0], key_value[1]
+    out_rows = out_pair[0]
+    upstream_group = upstream_group.reshape(-1, width)
     key_cosine = jnp.where(first_core, cosine, 1.0)
     key_sine = jnp.where(first_core, sine, 0.0)
-    mine_kv = rotate_head(projected[:, HD:], key_cosine, key_sine).astype(BF16)
-    other_kv = swap_halves(sibling(mine_kv))
-    key = jnp.where(first_core, mine_kv, other_kv)
-    value = jnp.where(first_core, other_kv, mine_kv)
-    attended, log_total = attend(query, key, value, code_column, low_column, code_row)
-
-    out_rows = jnp.zeros((HD, width), BF16)
-    for d, part in enumerate(gather_z(cut(w_out, (HD * ctx, 0), (HD, shard_width)))):
-        out_rows = lax.dynamic_update_slice(out_rows, part, (0, shard_width * (plane ^ d)))
-    out_pair = jnp.concatenate([out_rows, sibling(out_rows)], axis=0)
-    attended_pair = jnp.concatenate([attended[:half_seq], sibling(attended[half_seq:])], axis=1)
-    branch_parts = dot_nn(attended_pair, out_pair).reshape(chips, tok_rows, width)
-    mid = inputs + sum_chips(lambda d: branch_parts[d])
-    factor_two = lax.rsqrt(jnp.mean(mid * mid, axis=-1, keepdims=True) + EPSILON)
-    normed_two = (mid * factor_two * mlp_gain).astype(BF16)
-
-    quarter_hidden = hidden // chips
-    down_block = jnp.zeros((quarter_hidden, width), BF16)
-    for d in range(planes):
-        start = hidden_plane * (plane ^ d) + hidden * core + quarter_hidden * chip
-        part = cut(w_down, (start, 0), (quarter_hidden, shard_width))
-        if d:
-            part = over_z(part, d)
-        down_block = lax.dynamic_update_slice(down_block, part, (0, shard_width * (plane ^ d)))
-    down_rows = jnp.zeros((hidden, width), BF16)
-    for d, part in enumerate(gather_chips(down_block)):
-        down_rows = lax.dynamic_update_slice(down_rows, part, (quarter_hidden * (chip ^ d), 0))
-
-    upstream_low = cotangent[0]
-    upstream_group = gather_group(upstream_low)
+    factor_one = lax.rsqrt(jnp.mean(inputs * inputs, axis=-1, keepdims=True) + EPSILON)
     output, mid_grad, mlp_gain_term, branch_grad_all, gate_up_terms, down_terms = mlp_of(
         normed_two, mid, upstream_low, mlp_gain[None], upstream_group, w_gate, w_up, down_rows
     )
@@ -1035,10 +1349,9 @@
         [rotate_head(d_query, cosine, -sine), rotate_head(d_kv, key_cosine, -key_sine)], axis=1
     ).astype(BF16)
     d_head_pair = jnp.concatenate([d_head[:half_seq], sibling(d_head[half_seq:])], axis=1)
-    w_head_pair = jnp.concatenate([w_head, sibling(w_head)], axis=1)
+    w_head_pair = jnp.concatenate([w_head[0], w_head[1], w_sibling[0], w_sibling[1]], axis=1)
     normed_parts = dot_nt(d_head_pair, w_head_pair).reshape(chips, tok_rows, width)
     normed_grad = sum_chips(lambda d: normed_parts[d])
-    factor_one = factor_all[:tok_rows]
     attn_gain_term = jnp.sum(normed_grad * inputs * factor_one, axis=0)
     scaled_one = normed_grad * attn_gain
     grad_input = (

time: 679 us -> 628 us (0.925)
  Pallas kernels: 152 us -> 324 us
  waiting for transfers between devices: 284 us -> 137 us
  starting transfers between devices: 127 us -> 83.5 us
  local copies, waits for them, and re-layouts: 49.9 us -> 30.8 us
  matrix products: 17.4 us -> 9.51 us
    pallas_call x1, Pallas kernels: 4.58 us -> 162 us  [front_of(): pl.pallas_call(front_kernel, in_specs=[vmem] * 8 + [hbm] * 6, out_specs=[...]
    ppermute x27 -> x15, waiting for transfers between devices: 158 us -> 79.2 us  [over_z(): return lax.ppermute(values, 'shard', [(i, i ^ d) for i in range(planes)])]
    ppermute x30 -> x18, waiting for transfers between devices: 121 us -> 55.9 us  [over_chips(): lax.ppermute(values, 'ctx', [(i, i ^ 2 * d) for i in range(ctx_count)])]
    ppermute x27 -> x15, starting transfers between devices: 85.9 us -> 55.7 us  [over_z(): return lax.ppermute(values, 'shard', [(i, i ^ d) for i in range(planes)])]
    pallas_call x1, Pallas kernels: 142 us -> 157 us  [mlp_of(): pl.pallas_call(mlp_kernel, in_specs=[vmem] * 4 + [hbm] * 4, out_specs=[vm...]
    ppermute x30 -> x18, starting transfers between devices: 38.9 us -> 27 us  [over_chips(): lax.ppermute(values, 'ctx', [(i, i ^ 2 * d) for i in range(ctx_count)])]
    dynamic_update_slice x15 -> x0, local copies, waits for them, and re-layouts: 9.93 us -> none  [the longest x4 5 us: on_device_by_head(): lax.dynamic_update_slice(out_rows, part, (0, shard_width * (plane ^ d)))]
    dot_general x2 -> x0, matrix products: 7.64 us -> none  [dot_nn(): return jnp.dot(a, b, preferred_element_type=F32)]
  transfers between devices with their start and end apart: 68 -> 38, of which waited for: 26 -> 15; matrix products, arithmetic and copies ran while one was open for 13% -> 6% of each run, Pallas kernels for 1% -> 1%
where the time goes in v3:
time: 628 us; the launch traced here: 618 us
  Pallas kernels  324 us (52%)
  waiting for transfers between devices  137 us (22%)
  starting transfers between devices  83.5 us (13%)
  other arithmetic  31 us (5%)
  local copies, waits for them, and re-layouts  30.8 us (5%)
  matrix products  9.51 us (2%)
    pallas_call x1, Pallas kernels, front_of(): pl.pallas_call(front_kernel, in_specs=[vmem] * 8 + [hbm] * 6, out_specs=[...  162 us
    pallas_call x1, Pallas kernels, mlp_of(): pl.pallas_call(mlp_kernel, in_specs=[vmem] * 4 + [hbm] * 4, out_specs=[vm...  157 us
    ppermute x15, waiting for transfers between devices, over_z(): return lax.ppermute(values, 'shard', [(i, i ^ d) for i in range(planes)])  79.2 us
    ppermute x18, waiting for transfers between devices, over_chips(): lax.ppermute(values, 'ctx', [(i, i ^ 2 * d) for i in range(ctx_count)])  55.9 us
    ppermute x15, starting transfers between devices, over_z(): return lax.ppermute(values, 'shard', [(i, i ^ d) for i in range(planes)])  55.7 us
    ppermute x18, starting transfers between devices, over_chips(): lax.ppermute(values, 'ctx', [(i, i ^ 2 * d) for i in range(ctx_count)])  27 us
  transfers between devices with their start and end apart: 38, of which 15 were waited for; matrix products, arithmetic and copies ran while one was open for 6% of the time, Pallas kernels for 1%

profile of v3, /device:TPU:0, one launch (start us, length us, event | category | flops | bytes accessed | tf_op | source)
XLA Modules:
  0.0 618.1 jit_solution(4206270093364049127)
XLA Ops:
  1.1 1.6 fusion.72
  3.2 5.2 select_reduce_fusion
  9.3 0.9 fusion.51
  10.2 4.5 gather_fusion
  15.0 1.2 add_maximum_fusion
  16.1 3.0 multiply_sine_fusion
  19.8 161.7 %shard_map.212 = (bf16[128,2048]{1,0:T(8,128)(2,1)}, f32[128,2048]{1,0:T(8,128)}, bf16[1024,2048]{1,0:T(8,128)(2,1)}, bf16[1024,256]{1,0:T(8,128)(2,1)}, bf16[2,...) custom-call(bf16[128,2048]{1,0:T(8,128)(2,1)} %bitcast.224, ...), custom_call_target="tpu_custom_call" | custom-call | flops 4294967296 | bytes 41943040 | tf_op jit(solution)/shard_map/pallas_call | solution.py:1155
  181.5 157.0 %shard_map.213 = (bf16[128,2048]{1,0:T(8,128)(2,1)}, f32[128,2048]{1,0:T(8,128)}, f32[1,2048]{1,0:T(1,128)}, bf16[2,4,128,2048]{3,2,1,0:T(8,128)(2,1)}, bf16[4,5...) custom-call(bf16[128,2048]{1,0:T(8,128)(2,1)} %get-tuple-element.32.second_ref, f32[128,2048]{1,0:T(8,128)} %get-tuple-element.33.mid_ref, ...), custom_call_target="tpu_custom_call" | custom-call | flops 38654705664 | bytes 37748736 | tf_op jit(solution)/shard_map/pallas_call | solution.py:819
  338.6 3.8 dynamic-slice_bitcast_fusion.2
  343.0 1.9 collective-permute-start.23
  344.9 1.5 collective-permute-start.24
  346.6 3.5 fusion.74
  350.1 1.3 copy-done.9
  351.4 0.9 fusion.54
  352.3 18.3 %collective-permute-start.12 = (bf16[64,2048]{1,0:T(8,128)(2,1)}, bf16[64,2048]{1,0:T(8,128)(2,1)}, u32[]{:S(2)}, u32[]{:S(2)}) collective-permute-start(bf16[64,2048]{1,0:T(8,128)(2,1)} %get-tuple-element.75), channel_id=1, source_target_pairs={{0,1},{1,0},{2,3},{3,2},{4,5},{5,4},{6,7},{7,6},{8,9},{9,8},{10,11... | collective-permute-start | bytes 786440 | tf_op jit(solution)/shard_map/ppermute | solution.py:1247
  370.7 6.0 slice_bitcast_fusion.2
  376.7 1.3 convolution_convert_fusion.outgrad
  378.9 2.1 slice_bitcast_fusion.4
  381.7 5.4 shard_map.214
  387.2 1.1 broadcast_select_fusion
  388.3 2.4 collective-permute-start.14
  392.4 5.4 collective-permute-done.14
  397.7 1.3 collective-permute-start.15
  399.0 2.2 fusion.49
  401.2 1.8 collective-permute-start.16
  403.0 2.9 fusion.13
  406.0 7.8 %collective-permute-start.25 = (bf16[64,2048]{1,0:T(8,128)(2,1)S(1)}, bf16[64,2048]{1,0:T(8,128)(2,1)S(1)}, u32[]{:S(2)}, u32[]{:S(2)}) collective-permute-start(bf16[64,2048]{1,0:T(8,128)(2,1)S(1)} %get-tuple-element.95), channel_id=1, source_target_pairs={{0,1},{1,0},{2,3},{3,2},{4,5},{5,4},{6,7},{7,6},{8,9},{9,8},{10,11... | collective-permute-start | bytes 786440 | tf_op jit(solution)/shard_map/ppermute | solution.py:1247
  414.2 2.0 collective-permute-start.27
  416.5 2.7 fusion.41
  419.4 2.4 fusion.63
  422.6 12.5 %collective-permute-done.26 = bf16[64,2048]{1,0:T(8,128)(2,1)S(1)} collective-permute-done((bf16[64,2048]{1,0:T(8,128)(2,1)S(1)}, bf16[64,2048]{1,0:T(8,128)(2,1)S(1)}, u32[]{:S(2)}, u32[]{:S(2)}) %collective-permute-start.26) | collective-permute-done | bytes 262176 | tf_op jit(solution)/shard_map/ppermute | solution.py:1247
  435.1 5.6 collective-permute-start.6
  443.0 2.4 fusion.73
  445.5 3.9 collective-permute-done.5
  449.5 2.1 collective-permute-start.17
  451.6 22.6 %collective-permute-done.6 = bf16[8,64,512]{2,1,0:T(8,128)(2,1)S(1)} collective-permute-done((bf16[8,64,512]{2,1,0:T(8,128)(2,1)S(1)}, bf16[8,64,512]{2,1,0:T(8,128)(2,1)S(1)}, u32[]{:S(2)}, u32[]{:S(2)}) %collective-permute-start.6) | collective-permute-done | bytes 524320 | tf_op jit(solution)/shard_map/ppermute | solution.py:1247
  474.2 1.3 collective-permute-start.28
  476.6 22.1 %collective-permute-done.28 = bf16[64,2048]{1,0:T(8,128)(2,1)S(1)} collective-permute-done((bf16[64,2048]{1,0:T(8,128)(2,1)S(1)}, bf16[64,2048]{1,0:T(8,128)(2,1)S(1)}, u32[]{:S(2)}, u32[]{:S(2)}) %collective-permute-start.28) | collective-permute-done | bytes 262176 | tf_op jit(solution)/shard_map/ppermute | solution.py:1250
  498.6 2.1 collective-permute-start.30
  500.9 5.0 collective-permute-done.30
  506.2 1.1 copy-done.12
  508.0 2.9 collective-permute-start.10
  511.0 2.6 collective-permute-done.9
  514.3 2.6 collective-permute-start.11
  517.0 10.5 %collective-permute-done.11 = bf16[64,1024]{1,0:T(8,128)(2,1)S(1)} collective-permute-done((bf16[64,1024]{1,0:T(8,128)(2,1)S(1)}, bf16[64,1024]{1,0:T(8,128)(2,1)S(1)}, u32[]{:S(2)}, u32[]{:S(2)}) %collective-permute-start.11) | collective-permute-done | bytes 131104 | tf_op jit(solution)/shard_map/ppermute | solution.py:1250
  527.4 1.4 collective-permute-start.3
  528.9 1.9 collective-permute-start.4
  530.9 14.0 %collective-permute-done.3 = bf16[128,2048]{1,0:T(8,128)(2,1)S(1)} collective-permute-done((bf16[128,2048]{1,0:T(8,128)(2,1)S(1)}, bf16[128,2048]{1,0:T(8,128)(2,1)S(1)}, u32[]{:S(2)}, u32[]{:S(2)}) %collective-permute-start.3) | collective-permute-done | bytes 524320 | tf_op jit(solution)/shard_map/ppermute | solution.py:1250
  545.8 10.9 %collective-permute-start.31 = (f32[2,8,64]{2,1,0:T(8,128)S(1)}, f32[2,8,64]{2,1,0:T(8,128)S(1)}, u32[]{:S(2)}, u32[]{:S(2)}) collective-permute-start(f32[2,8,64]{2,1,0:T(8,128)S(1)} %bitcast.256), channel_id=1, source_target_pairs={{0,1},{1,0},{2,3},{3,2},{4,5},{5,4},{6,7},{7,6},{8,9},{9,8},{10,11... | collective-permute-start | bytes 12296 | tf_op jit(solution)/shard_map/ppermute | solution.py:1247
  556.7 1.9 collective-permute-start.32
  558.7 1.4 collective-permute-start.33
  560.0 5.2 fusion.10
  566.1 2.0 collective-permute-done.34
  568.2 1.4 collective-permute-start.35
  570.3 1.5 collective-permute-start.37
  571.7 1.1 fusion.47
  573.1 1.6 collective-permute-done.37
  576.0 1.1 collective-permute-start.19
  577.1 1.3 collective-permute-start.20
  578.8 2.1 collective-permute-start.21
  580.9 17.0 %collective-permute-done.19 = bf16[64,4096]{1,0:T(8,128)(2,1)S(1)} collective-permute-done((bf16[64,4096]{1,0:T(8,128)(2,1)S(1)}, bf16[64,4096]{1,0:T(8,128)(2,1)S(1)}, u32[]{:S(2)}, u32[]{:S(2)}) %collective-permute-start.19) | collective-permute-done | bytes 524320 | tf_op jit(solution)/shard_map/ppermute | solution.py:1247
  598.1 17.3 %collective-permute-done.20 = bf16[64,4096]{1,0:T(8,128)(2,1)S(1)} collective-permute-done((bf16[64,4096]{1,0:T(8,128)(2,1)S(1)}, bf16[64,4096]{1,0:T(8,128)(2,1)S(1)}, u32[]{:S(2)}, u32[]{:S(2)}) %collective-permute-start.20) | collective-permute-done | bytes 524320 | tf_op jit(solution)/shard_map/ppermute | solution.py:1247
  615.8 0.8 copy-done.23
  616.6 1.3 copy.85
  (178 shorter events, 18.8 us)
Async XLA Ops:
  0.6 9.6 %copy-start = (s32[1,1024]{1,0:T(1,128)S(1)}, s32[1,1024]{1,0:T(1,128)}, u32[]{:S(2)}) copy-start(s32[1,1024]{1,0:T(1,128)} %param.24) | copy-start | bytes 12292
  338.6 7.8 %copy-start.24 = (bf16[1024,256]{1,0:T(8,128)(2,1)S(1)}, bf16[1024,256]{1,0:T(8,128)(2,1)}, u32[]{:S(2)}) copy-start(bf16[1024,256]{1,0:T(8,128)(2,1)} %get-tuple-element.49) | copy-start | bytes 1572868
  342.4 58.8 %collective-permute-start.22 = (bf16[4,64,2048]{2,1,0:T(8,128)(2,1)}, bf16[4,64,2048]{2,1,0:T(8,128)(2,1)}, u32[]{:S(2)}, u32[]{:S(2)}) collective-permute-start(bf16[4,64,2048]{2,1,0:T(8,128)(2,1)} %get-tuple-element.63), channel_id=1, source_target_pairs={{0,8},{4,12},{8,0},{12,4},{16,24},{20,28},{24,16},{28,20},{1,9},{5... | collective-permute-start | bytes 3145736 | tf_op jit(solution)/shard_map/ppermute | solution.py:1250
  343.0 60.0 %collective-permute-start.23 = (bf16[4,64,2048]{2,1,0:T(8,128)(2,1)}, bf16[4,64,2048]{2,1,0:T(8,128)(2,1)}, u32[]{:S(2)}, u32[]{:S(2)}) collective-permute-start(bf16[4,64,2048]{2,1,0:T(8,128)(2,1)} %get-tuple-element.65), channel_id=1, source_target_pairs={{0,16},{4,20},{8,24},{12,28},{16,0},{20,4},{24,8},{28,12},{1,17},{... | collective-permute-start | bytes 3145736 | tf_op jit(solution)/shard_map/ppermute | solution.py:1250
  344.9 58.1 %collective-permute-start.24 = (bf16[4,64,2048]{2,1,0:T(8,128)(2,1)}, bf16[4,64,2048]{2,1,0:T(8,128)(2,1)}, u32[]{:S(2)}, u32[]{:S(2)}) collective-permute-start(bf16[4,64,2048]{2,1,0:T(8,128)(2,1)} %get-tuple-element.64), channel_id=1, source_target_pairs={{0,24},{4,28},{8,16},{12,20},{16,8},{20,12},{24,0},{28,4},{1,25},{... | collective-permute-start | bytes 3145736 | tf_op jit(solution)/shard_map/ppermute | solution.py:1250
  351.4 19.2 %copy-start.17 = (bf16[2,1024,256]{2,1,0:T(8,128)(2,1)S(1)}, bf16[2,1024,256]{2,1,0:T(8,128)(2,1)}, u32[]{:S(2)}) copy-start(bf16[2,1024,256]{2,1,0:T(8,128)(2,1)} %get-tuple-element.41) | copy-start | bytes 3145732
  352.3 36.0 %collective-permute-start.12 = (bf16[64,2048]{1,0:T(8,128)(2,1)}, bf16[64,2048]{1,0:T(8,128)(2,1)}, u32[]{:S(2)}, u32[]{:S(2)}) collective-permute-start(bf16[64,2048]{1,0:T(8,128)(2,1)} %get-tuple-element.75), channel_id=1, source_target_pairs={{0,1},{1,0},{2,3},{3,2},{4,5},{5,4},{6,7},{7,6},{8,9},{9,8},{10,11... | collective-permute-start | bytes 786440 | tf_op jit(solution)/shard_map/ppermute | solution.py:1247
  370.6 21.7 %collective-permute-start.13 = (bf16[64,2048]{1,0:T(8,128)(2,1)}, bf16[64,2048]{1,0:T(8,128)(2,1)}, u32[]{:S(2)}, u32[]{:S(2)}) collective-permute-start(bf16[64,2048]{1,0:T(8,128)(2,1)} %get-tuple-element.77), channel_id=1, source_target_pairs={{0,2},{1,3},{2,0},{3,1},{4,6},{5,7},{6,4},{7,5},{8,10},{9,11},{10,... | collective-permute-start | bytes 786440 | tf_op jit(solution)/shard_map/ppermute | solution.py:1247
  370.7 6.0 copy-start.10
  370.7 6.0 copy-start.30
  376.7 1.6 copy-start.14
  376.7 2.2 copy-start.15
  378.9 2.1 copy-start.2
  378.9 2.1 copy-start.3
  378.9 2.1 copy-start.4
  378.9 2.3 copy-start.5
  378.9 2.8 copy-start.6
  387.2 3.5 copy-start.7
  387.2 4.3 copy-start.28
  388.3 9.5 %collective-permute-start.14 = (bf16[64,2048]{1,0:T(8,128)(2,1)S(1)}, bf16[64,2048]{1,0:T(8,128)(2,1)}, u32[]{:S(2)}, u32[]{:S(2)}) collective-permute-start(bf16[64,2048]{1,0:T(8,128)(2,1)S(1)} %get-tuple-element.76), channel_id=1, source_target_pairs={{0,3},{1,2},{2,1},{3,0},{4,7},{5,6},{6,5},{7,4},{8,11},{9,10},{10,... | collective-permute-start | bytes 786440 | tf_op jit(solution)/shard_map/ppermute | solution.py:1247
  392.3 21.9 %collective-permute-start = (f32[1024,256]{1,0:T(8,128)}, f32[1024,256]{1,0:T(8,128)S(1)}, u32[]{:S(2)}, u32[]{:S(2)}) collective-permute-start(f32[1024,256]{1,0:T(8,128)} %broadcast_select_fusion), channel_id=1, source_target_pairs={{0,4},{4,0},{8,12},{12,8},{16,20},{20,16},{24,28},{28,24},{1,5},{5... | collective-permute-start | bytes 3145736 | tf_op jit(solution)/shard_map/ppermute | solution.py:1253
  397.7 160.9 %collective-permute-start.15 = (bf16[512,2048]{1,0:T(8,128)(2,1)}, bf16[512,2048]{1,0:T(8,128)(2,1)}, u32[]{:S(2)}, u32[]{:S(2)}) collective-permute-start(bf16[512,2048]{1,0:T(8,128)(2,1)} %get-tuple-element.60), channel_id=1, source_target_pairs={{0,8},{4,12},{8,0},{12,4},{16,24},{20,28},{24,16},{28,20},{1,9},{5... | collective-permute-start | bytes 6291464 | tf_op jit(solution)/shard_map/ppermute | solution.py:1250
  401.2 158.8 %collective-permute-start.16 = (bf16[512,2048]{1,0:T(8,128)(2,1)}, bf16[512,2048]{1,0:T(8,128)(2,1)}, u32[]{:S(2)}, u32[]{:S(2)}) collective-permute-start(bf16[512,2048]{1,0:T(8,128)(2,1)} %get-tuple-element.62), channel_id=1, source_target_pairs={{0,16},{4,20},{8,24},{12,28},{16,0},{20,4},{24,8},{28,12},{1,17},{... | collective-permute-start | bytes 6291464 | tf_op jit(solution)/shard_map/ppermute | solution.py:1250
  406.0 16.6 %collective-permute-start.25 = (bf16[64,2048]{1,0:T(8,128)(2,1)S(1)}, bf16[64,2048]{1,0:T(8,128)(2,1)S(1)}, u32[]{:S(2)}, u32[]{:S(2)}) collective-permute-start(bf16[64,2048]{1,0:T(8,128)(2,1)S(1)} %get-tuple-element.95), channel_id=1, source_target_pairs={{0,1},{1,0},{2,3},{3,2},{4,5},{5,4},{6,7},{7,6},{8,9},{9,8},{10,11... | collective-permute-start | bytes 786440 | tf_op jit(solution)/shard_map/ppermute | solution.py:1247
  413.7 21.4 %collective-permute-start.26 = (bf16[64,2048]{1,0:T(8,128)(2,1)S(1)}, bf16[64,2048]{1,0:T(8,128)(2,1)S(1)}, u32[]{:S(2)}, u32[]{:S(2)}) collective-permute-start(bf16[64,2048]{1,0:T(8,128)(2,1)S(1)} %get-tuple-element.94), channel_id=1, source_target_pairs={{0,2},{1,3},{2,0},{3,1},{4,6},{5,7},{6,4},{7,5},{8,10},{9,11},{10,... | collective-permute-start | bytes 786440 | tf_op jit(solution)/shard_map/ppermute | solution.py:1247
  414.2 20.9 %collective-permute-start.27 = (bf16[64,2048]{1,0:T(8,128)(2,1)S(1)}, bf16[64,2048]{1,0:T(8,128)(2,1)S(1)}, u32[]{:S(2)}, u32[]{:S(2)}) collective-permute-start(bf16[64,2048]{1,0:T(8,128)(2,1)S(1)} %get-tuple-element.93), channel_id=1, source_target_pairs={{0,3},{1,2},{2,1},{3,0},{4,7},{5,6},{6,5},{7,4},{8,11},{9,10},{10,... | collective-permute-start | bytes 786440 | tf_op jit(solution)/shard_map/ppermute | solution.py:1247
  416.5 2.9 copy-start.29
  422.6 18.6 %collective-permute-start.1 = (bf16[512,512]{1,0:T(8,128)(2,1)S(1)}, bf16[512,512]{1,0:T(8,128)(2,1)S(1)}, u32[]{:S(2)}, u32[]{:S(2)}) collective-permute-start(bf16[512,512]{1,0:T(8,128)(2,1)S(1)} %get-tuple-element.107), channel_id=1, source_target_pairs={{0,4},{4,0},{8,12},{12,8},{16,20},{20,16},{24,28},{28,24},{1,5},{5... | collective-permute-start | bytes 1572872 | tf_op jit(solution)/shard_map/ppermute | solution.py:1253
  435.1 14.4 %collective-permute-start.5 = (bf16[8,64,512]{2,1,0:T(8,128)(2,1)S(1)}, bf16[8,64,512]{2,1,0:T(8,128)(2,1)S(1)}, u32[]{:S(2)}, u32[]{:S(2)}) collective-permute-start(bf16[8,64,512]{2,1,0:T(8,128)(2,1)S(1)} %get-tuple-element.66), channel_id=1, source_target_pairs={{0,1},{1,0},{2,3},{3,2},{4,5},{5,4},{6,7},{7,6},{8,9},{9,8},{10,11... | collective-permute-start | bytes 1572872 | tf_op jit(solution)/shard_map/ppermute | solution.py:1247
  435.1 39.1 %collective-permute-start.6 = (bf16[8,64,512]{2,1,0:T(8,128)(2,1)S(1)}, bf16[8,64,512]{2,1,0:T(8,128)(2,1)S(1)}, u32[]{:S(2)}, u32[]{:S(2)}) collective-permute-start(bf16[8,64,512]{2,1,0:T(8,128)(2,1)S(1)} %get-tuple-element.68), channel_id=1, source_target_pairs={{0,2},{1,3},{2,0},{3,1},{4,6},{5,7},{6,4},{7,5},{8,10},{9,11},{10,... | collective-permute-start | bytes 1572872 | tf_op jit(solution)/shard_map/ppermute | solution.py:1247
  440.9 1.8 copy-start.20
  440.9 2.1 copy-start.21
  441.3 34.3 %collective-permute-start.7 = (bf16[8,64,512]{2,1,0:T(8,128)(2,1)S(1)}, bf16[8,64,512]{2,1,0:T(8,128)(2,1)S(1)}, u32[]{:S(2)}, u32[]{:S(2)}) collective-permute-start(bf16[8,64,512]{2,1,0:T(8,128)(2,1)S(1)} %get-tuple-element.67), channel_id=1, source_target_pairs={{0,3},{1,2},{2,1},{3,0},{4,7},{5,6},{6,5},{7,4},{8,11},{9,10},{10,... | collective-permute-start | bytes 1572872 | tf_op jit(solution)/shard_map/ppermute | solution.py:1247
  449.5 110.6 %collective-permute-start.17 = (bf16[512,2048]{1,0:T(8,128)(2,1)}, bf16[512,2048]{1,0:T(8,128)(2,1)}, u32[]{:S(2)}, u32[]{:S(2)}) collective-permute-start(bf16[512,2048]{1,0:T(8,128)(2,1)} %get-tuple-element.61), channel_id=1, source_target_pairs={{0,24},{4,28},{8,16},{12,20},{16,8},{20,12},{24,0},{28,4},{1,25},{... | collective-permute-start | bytes 6291464 | tf_op jit(solution)/shard_map/ppermute | solution.py:1250
  474.2 24.4 %collective-permute-start.28 = (bf16[64,2048]{1,0:T(8,128)(2,1)S(1)}, bf16[64,2048]{1,0:T(8,128)(2,1)S(1)}, u32[]{:S(2)}, u32[]{:S(2)}) collective-permute-start(bf16[64,2048]{1,0:T(8,128)(2,1)S(1)} %get-tuple-element.91), channel_id=1, source_target_pairs={{0,8},{4,12},{8,0},{12,4},{16,24},{20,28},{24,16},{28,20},{1,9},{5... | collective-permute-start | bytes 786440 | tf_op jit(solution)/shard_map/ppermute | solution.py:1250
  475.5 25.3 %collective-permute-start.29 = (bf16[64,2048]{1,0:T(8,128)(2,1)S(1)}, bf16[64,2048]{1,0:T(8,128)(2,1)S(1)}, u32[]{:S(2)}, u32[]{:S(2)}) collective-permute-start(bf16[64,2048]{1,0:T(8,128)(2,1)S(1)} %get-tuple-element.90), channel_id=1, source_target_pairs={{0,16},{4,20},{8,24},{12,28},{16,0},{20,4},{24,8},{28,12},{1,17},{... | collective-permute-start | bytes 786440 | tf_op jit(solution)/shard_map/ppermute | solution.py:1250
  498.6 7.3 %collective-permute-start.30 = (bf16[64,2048]{1,0:T(8,128)(2,1)S(1)}, bf16[64,2048]{1,0:T(8,128)(2,1)S(1)}, u32[]{:S(2)}, u32[]{:S(2)}) collective-permute-start(bf16[64,2048]{1,0:T(8,128)(2,1)S(1)} %get-tuple-element.89), channel_id=1, source_target_pairs={{0,24},{4,28},{8,16},{12,20},{16,8},{20,12},{24,0},{28,4},{1,25},{... | collective-permute-start | bytes 786440 | tf_op jit(solution)/shard_map/ppermute | solution.py:1250
  500.8 5.2 collective-permute-start.8
  507.3 6.4 %collective-permute-start.9 = (bf16[64,1024]{1,0:T(8,128)(2,1)S(1)}, bf16[64,1024]{1,0:T(8,128)(2,1)S(1)}, u32[]{:S(2)}, u32[]{:S(2)}) collective-permute-start(bf16[64,1024]{1,0:T(8,128)(2,1)S(1)} %get-tuple-element.118), channel_id=1, source_target_pairs={{0,8},{4,12},{8,0},{12,4},{16,24},{20,28},{24,16},{28,20},{1,9},{5... | collective-permute-start | bytes 393224 | tf_op jit(solution)/shard_map/ppermute | solution.py:1250
  508.0 6.3 %collective-permute-start.10 = (bf16[64,1024]{1,0:T(8,128)(2,1)S(1)}, bf16[64,1024]{1,0:T(8,128)(2,1)S(1)}, u32[]{:S(2)}, u32[]{:S(2)}) collective-permute-start(bf16[64,1024]{1,0:T(8,128)(2,1)S(1)} %get-tuple-element.117), channel_id=1, source_target_pairs={{0,16},{4,20},{8,24},{12,28},{16,0},{20,4},{24,8},{28,12},{1,17},{... | collective-permute-start | bytes 393224 | tf_op jit(solution)/shard_map/ppermute | solution.py:1250
  510.9 34.0 %copy-start.8 = (bf16[1,128,2048]{2,1,0:T(8,128)(2,1)S(1)}, bf16[1,128,2048]{2,1,0:T(8,128)(2,1)}, u32[]{:S(2)}) copy-start(bf16[1,128,2048]{2,1,0:T(8,128)(2,1)} %param.13) | copy-start | bytes 1572868
  510.9 34.0 %copy-start.27 = (f32[2048]{0:T(1024)S(1)}, f32[2048]{0:T(1024)}, u32[]{:S(2)}) copy-start(f32[2048]{0:T(1024)} %param.21) | copy-start | bytes 24580
  513.7 15.2 %collective-permute-start.2 = (bf16[128,2048]{1,0:T(8,128)(2,1)S(1)}, bf16[128,2048]{1,0:T(8,128)(2,1)S(1)}, u32[]{:S(2)}, u32[]{:S(2)}) collective-permute-start(bf16[128,2048]{1,0:T(8,128)(2,1)S(1)} %get-tuple-element.78), channel_id=1, source_target_pairs={{0,8},{4,12},{8,0},{12,4},{16,24},{20,28},{24,16},{28,20},{1,9},{5... | collective-permute-start | bytes 1572872 | tf_op jit(solution)/shard_map/ppermute | solution.py:1250
  514.3 13.1 %collective-permute-start.11 = (bf16[64,1024]{1,0:T(8,128)(2,1)S(1)}, bf16[64,1024]{1,0:T(8,128)(2,1)S(1)}, u32[]{:S(2)}, u32[]{:S(2)}) collective-permute-start(bf16[64,1024]{1,0:T(8,128)(2,1)S(1)} %get-tuple-element.116), channel_id=1, source_target_pairs={{0,24},{4,28},{8,16},{12,20},{16,8},{20,12},{24,0},{28,4},{1,25},{... | collective-permute-start | bytes 393224 | tf_op jit(solution)/shard_map/ppermute | solution.py:1250
  527.4 17.5 %collective-permute-start.3 = (bf16[128,2048]{1,0:T(8,128)(2,1)S(1)}, bf16[128,2048]{1,0:T(8,128)(2,1)S(1)}, u32[]{:S(2)}, u32[]{:S(2)}) collective-permute-start(bf16[128,2048]{1,0:T(8,128)(2,1)S(1)} %get-tuple-element.80), channel_id=1, source_target_pairs={{0,16},{4,20},{8,24},{12,28},{16,0},{20,4},{24,8},{28,12},{1,17},{... | collective-permute-start | bytes 1572872 | tf_op jit(solution)/shard_map/ppermute | solution.py:1250
  528.9 16.0 %collective-permute-start.4 = (bf16[128,2048]{1,0:T(8,128)(2,1)S(1)}, bf16[128,2048]{1,0:T(8,128)(2,1)S(1)}, u32[]{:S(2)}, u32[]{:S(2)}) collective-permute-start(bf16[128,2048]{1,0:T(8,128)(2,1)S(1)} %get-tuple-element.79), channel_id=1, source_target_pairs={{0,24},{4,28},{8,16},{12,20},{16,8},{20,12},{24,0},{28,4},{1,25},{... | collective-permute-start | bytes 1572872 | tf_op jit(solution)/shard_map/ppermute | solution.py:1250
  530.9 14.8 %copy-start.25 = (f32[64,1024]{1,0:T(8,128)}, f32[64,1024]{1,0:T(8,128)S(1)}, u32[]{:S(2)}) copy-start(f32[64,1024]{1,0:T(8,128)S(1)} %get-tuple-element.178) | copy-start | bytes 786436
  530.9 14.8 %copy-start.26 = (f32[64,1024]{1,0:T(8,128)}, f32[64,1024]{1,0:T(8,128)S(1)}, u32[]{:S(2)}) copy-start(f32[64,1024]{1,0:T(8,128)S(1)} %get-tuple-element.179) | copy-start | bytes 786436
  530.9 14.8 %copy-start.22 = (f32[64,2048]{1,0:T(8,128)}, f32[64,2048]{1,0:T(8,128)S(1)}, u32[]{:S(2)}) copy-start(f32[64,2048]{1,0:T(8,128)S(1)} %slice_dynamic-update-slice_fusion.8) | copy-start | bytes 1572868
  545.8 19.7 %collective-permute-start.31 = (f32[2,8,64]{2,1,0:T(8,128)S(1)}, f32[2,8,64]{2,1,0:T(8,128)S(1)}, u32[]{:S(2)}, u32[]{:S(2)}) collective-permute-start(f32[2,8,64]{2,1,0:T(8,128)S(1)} %bitcast.256), channel_id=1, source_target_pairs={{0,1},{1,0},{2,3},{3,2},{4,5},{5,4},{6,7},{7,6},{8,9},{9,8},{10,11... | collective-permute-start | bytes 12296 | tf_op jit(solution)/shard_map/ppermute | solution.py:1247
  556.7 8.8 %collective-permute-start.32 = (f32[2,8,64]{2,1,0:T(8,128)S(1)}, f32[2,8,64]{2,1,0:T(8,128)S(1)}, u32[]{:S(2)}, u32[]{:S(2)}) collective-permute-start(f32[2,8,64]{2,1,0:T(8,128)S(1)} %bitcast.255), channel_id=1, source_target_pairs={{0,2},{1,3},{2,0},{3,1},{4,6},{5,7},{6,4},{7,5},{8,10},{9,11},{10,... | collective-permute-start | bytes 12296 | tf_op jit(solution)/shard_map/ppermute | solution.py:1247
  558.7 6.9 %collective-permute-start.33 = (f32[2,8,64]{2,1,0:T(8,128)S(1)}, f32[2,8,64]{2,1,0:T(8,128)S(1)}, u32[]{:S(2)}, u32[]{:S(2)}) collective-permute-start(f32[2,8,64]{2,1,0:T(8,128)S(1)} %bitcast.254), channel_id=1, source_target_pairs={{0,3},{1,2},{2,1},{3,0},{4,7},{5,6},{6,5},{7,4},{8,11},{9,10},{10,... | collective-permute-start | bytes 12296 | tf_op jit(solution)/shard_map/ppermute | solution.py:1247
  565.3 6.4 %copy-start.16 = (f32[128,2048]{1,0:T(8,128)S(1)}, f32[128,2048]{1,0:T(8,128)}, u32[]{:S(2)}) copy-start(f32[128,2048]{1,0:T(8,128)} %get-tuple-element.37) | copy-start | bytes 3145732
  565.4 9.8 %collective-permute-start.18 = (bf16[256,2048]{1,0:T(8,128)(2,1)S(1)}, bf16[256,2048]{1,0:T(8,128)(2,1)S(1)}, u32[]{:S(2)}, u32[]{:S(2)}) collective-permute-start(bf16[256,2048]{1,0:T(8,128)(2,1)S(1)} %dynamic-slice_bitcast_fusion.3), channel_id=1, source_target_pairs={{0,4},{4,0},{8,12},{12,8},{16,20},{20,16},{24,28},{28,24},{1,5},{5... | collective-permute-start | bytes 3145736 | tf_op jit(solution)/shard_map/ppermute | solution.py:1253
  565.6 2.6 collective-permute-start.34
  568.2 4.7 collective-permute-start.35
  569.6 3.6 collective-permute-start.36
  570.3 4.5 collective-permute-start.37
  576.0 21.9 %collective-permute-start.19 = (bf16[64,4096]{1,0:T(8,128)(2,1)S(1)}, bf16[64,4096]{1,0:T(8,128)(2,1)S(1)}, u32[]{:S(2)}, u32[]{:S(2)}) collective-permute-start(bf16[64,4096]{1,0:T(8,128)(2,1)S(1)} %get-tuple-element.73), channel_id=1, source_target_pairs={{0,1},{1,0},{2,3},{3,2},{4,5},{5,4},{6,7},{7,6},{8,9},{9,8},{10,11... | collective-permute-start | bytes 1572872 | tf_op jit(solution)/shard_map/ppermute | solution.py:1247
  577.1 38.2 %collective-permute-start.20 = (bf16[64,4096]{1,0:T(8,128)(2,1)S(1)}, bf16[64,4096]{1,0:T(8,128)(2,1)S(1)}, u32[]{:S(2)}, u32[]{:S(2)}) collective-permute-start(bf16[64,4096]{1,0:T(8,128)(2,1)S(1)} %get-tuple-element.72), channel_id=1, source_target_pairs={{0,2},{1,3},{2,0},{3,1},{4,6},{5,7},{6,4},{7,5},{8,10},{9,11},{10,... | collective-permute-start | bytes 1572872 | tf_op jit(solution)/shard_map/ppermute | solution.py:1247
  578.8 36.8 %collective-permute-start.21 = (bf16[64,4096]{1,0:T(8,128)(2,1)S(1)}, bf16[64,4096]{1,0:T(8,128)(2,1)S(1)}, u32[]{:S(2)}, u32[]{:S(2)}) collective-permute-start(bf16[64,4096]{1,0:T(8,128)(2,1)S(1)} %get-tuple-element.71), channel_id=1, source_target_pairs={{0,3},{1,2},{2,1},{3,0},{4,7},{5,6},{6,5},{7,4},{8,11},{9,10},{10,... | collective-permute-start | bytes 1572872 | tf_op jit(solution)/shard_map/ppermute | solution.py:1247
  615.4 2.5 copy-start.1
  615.8 2.2 copy-start.11
  615.8 2.2 copy-start.13
  (5 other events, 6.4 us)

commit v4 on v3

--- a/solution.py
+++ b/solution.py
@@ -466,97 +466,6 @@
     return jnp.where(mask, scores, MASKED)
 
 
-def attend_kernel(query, key, value, code, low_code, key_code, attended, log_total):
-    scores = scores_of(query[...], key[...], code[...], low_code[...], key_code[...])
-    top = jnp.max(scores, axis=-1, keepdims=True)
-    weights = jnp.exp(scores - top)
-    total = jnp.sum(weights, axis=-1, keepdims=True)
-    mixed = dot_nn(weights.astype(BF16), value[...])
-    attended[...] = (mixed / total).astype(BF16)
-    log_total[...] = top + jnp.log(total)
-
-
-def attend(query, key, value, code, low_code, key_code):
-    rows, head = query.shape
-    step = math.gcd(rows, VISIBLE_ROWS)
-    by_row = lambda width: pl.BlockSpec((step, width), lambda i: (i, 0))
-    whole = lambda shape: pl.BlockSpec(shape, lambda i: (0, 0))
-    return pl.pallas_call(
-        attend_kernel,
-        grid=(rows // step,),
-        in_specs=[
-            by_row(head),
-            whole(key.shape),
-            whole(value.shape),
-            by_row(1),
-            by_row(1),
-            whole(key_code.shape),
-        ],
-        out_specs=[by_row(head), by_row(1)],
-        out_shape=[
-            jax.ShapeDtypeStruct((rows, head), BF16),
-            jax.ShapeDtypeStruct((rows, 1), F32),
-        ],
-        compiler_params=pltpu.CompilerParams(vmem_limit_bytes=32 << 20),
-        cost_estimate=pl.CostEstimate(
-            flops=4 * rows * key.shape[0] * head,
-            bytes_accessed=8 * rows * head,
-            transcendentals=rows * key.shape[0],
-        ),
-    )(query, key, value, code, low_code, key_code)
-
-
-def attend_back_kernel(
-    query, outgrad, key, value, log_total, code, low_code, key_code, d_query, d_key, d_value
-):
-    @pl.when(pl.program_id(0) == 0)
-    def _():
-        d_key[...] = jnp.zeros_like(d_key)
-        d_value[...] = jnp.zeros_like(d_value)
-
-    scores = scores_of(query[...], key[...], code[...], low_code[...], key_code[...])
-    probs = jnp.exp(scores - log_total[...])
-    prob_grad = dot_nt(outgrad[...], value[...])
-    delta = jnp.sum(probs * prob_grad, axis=-1, keepdims=True)
-    score_grad = (probs * (prob_grad - delta)).astype(BF16)
-    d_query[...] = dot_nn(score_grad, key[...]) * SCORE_SCALE
-    d_key[...] += dot_tn(score_grad, query[...]) * SCORE_SCALE
-    d_value[...] += dot_tn(probs.astype(BF16), outgrad[...])
-
-
-def attend_back(query, outgrad, key, value, log_total, code, low_code, key_code):
-    rows, head = query.shape
-    step = math.gcd(rows, VISIBLE_ROWS)
-    by_row = lambda width: pl.BlockSpec((step, width), lambda i: (i, 0))
-    whole = lambda shape: pl.BlockSpec(shape, lambda i: (0, 0))
-    return pl.pallas_call(
-        attend_back_kernel,
-        grid=(rows // step,),
-        in_specs=[
-            by_row(head),
-            by_row(head),
-            whole(key.shape),
-            whole(value.shape),
-            by_row(1),
-            by_row(1),
-            by_row(1),
-            whole(key_code.shape),
-        ],
-        out_specs=[by_row(head), whole(key.shape), whole(value.shape)],
-        out_shape=[
-            jax.ShapeDtypeStruct((rows, head), F32),
-            jax.ShapeDtypeStruct(key.shape, F32),
-            jax.ShapeDtypeStruct(value.shape, F32),
-        ],
-        compiler_params=pltpu.CompilerParams(vmem_limit_bytes=40 << 20),
-        cost_estimate=pl.CostEstimate(
-            flops=10 * rows * key.shape[0] * head,
-            bytes_accessed=20 * rows * head,
-            transcendentals=rows * key.shape[0],
-        ),
-    )(query, outgrad, key, value, log_total, code, low_code, key_code)
-
-
 MESH = pl.DeviceIdType.MESH
 TILE = 256
 
@@ -579,6 +488,7 @@
     gain_grad_ref,
     branch_all,
     gate_up_terms,
+    gate_up_near,
     down_terms,
     gate_w,
     up_w,
@@ -727,19 +637,23 @@
     def to_hbm(slot, target):
         return pltpu.make_async_copy(staged.at[slot], target, staged_sem.at[slot])
 
-    def gate_up_step(d):
+    chunks = (1, 2, 3, 0)
+    near = {}
+    for i, d in enumerate(chunks):
         for h in range(2):
             first = flip(chip, d) * (2 * TILE) + h * TILE
             left = second_rows[:, pl.ds(pl.multiple_of(first, TILE), TILE)]
             target = gate_up_terms.at[d, pl.ds(h * TILE, TILE)]
-            if d:
+            if i:
                 to_hbm(h, target).wait()
+            if h and 1 <= i <= 2:
+                done = chunks[i - 1]
+                near[done] = send(
+                    27 + done, gate_up_terms.at[done], gate_up_near.at[done - 1], over_chips[done]
+                )
             staged[h, :, :hidden] = dot_tn(left, gate_grad[...]).astype(BF16)
             staged[h, :, hidden:] = dot_tn(left, up_grad[...]).astype(BF16)
             to_hbm(h, target).start()
-
-    for d in range(4):
-        gate_up_step(d)
 
     for d in (1, 2, 3):
         planes[d].wait_recv()
@@ -806,6 +720,8 @@
         for copy in (gather_z[d], planes[d], out_planes[d], branch_chips[d]):
             copy.wait_send()
     keep.wait()
+    for d in (1, 2):
+        near[d].wait()
     for slot in range(2):
         to_hbm(slot, down_terms.at[pl.ds(0, TILE)]).wait()
 
@@ -819,13 +735,14 @@
     return pl.pallas_call(
         mlp_kernel,
         in_specs=[vmem] * 4 + [hbm] * 4,
-        out_specs=[vmem] * 3 + [hbm] * 3,
+        out_specs=[vmem] * 3 + [hbm] * 4,
         out_shape=[
             jax.ShapeDtypeStruct((tok, width), BF16),
             jax.ShapeDtypeStruct((tok, width), F32),
             jax.ShapeDtypeStruct((1, width), F32),
             jax.ShapeDtypeStruct((2, 4, tok, width), BF16),
             jax.ShapeDtypeStruct((4, 2 * TILE, 2 * hidden), BF16),
+            jax.ShapeDtypeStruct((2, 2 * TILE, 2 * hidden), BF16),
             jax.ShapeDtypeStruct((hidden, width), BF16),
         ],
         scratch_shapes=[
@@ -847,8 +764,8 @@
             pltpu.VMEM((2, TILE, width), BF16),
             pltpu.SemaphoreType.DMA((5,)),
             pltpu.SemaphoreType.DMA((2,)),
-            pltpu.SemaphoreType.DMA((28,)),
-            pltpu.SemaphoreType.DMA((28,)),
+            pltpu.SemaphoreType.DMA((30,)),
+            pltpu.SemaphoreType.DMA((30,)),
         ],
         compiler_params=pltpu.CompilerParams(
             collective_id=1, has_side_effects=True, vmem_limit_bytes=60 << 20
@@ -1195,23 +1112,425 @@
     )
 
 
-def rotate_head(values, cosine, sine):
-    half = values.shape[-1] // 2
-    first, second = values[:, :half], values[:, half:]
-    return jnp.concatenate([first * cosine - second * sine, second * cosine + first * sine], axis=1)
-
-
-def swap_halves(values):
-    half = values.shape[0] // 2
-    return jnp.concatenate([values[half:], values[:half]], axis=0)
-
-
-def index_of(stacked, i):
-    return lax.dynamic_index_in_dim(stacked, i, 0, keepdims=False)
-
-
-def cut(values, starts, sizes):
-    return lax.dynamic_slice(values, starts, sizes)
+def back_kernel(
+    input_ref,
+    mid_grad_ref,
+    attn_gain_ref,
+    mlp_gain_grad_ref,
+    cosine_ref,
+    sine_ref,
+    code_ref,
+    low_code_ref,
+    key_code_ref,
+    normed_ref,
+    query_ref,
+    kv_ref,
+    attended_ref,
+    log_total_ref,
+    w_head,
+    w_sibling,
+    out_rows_ref,
+    branch_hbm,
+    gate_up_terms,
+    gate_up_near,
+    down_terms,
+    grad_input_ref,
+    gain_total_ref,
+    grad_out_ref,
+    head_in,
+    gate_up_in,
+    down_in,
+    branch_all,
+    d_attended,
+    d_head,
+    d_other,
+    d_kv,
+    d_kv_other,
+    out_send,
+    out_recv,
+    head_terms,
+    head_recv,
+    own_sum,
+    chip_send,
+    chip_recv,
+    gate_up_parts,
+    gate_up_sum,
+    down_parts,
+    down_sum,
+    down_planes,
+    gains,
+    gains_z,
+    gains_ctx,
+    local_sem,
+    send_sem,
+    recv_sem,
+):
+    tok, width = input_ref.shape
+    seq = 8 * tok
+    half_seq = 4 * tok
+    share = out_send.shape[1]
+    ctx, plane = lax.axis_index("ctx"), lax.axis_index("shard")
+    chip, core = ctx // 2, ctx % 2
+    other_core = 1 - core
+    sibling = (2 * chip + other_core, plane)
+    over_z = [(ctx, flip(plane, d)) for d in range(4)]
+    over_chips = [(2 * flip(chip, d) + core, plane) for d in range(4)]
+    over_chips_cross = [(2 * flip(chip, d) + other_core, plane) for d in range(4)]
+    over_z_cross = [(2 * chip + other_core, flip(plane, d)) for d in range(4)]
+    others = (1, 2, 3)
+
+    def at(i, size):
+        return pl.ds(pl.multiple_of(i * size, size), size)
+
+    def remote(slot, source, target, device):
+        return pltpu.make_async_remote_copy(
+            src_ref=source,
+            dst_ref=target,
+            send_sem=send_sem.at[slot],
+            recv_sem=recv_sem.at[slot],
+            device_id=device,
+            device_id_type=MESH,
+        )
+
+    def send(slot, source, target, device):
+        copy = remote(slot, source, target, device)
+        copy.start()
+        return copy
+
+    def local(slot, source, target):
+        return pltpu.make_async_copy(source, target, local_sem.at[slot])
+
+    loads = [
+        local(0, branch_hbm, branch_all),
+        local(1, gate_up_terms.at[0], gate_up_parts.at[0]),
+        local(2, gate_up_near, gate_up_parts.at[pl.ds(1, 2)]),
+        local(3, down_terms.at[:, chip], down_parts.at[0]),
+    ]
+    for load in loads:
+        load.start()
+
+    barrier = pltpu.get_barrier_semaphore()
+    partners = (
+        over_z[1:] + over_z_cross + over_chips[1:] + over_chips_cross[1:]
+    )
+    for partner in partners:
+        pl.semaphore_signal(barrier, inc=1, device_id=partner, device_id_type=MESH)
+    pl.semaphore_wait(barrier, len(partners))
+
+    gate_up_far = send(0, gate_up_terms.at[3], gate_up_parts.at[3], over_chips[3])
+    down_chips = {
+        d: send(d, down_terms.at[:, flip(chip, d)], down_parts.at[d], over_chips[d])
+        for d in others
+    }
+
+    loads[0].wait()
+
+    def out_step(t, carry):
+        here = at(t, TILE)
+        made = dot_tn(attended_ref[...], branch_all[:, here])
+        out_send[:, :, here] = made.reshape(4, share, TILE).astype(BF16)
+        return carry
+
+    lax.fori_loop(0, width // TILE, out_step, 0)
+    out_z = {
+        d: send(3 + d, out_send.at[flip(plane, d)], out_recv.at[d - 1], over_z[d]) for d in others
+    }
+
+    def attended_step(t, carry):
+        here = at(t, TILE)
+        d_attended[here, :] = dot_nt(branch_all[here, :], out_rows_ref[...]).astype(BF16)
+        return carry
+
+    lax.fori_loop(0, seq // TILE, attended_step, 0)
+    d_kv[...] = jnp.zeros_like(d_kv)
+
+    def attend_step(t, carry):
+        here = at(t, TILE)
+        query, outgrad = query_ref[here, :], d_attended[here, :]
+        scores = scores_of(
+            query, kv_ref[0], code_ref[here, :], low_code_ref[here, :], key_code_ref[...]
+        )
+        probs = jnp.exp(scores - log_total_ref[here, :])
+        prob_grad = dot_nt(outgrad, kv_ref[1])
+        delta = jnp.sum(probs * prob_grad, axis=-1, keepdims=True)
+        score_grad = (probs * (prob_grad - delta)).astype(BF16)
+        d_query = dot_nn(score_grad, kv_ref[0]) * SCORE_SCALE
+        d_head[here, :HD] = rotated(d_query, cosine_ref[here, :], -sine_ref[here, :]).astype(BF16)
+        d_kv[0] += dot_tn(score_grad, query)
+        d_kv[1] += dot_tn(probs.astype(BF16), outgrad)
+        return carry
+
+    lax.fori_loop(0, seq // TILE, attend_step, 0)
+
+    give = d_kv.at[other_core]
+    kv_pair = [
+        send(
+            7 + e,
+            give.at[pl.ds(e * half_seq, half_seq)],
+            d_kv_other.at[pl.ds((1 - e) * half_seq, half_seq)],
+            sibling,
+        )
+        for e in range(2)
+    ]
+    for copy in kv_pair:
+        copy.wait_recv()
+
+    def kv_step(t, carry):
+        here = at(t, TILE)
+        total = d_kv[core, here, :] + d_kv_other[here, :]
+        total = total * jnp.where(core == 0, SCORE_SCALE, 1.0)
+        cosine = jnp.where(core == 0, cosine_ref[here, :], 1.0)
+        sine = jnp.where(core == 0, sine_ref[here, :], 0.0)
+        d_head[here, HD:] = rotated(total, cosine, -sine).astype(BF16)
+        return carry
+
+    lax.fori_loop(0, seq // TILE, kv_step, 0)
+    head_pair = send(9, d_head.at[pl.ds(half_seq, half_seq)], d_other, sibling)
+
+    def head_step(t, carry):
+        made = dot_tn(normed_ref[:, at(t, TILE)], d_head[...])
+        head_terms[:, t] = made.reshape(4, share, 2 * HD).astype(BF16)
+        return carry
+
+    lax.fori_loop(0, width // TILE, head_step, 0)
+    head_z = {
+        d: send(9 + d, head_terms.at[flip(plane, d)], head_recv.at[d - 1], over_z[d])
+        for d in others
+    }
+
+    head_pair.wait_recv()
+
+    def normed_step(t, carry):
+        here = at(t, TILE)
+        made = (
+            dot_nt(d_head[:half_seq, :HD], w_head[0, here, :])
+            + dot_nt(d_head[:half_seq, HD:], w_head[1, here, :])
+            + dot_nt(d_other[:, :HD], w_sibling[0, here, :])
+            + dot_nt(d_other[:, HD:], w_sibling[1, here, :])
+        )
+        own_sum[:, here] = made[:tok]
+        for d in others:
+            chip_send[d - 1, :, here] = made[d * tok : (d + 1) * tok].astype(BF16)
+        return carry
+
+    lax.fori_loop(0, width // TILE, normed_step, 0)
+    normed_chips = {
+        d: send(12 + d, chip_send.at[d - 1], chip_recv.at[d - 1], over_chips[d]) for d in others
+    }
+
+    loads[3].wait()
+    for d in others:
+        down_chips[d].wait_recv()
+
+    def down_step(p, carry):
+        total = down_parts[0, p].astype(F32)
+        for d in others:
+            total = total + down_parts[d, p].astype(F32)
+        down_sum[p] = total.astype(BF16)
+        return carry
+
+    lax.fori_loop(0, 4, down_step, 0)
+    down_z = {
+        d: send(15 + d, down_sum.at[flip(plane, d)], down_planes.at[plane], over_z[d])
+        for d in others
+    }
+    keep_down = local(3, down_sum.at[plane], down_planes.at[plane])
+    keep_down.start()
+
+    loads[1].wait()
+    loads[2].wait()
+    gate_up_far.wait_recv()
+
+    def gate_up_step(i, carry):
+        here = at(i, share)
+        total = gate_up_parts[0, here, :].astype(F32)
+        for d in others:
+            total = total + gate_up_parts[d, here, :].astype(F32)
+        gate_up_sum[i // 4, i % 4] = total.astype(BF16)
+        return carry
+
+    lax.fori_loop(0, 8, gate_up_step, 0)
+    place = gate_up_in.at[plane, core]
+    gate_up_z = {
+        d: send(18 + d, gate_up_sum.at[core, flip(plane, d)], place, over_z[d]) for d in others
+    }
+    gate_up_cross = {
+        d: send(22 + d, gate_up_sum.at[other_core, flip(plane, d)], place, over_z_cross[d])
+        for d in range(4)
+    }
+    keep_gate_up = local(1, gate_up_sum.at[core, plane], place)
+    keep_gate_up.start()
+
+    for d in others:
+        normed_chips[d].wait_recv()
+    chunk = 32
+    gain = attn_gain_ref[...]
+
+    def input_step(i, carry):
+        here = at(i, chunk)
+        grad = own_sum[here, :]
+        for d in range(3):
+            grad = grad + chip_recv[d, here, :].astype(F32)
+        block = input_ref[here, :].astype(F32)
+        factor = lax.rsqrt(jnp.mean(block * block, axis=-1, keepdims=True) + EPSILON)
+        scaled = grad * gain
+        grad_input_ref[here, :] = (
+            mid_grad_ref[here, :]
+            + factor * scaled
+            - block * (factor * factor * factor * jnp.mean(scaled * block, axis=-1, keepdims=True))
+        ).astype(BF16)
+        return carry + jnp.sum(grad * block * factor, axis=0, keepdims=True)
+
+    gain_grad = lax.fori_loop(0, tok // chunk, input_step, jnp.zeros((1, width), F32))
+    gains[...] = jnp.concatenate(
+        [gain_grad, mlp_gain_grad_ref[...], jnp.zeros((6, width), F32)], axis=0
+    )
+    gains_planes = {d: send(25 + d, gains, gains_z.at[d - 1], over_z[d]) for d in others}
+
+    for d in others:
+        out_z[d].wait_recv()
+    total = out_send[plane].astype(F32)
+    for d in range(3):
+        total = total + out_recv[d].astype(F32)
+    grad_out_ref[...] = total
+
+    for d in others:
+        head_z[d].wait_recv()
+
+    def head_sum(i, carry):
+        total = head_terms[plane, i].astype(F32)
+        for d in range(3):
+            total = total + head_recv[d, i].astype(F32)
+        head_terms[plane, i] = total.astype(BF16)
+        return carry
+
+    lax.fori_loop(0, 8, head_sum, 0)
+    head_place = head_in.at[ctx]
+    head_chips = {
+        d: send(28 + d, head_terms.at[plane, 2 * flip(chip, d) + core], head_place, over_chips[d])
+        for d in others
+    }
+    head_cross = {
+        d: send(
+            32 + d, head_terms.at[plane, 2 * flip(chip, d) + other_core], head_place,
+            over_chips_cross[d],
+        )
+        for d in range(4)
+    }
+    keep_head = local(0, head_terms.at[plane, ctx], head_place)
+    keep_head.start()
+
+    for d in others:
+        gains_planes[d].wait_recv()
+        gains_planes[d].wait_send()
+    gains[...] = gains[...] + gains_z[0] + gains_z[1] + gains_z[2]
+    gains_chips = {
+        d: send(35 + d, gains, gains_ctx.at[0, d], over_chips[d]) for d in others
+    }
+    gains_cross = {
+        d: send(39 + d, gains, gains_ctx.at[1, d], over_chips_cross[d]) for d in range(4)
+    }
+
+    keep_down.wait()
+    down_place = down_in.at[chip]
+    for d in range(4):
+        if d:
+            down_z[d].wait_recv()
+        source = flip(plane, d)
+        apart = xor4(chip, source)
+        block = down_planes.at[source]
+
+        @pl.when(apart == 0)
+        def _(block=block):
+            local(4, block, down_place).start()
+
+        @pl.when(apart != 0)
+        def _(block=block, source=source, apart=apart):
+            remote(42 + apart, block, down_place, (2 * source + core, plane)).start()
+
+    for d in others:
+        gains_chips[d].wait_recv()
+    for d in range(4):
+        gains_cross[d].wait_recv()
+    total = gains[...] + gains_ctx[1, 0]
+    for d in others:
+        total = total + gains_ctx[0, d] + gains_ctx[1, d]
+    gain_total_ref[...] = total
+
+    local(4, down_sum.at[plane], down_place).wait()
+    keep_gate_up.wait()
+    keep_head.wait()
+    for d in others:
+        remote(42 + d, down_sum.at[plane], down_place, over_chips[d]).wait()
+        gate_up_z[d].wait_recv()
+        head_chips[d].wait_recv()
+        for copies in (
+            down_chips, out_z, head_z, normed_chips, down_z, gate_up_z, head_chips, gains_chips
+        ):
+            copies[d].wait_send()
+    for d in range(4):
+        for copies in (gate_up_cross, head_cross):
+            copies[d].wait()
+        gains_cross[d].wait_send()
+    for copy in (gate_up_far, head_pair, *kv_pair):
+        copy.wait_send()
+
+
+def back_of(*operands):
+    inputs, query, out_rows = operands[0], operands[10], operands[16]
+    tok, width = inputs.shape
+    seq = query.shape[0]
+    hidden = operands[20].shape[0] * operands[20].shape[1] * operands[20].shape[2]
+    share = HD // 4
+    vmem = pl.BlockSpec(memory_space=pltpu.VMEM)
+    hbm = pl.BlockSpec(memory_space=pl.ANY)
+    return pl.pallas_call(
+        back_kernel,
+        in_specs=[vmem] * 17 + [hbm] * 4,
+        out_specs=[vmem] * 6,
+        out_shape=[
+            jax.ShapeDtypeStruct((tok, width), BF16),
+            jax.ShapeDtypeStruct((8, width), F32),
+            jax.ShapeDtypeStruct((share, width), F32),
+            jax.ShapeDtypeStruct((8, share, 2 * HD), BF16),
+            jax.ShapeDtypeStruct((4, 2, share, 2 * hidden), BF16),
+            jax.ShapeDtypeStruct((4, share, width), BF16),
+        ],
+        scratch_shapes=[
+            pltpu.VMEM((seq, width), BF16),
+            pltpu.VMEM((seq, HD), BF16),
+            pltpu.VMEM((seq, 2 * HD), BF16),
+            pltpu.VMEM((4 * tok, 2 * HD), BF16),
+            pltpu.VMEM((2, seq, HD), F32),
+            pltpu.VMEM((seq, HD), F32),
+            pltpu.VMEM((4, share, width), BF16),
+            pltpu.VMEM((3, share, width), BF16),
+            pltpu.VMEM((4, 8, share, 2 * HD), BF16),
+            pltpu.VMEM((3, 8, share, 2 * HD), BF16),
+            pltpu.VMEM((tok, width), F32),
+            pltpu.VMEM((3, tok, width), BF16),
+            pltpu.VMEM((3, tok, width), BF16),
+            pltpu.VMEM((4, 2 * TILE, 2 * hidden), BF16),
+            pltpu.VMEM((2, 4, share, 2 * hidden), BF16),
+            pltpu.VMEM((4, 4, share, width), BF16),
+            pltpu.VMEM((4, share, width), BF16),
+            pltpu.VMEM((4, share, width), BF16),
+            pltpu.VMEM((8, width), F32),
+            pltpu.VMEM((3, 8, width), F32),
+            pltpu.VMEM((2, 4, 8, width), F32),
+            pltpu.SemaphoreType.DMA((5,)),
+            pltpu.SemaphoreType.DMA((46,)),
+            pltpu.SemaphoreType.DMA((46,)),
+        ],
+        compiler_params=pltpu.CompilerParams(
+            collective_id=3, has_side_effects=True, vmem_limit_bytes=60 << 20
+        ),
+        cost_estimate=pl.CostEstimate(
+            flops=2 * seq * width * 6 * HD + 10 * seq * seq * HD,
+            bytes_accessed=20 * seq * width,
+            transcendentals=seq * seq,
+        ),
+    )(*operands)
 
 
 def on_device_by_head(
@@ -1235,55 +1554,10 @@
     chips = ctx_count // 2
     ctx, plane = lax.axis_index("ctx"), lax.axis_index("shard")
     chip, core = ctx // 2, ctx % 2
-    first_core = core == 0
     seq_rows = tok_rows * ctx_count
-    half_seq = seq_rows // 2
-    shard_width = w_down.shape[1]
-    hidden_plane = w_gate.shape[1]
-    hidden = hidden_plane // 2
     own_share = width // (planes * ctx_count)
 
-    def over_z(values, d):
-        return lax.ppermute(values, "shard", [(i, i ^ d) for i in range(planes)])
-
-    def over_chips(values, d):
-        return lax.ppermute(values, "ctx", [(i, i ^ (2 * d)) for i in range(ctx_count)])
-
-    def sibling(values):
-        return lax.ppermute(values, "ctx", [(i, i ^ 1) for i in range(ctx_count)])
-
-    z_steps = range(1, planes)
-    chip_steps = range(1, chips)
-
-    def gather_z(values):
-        return [values] + [over_z(values, d) for d in z_steps]
-
-    def gather_chips(values):
-        return [values] + [over_chips(values, d) for d in chip_steps]
-
-    def gather_seq(values):
-        mine = jnp.concatenate(gather_chips(values), axis=0)
-        return jnp.concatenate([mine, sibling(mine)], axis=0)
-
-    def gather_group(values):
-        mine = jnp.stack(gather_z(values))
-        return jnp.stack([mine, sibling(mine)], axis=1).reshape(-1, width)
-
-    def sum_chips(block_of):
-        total = block_of(0)
-        for d in chip_steps:
-            total = total + over_chips(block_of(d).astype(BF16), d).astype(F32)
-        return total
-
-    def sum_z(block_of):
-        total = block_of(0)
-        for d in z_steps:
-            total = total + over_z(block_of(d).astype(BF16), d).astype(F32)
-        return total
-
-    quarter = width // chips
     inputs_low = layer_input[0]
-    inputs = inputs_low.astype(F32)
     pairs, documents = block_pairs[0], doc_ids[0]
     order = jnp.stack([(chip ^ d) * 2 + (core ^ e) for e in range(2) for d in range(chips)])
     rows = (order[:, None] * tok_rows + jnp.arange(tok_rows, dtype=jnp.int32)[None, :]).reshape(-1)
@@ -1325,125 +1599,53 @@
         w_down,
         upstream_low,
     )
-    key, value = key_value[0], key_value[1]
-    out_rows = out_pair[0]
-    upstream_group = upstream_group.reshape(-1, width)
-    key_cosine = jnp.where(first_core, cosine, 1.0)
-    key_sine = jnp.where(first_core, sine, 0.0)
-    factor_one = lax.rsqrt(jnp.mean(inputs * inputs, axis=-1, keepdims=True) + EPSILON)
-    output, mid_grad, mlp_gain_term, branch_grad_all, gate_up_terms, down_terms = mlp_of(
-        normed_two, mid, upstream_low, mlp_gain[None], upstream_group, w_gate, w_up, down_rows
-    )
-    output = output[None]
-    mlp_gain_term = mlp_gain_term[0]
-    branch_grad_all = branch_grad_all.reshape(seq_rows, width)
-
-    attended_grad = dot_nt(branch_grad_all, out_rows).astype(BF16)
-    d_query, d_key, d_value = attend_back(
-        query, attended_grad, key, value, log_total, code_column, low_column, code_row
-    )
-    keep = jnp.where(first_core, d_key, d_value)
-    give = jnp.where(first_core, d_value, d_key)
-    d_kv = keep + swap_halves(sibling(give))
-    d_head = jnp.concatenate(
-        [rotate_head(d_query, cosine, -sine), rotate_head(d_kv, key_cosine, -key_sine)], axis=1
-    ).astype(BF16)
-    d_head_pair = jnp.concatenate([d_head[:half_seq], sibling(d_head[half_seq:])], axis=1)
-    w_head_pair = jnp.concatenate([w_head[0], w_head[1], w_sibling[0], w_sibling[1]], axis=1)
-    normed_parts = dot_nt(d_head_pair, w_head_pair).reshape(chips, tok_rows, width)
-    normed_grad = sum_chips(lambda d: normed_parts[d])
-    attn_gain_term = jnp.sum(normed_grad * inputs * factor_one, axis=0)
-    scaled_one = normed_grad * attn_gain
-    grad_input = (
-        mid_grad
-        + factor_one * scaled_one
-        - inputs * factor_one**3 * jnp.mean(scaled_one * inputs, axis=-1, keepdims=True)
-    ).astype(BF16)[None]
-
-    mlp_sum = sum_chips(lambda d: gate_up_terms[d].astype(F32)).astype(BF16).reshape(2, quarter // 2, 2 * hidden)
-    mlp_mine = index_of(mlp_sum, core)
-    mlp_other = sibling(index_of(mlp_sum, 1 - core))
-    left_half = jnp.where(first_core, mlp_mine, mlp_other)
-    right_half = jnp.where(first_core, mlp_other, mlp_mine)
-    mlp_rows_all = jnp.concatenate(
-        [left_half[:, :hidden], right_half[:, :hidden], left_half[:, hidden:], right_half[:, hidden:]],
-        axis=1,
-    ).reshape(planes, own_share, 2 * hidden_plane)
-    grad_gate = jnp.zeros((own_share, planes * hidden_plane), F32)
-    grad_up = jnp.zeros((own_share, planes * hidden_plane), F32)
-    for d in range(planes):
-        part = index_of(mlp_rows_all, plane ^ d)
-        if d:
-            part = over_z(part, d)
-        part = part.astype(F32)
-        at = (0, hidden_plane * (plane ^ d))
-        grad_gate = lax.dynamic_update_slice(grad_gate, part[:, :hidden_plane], at)
-        grad_up = lax.dynamic_update_slice(grad_up, part[:, hidden_plane:], at)
-
-    down_terms = down_terms.reshape(planes, chips, -1, width)
-    down_sum = sum_chips(
-        lambda d: lax.dynamic_index_in_dim(down_terms, chip ^ d, 1, keepdims=False).astype(F32)
-    ).astype(BF16)
-    down_parts = []
-    for d in range(planes):
-        part = index_of(down_sum, plane ^ d)
-        down_parts.append(over_z(part, d) if d else part)
-    down_parts = jnp.stack(down_parts)
-    share = down_parts.shape[1]
-    grad_down = jnp.zeros((chips * share, width), F32)
-    for d in range(chips):
-        part = index_of(down_parts, plane ^ chip ^ d)
-        if d:
-            part = over_chips(part, d)
-        grad_down = lax.dynamic_update_slice(grad_down, part.astype(F32), (share * (chip ^ d), 0))
-
-    out_terms = dot_tn(attended, branch_grad_all).reshape(planes, own_share, width)
-    grad_out = sum_z(lambda d: index_of(out_terms, plane ^ d))
-
-    head_terms = dot_tn(normed_all, d_head).reshape(ctx_count, planes, own_share, 2 * HD)
-    head_sum = sum_z(
-        lambda d: lax.dynamic_index_in_dim(head_terms, plane ^ d, 1, keepdims=False)
-    ).astype(BF16)
-    head_sum = head_sum.reshape(chips, 2, own_share, 2 * HD)
-    head_mine = lax.dynamic_index_in_dim(head_sum, core, 1, keepdims=False)
-    head_other = sibling(lax.dynamic_index_in_dim(head_sum, 1 - core, 1, keepdims=False))
-    left_half = jnp.where(first_core, head_mine, head_other)
-    right_half = jnp.where(first_core, head_other, head_mine)
-    head_rows = jnp.concatenate(
-        [left_half[..., :HD], right_half[..., :HD], left_half[..., HD:], right_half[..., HD:]], axis=2
-    )
-    grad_query = jnp.zeros((own_share, HQ * HD), F32)
-    grad_key = jnp.zeros((own_share, HK * HD), F32)
-    grad_value = jnp.zeros((own_share, HK * HD), F32)
-    for d in range(chips):
-        part = index_of(head_rows, chip ^ d)
-        if d:
-            part = over_chips(part, d)
-        part = part.astype(F32)
-        grad_query = lax.dynamic_update_slice(grad_query, part[:, : 2 * HD], (0, 2 * HD * (chip ^ d)))
-        grad_key = lax.dynamic_update_slice(grad_key, part[:, 2 * HD : 3 * HD], (0, HD * (chip ^ d)))
-        grad_value = lax.dynamic_update_slice(grad_value, part[:, 3 * HD :], (0, HD * (chip ^ d)))
-
-    gains = jnp.stack([attn_gain_term, mlp_gain_term]).reshape(2, ctx_count, planes, own_share)
-
-    def gain_block(d):
-        return lax.dynamic_index_in_dim(gains, plane ^ d, 2, keepdims=False)
-
-    gain_sum = gain_block(0)
-    for d in z_steps:
-        gain_sum = gain_sum + over_z(gain_block(d), d)
-    gain_sum = gain_sum.reshape(2, chips, 2, own_share)
-    gain_sum = lax.dynamic_index_in_dim(gain_sum, core, 2, keepdims=False) + sibling(
-        lax.dynamic_index_in_dim(gain_sum, 1 - core, 2, keepdims=False)
-    )
-    gain_mine = lax.dynamic_index_in_dim(gain_sum, chip, 1, keepdims=False)
-    for d in chip_steps:
-        gain_mine = gain_mine + over_chips(
-            lax.dynamic_index_in_dim(gain_sum, chip ^ d, 1, keepdims=False), d
-        )
+    output, mid_grad, mlp_gain_grad, branch_all, gate_up_terms, gate_up_near, down_terms = mlp_of(
+        normed_two,
+        mid,
+        upstream_low,
+        mlp_gain[None],
+        upstream_group.reshape(-1, width),
+        w_gate,
+        w_up,
+        down_rows,
+    )
+    grad_input, gain_total, grad_out, head_in, gate_up_in, down_in = back_of(
+        inputs_low,
+        mid_grad,
+        attn_gain[None],
+        mlp_gain_grad,
+        cosine,
+        sine,
+        code_column,
+        low_column,
+        code_row,
+        normed_all,
+        query,
+        key_value,
+        attended,
+        log_total,
+        w_head,
+        w_sibling,
+        out_pair[0],
+        branch_all.reshape(seq_rows, width),
+        gate_up_terms,
+        gate_up_near,
+        down_terms.reshape(planes, chips, -1, width),
+    )
+    hidden = gate_up_in.shape[-1] // 2
+    gate_up = gate_up_in.astype(F32)
+    columns = lambda parts: jnp.concatenate(parts, axis=1)
+    grad_gate = columns([gate_up[p, e, :, :hidden] for p in range(planes) for e in range(2)])
+    grad_up = columns([gate_up[p, e, :, hidden:] for p in range(planes) for e in range(2)])
+    head = head_in.astype(F32)
+    grad_query = columns([head[i, :, :HD] for i in range(ctx_count)])
+    grad_key = columns([head[i, :, HD:] for i in range(0, ctx_count, 2)])
+    grad_value = columns([head[i, :, HD:] for i in range(1, ctx_count, 2)])
+    grad_down = down_in.astype(F32).reshape(-1, width)
+    gains = lax.dynamic_slice(gain_total, (0, own_share * (planes * ctx + plane)), (2, own_share))
     return (
-        output,
-        grad_input,
+        output[None],
+        grad_input[None],
         grad_query,
         grad_key,
         grad_value,
@@ -1451,8 +1653,8 @@
         grad_gate,
         grad_up,
         grad_down,
-        gain_mine[0],
-        gain_mine[1],
+        gains[0],
+        gains[1],
     )
 
 

time: 628 us -> 563 us (0.90); the launches traced: 618 us -> 563 us
  Pallas kernels: 324 us -> 531 us
  waiting for transfers between devices: 137 us -> 0 us
  starting transfers between devices: 83.5 us -> 0 us
  local copies, waits for them, and re-layouts: 30.8 us -> 14.6 us
  other arithmetic: 31 us -> 16.4 us
  matrix products: 9.51 us -> 0 us
    pallas_call x1, Pallas kernels: 5.44 us -> 197 us  [back_of(): pl.pallas_call(back_kernel, in_specs=[vmem] * 17 + [hbm] * 4, out_specs=[...]
    ppermute x38 -> x0, waiting for transfers between devices: 137 us -> none  [the longest x15 79.2 us: over_z(): return lax.ppermute(values, 'shard', [(i, i ^ d) for i in range(planes)])]
    ppermute x38 -> x0, starting transfers between devices: 83.5 us -> none  [the longest x15 55.7 us: over_z(): return lax.ppermute(values, 'shard', [(i, i ^ d) for i in range(planes)])]
    pallas_call x1, Pallas kernels: 157 us -> 172 us  [mlp_of(): pl.pallas_call(mlp_kernel, in_specs=[vmem] * 4 + [hbm] * 4, out_specs=[vm...]
    squeeze x8 -> x3, local copies, waits for them, and re-layouts: 12.7 us -> 2.86 us  [the longest x1 2.3 us: on_device_by_head(): out_pair[0]]
    dot_general x4 -> x0, matrix products: 9.51 us -> none  [the longest x2 5.86 us: dot_tn(): lax.dot_general(a, b, (((0,), (0,)), ((), ())), preferred_element_type=F32)]
    convert_element_type x9 -> x2, other arithmetic: 8.68 us -> 1.76 us  [the longest x1 1.25 us: on_device_by_head(): head = head_in.astype(F32)]
  transfers between devices with their start and end apart: 38 -> 0, of which waited for: 15 -> 0; matrix products, arithmetic and copies ran while one was open for 6% -> 0% of each run, Pallas kernels for 1% -> 0%
where the time goes in v4:
time: 563 us
  Pallas kernels  531 us (94%)
  other arithmetic  16.4 us (3%)
  local copies, waits for them, and re-layouts  14.6 us (3%)
    pallas_call x1, Pallas kernels, back_of(): pl.pallas_call(back_kernel, in_specs=[vmem] * 17 + [hbm] * 4, out_specs=[...  197 us
    pallas_call x1, Pallas kernels, mlp_of(): pl.pallas_call(mlp_kernel, in_specs=[vmem] * 4 + [hbm] * 4, out_specs=[vm...  172 us
    pallas_call x1, Pallas kernels, front_of(): pl.pallas_call(front_kernel, in_specs=[vmem] * 8 + [hbm] * 6, out_specs=[...  162 us

profile of v4, /device:TPU:0, one launch (start us, length us, event | category | flops | bytes accessed | tf_op | source)
XLA Modules:
  0.0 562.6 jit_solution(10623906501146370693)
XLA Ops:
  0.6 0.0 copy-start
  0.7 0.1 stack.35
  0.8 0.6 copy-done
  1.3 0.1 iota_add_fusion
  1.4 1.6 fusion.33
  3.0 0.2 copy.24
  3.2 5.2 select_reduce_fusion
  8.4 0.5 compare_reduce_fusion
  8.9 0.7 select_convert_fusion
  9.6 0.2 copy.28
  9.8 0.9 fusion.1
  10.7 4.5 gather_fusion
  15.2 0.7 multiply_add_fusion.key_code_ref
  15.9 0.2 copy.29
  16.1 1.2 add_maximum_fusion
  17.3 3.0 multiply_sine_fusion
  20.3 161.7 %shard_map.212 = (bf16[128,2048]{1,0:T(8,128)(2,1)}, f32[128,2048]{1,0:T(8,128)}, bf16[1024,2048]{1,0:T(8,128)(2,1)}, bf16[1024,256]{1,0:T(8,128)(2,1)}, bf16[2,...) custom-call(bf16[128,2048]{1,0:T(8,128)(2,1)} %bitcast.194, ...), custom_call_target="tpu_custom_call" | custom-call | flops 4294967296 | bytes 41943040 | tf_op jit(solution)/shard_map/pallas_call | solution.py:1072
  182.0 2.3 slice_bitcast_fusion.out_rows_ref
  184.3 171.9 %shard_map.213 = (bf16[128,2048]{1,0:T(8,128)(2,1)}, f32[128,2048]{1,0:T(8,128)}, f32[1,2048]{1,0:T(1,128)}, bf16[2,4,128,2048]{3,2,1,0:T(8,128)(2,1)}, bf16[4,5...) custom-call(bf16[128,2048]{1,0:T(8,128)(2,1)} %get-tuple-element.36.second_ref, ...), custom_call_target="tpu_custom_call" | custom-call | flops 38654705664 | bytes 37748736 | tf_op jit(solution)/shard_map/pallas_call | solution.py:735
  356.3 197.0 %shard_map.214 = (bf16[128,2048]{1,0:T(8,128)(2,1)}, f32[8,2048]{1,0:T(8,128)}, f32[64,2048]{1,0:T(8,128)}, bf16[8,64,512]{2,1,0:T(8,128)(2,1)}, bf16[4,2,64,204...) custom-call(bf16[128,2048]{1,0:T(8,128)(2,1)} %bitcast.195, f32[128,2048]{1,0:T(8,128)} %get-tuple-element.41.mid_grad_ref, ...), custom_call_target="tpu_custom_call" | custom-call | flops 9126805504 | bytes 41943040 | tf_op jit(solution)/shard_map/pallas_call | solution.py:1487
  553.3 0.8 constant_dynamic-slice_fusion
  554.0 0.5 slice_bitcast_fusion.33
  554.5 0.0 copy-start.3
  554.5 1.2 convert_element_type.15
  555.9 0.0 copy-start.9
  556.0 0.0 copy-start.2
  556.0 0.8 pad_maximum_fusion
  556.8 0.0 copy-done.3
  556.8 1.6 bitcast_convert_fusion
  558.5 0.0 copy-done.9
  558.5 0.0 copy-done.2
  558.5 0.5 convert_element_type.16
  559.2 0.0 copy-start.4
  559.2 0.0 copy-start.6
  559.3 0.0 copy-start.5
  559.3 0.0 copy-start.1
  559.4 0.0 copy-start.7
  559.4 0.0 copy-start.8
  559.4 0.8 copy-done.4
  560.2 0.8 copy.54
  561.0 0.0 copy-done.6
  561.0 0.8 copy.55
  561.8 0.0 copy-done.5
  561.8 0.8 copy.56
  562.6 0.0 copy-done.7
  562.6 0.0 copy-done.8
  562.6 0.0 copy-done.1
  (20 shorter events, 0.4 us)
Async XLA Ops:
  0.6 0.7 copy-start
  554.5 2.3 copy-start.3
  555.9 2.6 copy-start.9
  556.0 2.5 copy-start.2
  559.2 1.0 copy-start.4
  559.2 1.8 copy-start.6
  559.3 2.5 copy-start.5
  559.3 3.3 copy-start.1
  559.4 3.2 copy-start.7
  559.4 3.2 copy-start.8

commit v5 on v4

--- a/solution.py
+++ b/solution.py
@@ -1,4 +1,3 @@
-import functools
 import math
 
 import jax
@@ -443,6 +442,7 @@
     )
 
 
+DOCS = 4
 BF16 = jnp.bfloat16
 F32 = jnp.float32
 VISIBLE_ROWS = 256
@@ -472,6 +472,61 @@
 
 def flip(i, d):
     return (i, i + 1 - 2 * (i % 2), (i + 2) % 4, 3 - i)[d]
+
+
+def line_gather(remote, ctx, plane, slot, own, place):
+    def copy(i, way, block, source):
+        to = plane + way
+        return remote(
+            slot + 2 * i + (way + 1) // 2, source, place(to, block), (ctx, to), slot + block
+        )
+
+    def sends(i):
+        if i == 0:
+            return [(plane < 3, lambda: copy(0, 1, plane, own)), (plane > 0, lambda: copy(0, -1, plane, own))]
+        return [
+            (
+                jnp.logical_and(plane >= i, plane < 3),
+                lambda: copy(i, 1, plane - i, place(plane, plane - i)),
+            ),
+            (
+                jnp.logical_and(plane + i <= 3, plane > 0),
+                lambda: copy(i, -1, plane + i, place(plane, plane + i)),
+            ),
+        ]
+
+    def start(i):
+        for whether, made in sends(i):
+
+            @pl.when(whether)
+            def _(made=made):
+                made().start()
+
+    def step(i, then=None):
+        for whether, block in ((plane >= i, plane - i), (plane + i <= 3, plane + i)):
+
+            @pl.when(whether)
+            def _(block=block):
+                remote(slot, own, place(plane, block), (ctx, plane), slot + block).wait_recv()
+                if then is not None:
+                    then(block)
+
+        if i < 3:
+            start(i)
+
+    def finish():
+        for i in range(3):
+            for whether, made in sends(i):
+
+                @pl.when(whether)
+                def _(made=made):
+                    made().wait_send()
+
+    return start, step, finish
+
+
+def xor4(a, b):
+    return 2 * ((a // 2 + b // 2) % 2) + (a % 2 + b % 2) % 2
 
 
 def mlp_kernel(
@@ -538,19 +593,25 @@
         pl.semaphore_signal(barrier, inc=1, device_id=partner, device_id_type=MESH)
     pl.semaphore_wait(barrier, len(partners))
 
-    def send(slot, source, target, device):
-        copy = pltpu.make_async_remote_copy(
+    def remote(slot, source, target, device, recv=None):
+        return pltpu.make_async_remote_copy(
             src_ref=source,
             dst_ref=target,
             send_sem=send_sem.at[slot],
-            recv_sem=recv_sem.at[slot],
+            recv_sem=recv_sem.at[slot if recv is None else recv],
             device_id=device,
             device_id_type=MESH,
         )
+
+    def send(slot, source, target, device):
+        copy = remote(slot, source, target, device)
         copy.start()
         return copy
 
-    gather_z = {d: send(d, second_ref, second_all.at[d, 0], over_z[d]) for d in (1, 2, 3)}
+    start_line, step_line, finish_line = line_gather(
+        remote, ctx, plane, 30, second_ref, lambda r, b: second_all.at[xor4(r, b), 0]
+    )
+    start_line(0)
     gather_pair = {0: send(0, second_ref, second_all.at[0, 1], sibling)}
     for load in loads:
         load.wait()
@@ -599,7 +660,12 @@
             own_sum[which] = total
             return None
         z_send[which, d - 1] = total.astype(BF16)
-        return send(base + 3 + d, z_send.at[which, d - 1], z_recv.at[which, d - 1], over_z[d])
+        copy = remote(
+            base + 3 + d, z_send.at[which, d - 1], z_recv.at[which, d - 1], over_z[d]
+        )
+        if which == 0:
+            copy.start()
+        return copy
 
     def back(d):
         rows = rows_of(d)
@@ -614,7 +680,7 @@
     pairs, planes = {}, {}
     for d in range(4):
         if d:
-            gather_z[d].wait_recv()
+            step_line(d)
             gather_pair[d] = send(
                 3 + d, second_all.at[d, 0], second_all.at[d, 1], sibling
             )
@@ -657,6 +723,8 @@
 
     for d in (1, 2, 3):
         planes[d].wait_recv()
+    for d in (1, 2, 3):
+        out_planes[d].start()
     chunk = 32
     gain = gain_ref[...]
 
@@ -717,8 +785,9 @@
         for copy in (gather_pair[d], pairs[d], out_pairs[d], branch_pairs[d]):
             copy.wait_send()
     for d in (1, 2, 3):
-        for copy in (gather_z[d], planes[d], out_planes[d], branch_chips[d]):
+        for copy in (planes[d], out_planes[d], branch_chips[d]):
             copy.wait_send()
+    finish_line()
     keep.wait()
     for d in (1, 2):
         near[d].wait()
@@ -764,8 +833,8 @@
             pltpu.VMEM((2, TILE, width), BF16),
             pltpu.SemaphoreType.DMA((5,)),
             pltpu.SemaphoreType.DMA((2,)),
-            pltpu.SemaphoreType.DMA((30,)),
-            pltpu.SemaphoreType.DMA((30,)),
+            pltpu.SemaphoreType.DMA((36,)),
+            pltpu.SemaphoreType.DMA((36,)),
         ],
         compiler_params=pltpu.CompilerParams(
             collective_id=1, has_side_effects=True, vmem_limit_bytes=60 << 20
@@ -776,10 +845,6 @@
             transcendentals=rows * hidden,
         ),
     )(normed_two, mid, upstream, gain, upstream_group, w_gate, w_up, down_rows)
-
-
-def xor4(a, b):
-    return 2 * ((a // 2 + b // 2) % 2) + (a % 2 + b % 2) % 2
 
 
 def rotated(values, cosine, sine):
@@ -842,12 +907,12 @@
     def at(i, size):
         return pl.ds(pl.multiple_of(i * size, size), size)
 
-    def remote(slot, source, target, device):
+    def remote(slot, source, target, device, recv=None):
         return pltpu.make_async_remote_copy(
             src_ref=source,
             dst_ref=target,
             send_sem=send_sem.at[slot],
-            recv_sem=recv_sem.at[slot],
+            recv_sem=recv_sem.at[slot if recv is None else recv],
             device_id=device,
             device_id_type=MESH,
         )
@@ -885,8 +950,15 @@
         first = to_plane * (2 * hidden) + core * hidden + chip * part
         return down_hbm.at[pl.ds(pl.multiple_of(first, part), part), :]
 
-    down_place = down_rows.at[at(chip, part), at(plane, shard)]
-    keep_down = local(4, down_block(plane), down_place)
+    def down_place(column):
+        return down_rows.at[at(chip, part), at(column, shard)]
+
+    first_own = plane * (2 * hidden) + core * hidden
+    keep_down = local(
+        4,
+        down_hbm.at[pl.ds(pl.multiple_of(first_own, hidden), hidden), :],
+        down_rows.at[:, at(plane, shard)],
+    )
     keep_down.start()
     keep_upstream = local(5, upstream_hbm, upstream_all.at[0, 0])
     keep_upstream.start()
@@ -903,8 +975,32 @@
     input_pairs = {0: send(3, input_ref, inputs_all.at[1, 0], sibling)}
     load_query.wait()
     load_key.wait()
-    head_z = {d: send(6 + d, mine, w_parts.at[plane], over_z[d]) for d in others}
-
+    start_head, step_head, finish_head = line_gather(
+        remote, ctx, plane, 37, mine, lambda r, b: w_parts.at[b]
+    )
+    start_out, step_out, finish_out = line_gather(
+        remote, ctx, plane, 43, out_own, lambda r, b: out_pair.at[0, :, at(b, shard)]
+    )
+    start_up, step_up, finish_up = line_gather(
+        remote, ctx, plane, 49, upstream_hbm, lambda r, b: upstream_all.at[xor4(r, b), 0]
+    )
+    start_head(0)
+
+    head_rows = w_head.at[:, rows, :]
+
+    def pass_head(source):
+        apart = xor4(chip, source)
+        block = w_parts.at[source]
+
+        @pl.when(apart == 0)
+        def _():
+            local(6, block, head_rows).start()
+
+        @pl.when(apart != 0)
+        def _():
+            remote(9 + apart, block, head_rows, (2 * source + core, plane)).start()
+
+    pass_head(plane)
     chunk = 32
     attn_gain = attn_gain_ref[...]
 
@@ -922,38 +1018,31 @@
 
     keep_input.wait()
     norm(0, 0)
-    for d in others:
+    step_head(1, pass_head)
+    input_pairs[0].wait_recv()
+    norm(1, 0)
+    for d in (1, 2):
         input_chips[d].wait_recv()
         input_pairs[d] = send(3 + d, inputs_all.at[0, d], inputs_all.at[1, d], sibling)
-        norm(0, d)
-    for d in range(4):
+    norm(0, 1)
+    norm(0, 2)
+    step_head(2, pass_head)
+    input_chips[3].wait_recv()
+    input_pairs[3] = send(6, inputs_all.at[0, 3], inputs_all.at[1, 3], sibling)
+    norm(0, 3)
+    for d in others:
         input_pairs[d].wait_recv()
         norm(1, d)
-
-    head_rows = w_head.at[:, rows, :]
-    for d in range(4):
-        if d:
-            head_z[d].wait_recv()
-        source = flip(plane, d)
-        apart = xor4(chip, source)
-        block = w_parts.at[source]
-
-        @pl.when(apart == 0)
-        def _(block=block):
-            local(6, block, head_rows).start()
-
-        @pl.when(apart != 0)
-        def _(block=block, source=source, apart=apart):
-            remote(9 + apart, block, head_rows, (2 * source + core, plane)).start()
-
-    out_z = {
-        d: send(12 + d, out_own, out_pair.at[0, :, at(plane, shard)], over_z[d]) for d in others
+    step_head(3, pass_head)
+
+    down_z = {
+        d: send(16 + d, down_block(flip(plane, d)), down_place(plane), over_z[d]) for d in others
     }
+    start_out(0)
     local(6, mine, head_rows).wait()
     for d in others:
         remote(9 + d, mine, head_rows, over_chips[d]).wait_recv()
     head_pair = send(16, w_head, w_sibling, sibling)
-    down_z = {d: send(16 + d, down_block(flip(plane, d)), down_place, over_z[d]) for d in others}
 
     def project(which, target, flat):
         def step(t, carry):
@@ -976,6 +1065,7 @@
         for e in range(2)
     ]
     project(0, query_ref, False)
+    step_out(1)
     for copy in kv_pair:
         copy.wait_recv()
 
@@ -994,9 +1084,17 @@
 
     lax.fori_loop(0, seq // TILE, attend_step, 0)
     attended_pair = send(22, attended_ref.at[pl.ds(half_seq, half_seq)], attended_other, sibling)
+    step_out(2)
+    for d in others:
+        down_z[d].wait_recv()
+    down_chips = {}
+    for e in others:
+        for d in others:
+            block = down_place(flip(plane, d))
+            down_chips[e, d] = send(51 + 3 * e + d, block, block, over_chips[e])
+    step_out(3)
+    start_up(0)
     keep_out.wait()
-    for d in others:
-        out_z[d].wait_recv()
     out_sibling = send(23, out_pair.at[0], out_pair.at[1], sibling)
     attended_pair.wait_recv()
     out_sibling.wait_recv()
@@ -1016,18 +1114,16 @@
         d: send(23 + d, chip_send.at[d - 1], chip_recv.at[d - 1], over_chips[d]) for d in others
     }
 
-    keep_down.wait()
-    for d in others:
-        down_z[d].wait_recv()
-    upstream_z = {
-        d: send(29 + d, upstream_hbm, upstream_all.at[d, 0], over_z[d]) for d in others
-    }
     upstream_pair = {0: send(33, upstream_hbm, upstream_all.at[0, 1], sibling)}
 
+    def pass_up(d):
+        step_up(d)
+        upstream_pair[d] = send(33 + d, upstream_all.at[d, 0], upstream_all.at[d, 1], sibling)
+
+    pass_up(1)
+    pass_up(2)
     for d in others:
         branch[d].wait_recv()
-    down_mine = down_rows.at[at(chip, part), :]
-    down_chips = {d: send(26 + d, down_mine, down_mine, over_chips[d]) for d in others}
     mlp_gain = mlp_gain_ref[...]
 
     def mid_step(i, carry):
@@ -1042,9 +1138,7 @@
 
     lax.fori_loop(0, tok // chunk, mid_step, 0)
 
-    for d in others:
-        upstream_z[d].wait_recv()
-        upstream_pair[d] = send(33 + d, upstream_all.at[d, 0], upstream_all.at[d, 1], sibling)
+    pass_up(3)
     keep_upstream.wait()
     for d in range(4):
         upstream_pair[d].wait_recv()
@@ -1053,11 +1147,16 @@
     head_pair.wait_recv()
     for copy in (head_pair, attended_pair, out_sibling, *kv_pair):
         copy.wait_send()
+    keep_down.wait()
     for d in others:
-        down_chips[d].wait_recv()
-        for copies in (input_chips, head_z, out_z, down_z, branch, down_chips, upstream_z):
+        for e in others:
+            down_chips[e, d].wait()
+        for copies in (input_chips, down_z, branch):
             copies[d].wait_send()
         remote(9 + d, mine, head_rows, over_chips[d]).wait_send()
+    finish_head()
+    finish_out()
+    finish_up()
 
 
 def front_of(
@@ -1095,8 +1194,8 @@
             pltpu.VMEM((3, tok, width), BF16),
             pltpu.VMEM((3, tok, width), BF16),
             pltpu.SemaphoreType.DMA((7,)),
-            pltpu.SemaphoreType.DMA((37,)),
-            pltpu.SemaphoreType.DMA((37,)),
+            pltpu.SemaphoreType.DMA((64,)),
+            pltpu.SemaphoreType.DMA((64,)),
         ],
         compiler_params=pltpu.CompilerParams(
             collective_id=2, has_side_effects=True, vmem_limit_bytes=56 << 20
@@ -1560,10 +1659,19 @@
     inputs_low = layer_input[0]
     pairs, documents = block_pairs[0], doc_ids[0]
     order = jnp.stack([(chip ^ d) * 2 + (core ^ e) for e in range(2) for d in range(chips)])
-    rows = (order[:, None] * tok_rows + jnp.arange(tok_rows, dtype=jnp.int32)[None, :]).reshape(-1)
-    positions = position_of(rows, pairs, tok_rows, 2 * ctx_count).astype(jnp.int32)
+    chosen = jnp.sum(
+        jnp.where(order[:, None] == jnp.arange(ctx_count)[None, :], pairs[None, :], 0), axis=1
+    )[:, None]
+    within = jnp.arange(tok_rows, dtype=jnp.int32)[None, :]
+    block = tok_rows // 2
+    positions = jnp.where(
+        within < block, chosen * block, (2 * ctx_count - 1 - chosen) * block - block
+    )
+    positions = (positions + within).reshape(-1)
+    begins = jnp.sum(documents[None, :] < jnp.arange(1, DOCS)[:, None], axis=1)
+    document = jnp.sum((positions[None, :] >= begins[:, None]).astype(jnp.int32), axis=0)
     span = 2 * seq_rows
-    doc_first = jnp.take(documents, positions).astype(jnp.int32) * span
+    doc_first = document * span
     code = doc_first + positions
     low_code = jnp.maximum(doc_first, code - (WINDOW - 1))
     code_column, low_column, code_row = code[:, None], low_code[:, None], code[None, :]

time: 563 us -> 510 us (0.906)
  Pallas kernels: 531 us -> 490 us
  local copies, waits for them, and re-layouts: 14.6 us -> 8.75 us
  other arithmetic: 16.4 us -> 10.6 us
    pallas_call x1, Pallas kernels: 172 us -> 146 us  [mlp_of(): pl.pallas_call(mlp_kernel, in_specs=[vmem] * 4 + [hbm] * 4, out_specs=[vm...]
    pallas_call x1, Pallas kernels: 162 us -> 150 us  [front_of(): pl.pallas_call(front_kernel, in_specs=[vmem] * 8 + [hbm] * 6, out_specs=[...]
    gather x4 -> x0, local copies, waits for them, and re-layouts: 6.53 us -> none  [the longest x2 4.75 us: on_device_by_head(): doc_first = jnp.take(documents, positions).astype(jnp.int32) * span]
    gather x3 -> x0, other arithmetic: 5.67 us -> none  [the longest x2 5.66 us: position_of(): chosen = jnp.take(pairs, device)]
where the time goes in v5:
time: 510 us
  Pallas kernels  490 us (96%)
  other arithmetic  10.6 us (2%)
  local copies, waits for them, and re-layouts  8.75 us (2%)
    pallas_call x1, Pallas kernels, back_of(): pl.pallas_call(back_kernel, in_specs=[vmem] * 17 + [hbm] * 4, out_specs=[...  194 us
    pallas_call x1, Pallas kernels, front_of(): pl.pallas_call(front_kernel, in_specs=[vmem] * 8 + [hbm] * 6, out_specs=[...  150 us
    pallas_call x1, Pallas kernels, mlp_of(): pl.pallas_call(mlp_kernel, in_specs=[vmem] * 4 + [hbm] * 4, out_specs=[vm...  146 us

profile of v5, /device:TPU:0, one launch (start us, length us, event | category | flops | bytes accessed | tf_op | source)
XLA Modules:
  0.0 509.9 jit_solution(6300999651775296371)
XLA Ops:
  0.7 0.1 stack.35
  0.8 0.8 select_reduce_fusion
  1.6 0.9 convert_reduce_fusion.1
  2.5 0.1 iota_add_fusion
  2.6 0.1 convert_reduce_fusion
  2.7 0.6 add.137.key_code_ref
  3.3 0.2 copy.32
  3.5 0.2 copy.31
  3.8 0.9 max.10.low_code_ref
  4.6 1.0 copy.33.code_ref
  5.6 3.0 multiply_sine_fusion
  8.7 150.0 %shard_map.212 = (bf16[128,2048]{1,0:T(8,128)(2,1)}, f32[128,2048]{1,0:T(8,128)}, bf16[1024,2048]{1,0:T(8,128)(2,1)}, bf16[1024,256]{1,0:T(8,128)(2,1)}, bf16[2,...) custom-call(bf16[128,2048]{1,0:T(8,128)(2,1)} %bitcast.150, ...), custom_call_target="tpu_custom_call" | custom-call | flops 4294967296 | bytes 41943040 | tf_op jit(solution)/shard_map/pallas_call | solution.py:1171
  158.7 2.3 slice_bitcast_fusion.out_rows_ref
  161.0 145.9 %shard_map.213 = (bf16[128,2048]{1,0:T(8,128)(2,1)}, f32[128,2048]{1,0:T(8,128)}, f32[1,2048]{1,0:T(1,128)}, bf16[2,4,128,2048]{3,2,1,0:T(8,128)(2,1)}, bf16[4,5...) custom-call(bf16[128,2048]{1,0:T(8,128)(2,1)} %get-tuple-element.36.second_ref, ...), custom_call_target="tpu_custom_call" | custom-call | flops 38654705664 | bytes 37748736 | tf_op jit(solution)/shard_map/pallas_call | solution.py:804
  306.9 193.6 %shard_map.214 = (bf16[128,2048]{1,0:T(8,128)(2,1)}, f32[8,2048]{1,0:T(8,128)}, f32[64,2048]{1,0:T(8,128)}, bf16[8,64,512]{2,1,0:T(8,128)(2,1)}, bf16[4,2,64,204...) custom-call(bf16[128,2048]{1,0:T(8,128)(2,1)} %bitcast.151, f32[128,2048]{1,0:T(8,128)} %get-tuple-element.41.mid_grad_ref, ...), custom_call_target="tpu_custom_call" | custom-call | flops 9126805504 | bytes 41943040 | tf_op jit(solution)/shard_map/pallas_call | solution.py:1586
  500.6 0.8 constant_dynamic-slice_fusion
  501.3 0.5 slice_bitcast_fusion.33
  501.8 0.0 copy-start.1
  501.8 1.2 convert_element_type.23
  503.2 0.0 copy-start.7
  503.3 0.0 copy-start
  503.3 0.8 pad_maximum_fusion
  504.1 0.0 copy-done.1
  504.1 1.6 bitcast_convert_fusion
  505.8 0.0 copy-done.7
  505.8 0.0 copy-done
  505.8 0.5 convert_element_type.24
  506.5 0.0 copy-start.2
  506.5 0.0 copy-start.4
  506.6 0.0 copy-start.3
  506.7 0.0 copy-start.5
  506.7 0.0 copy-start.6
  506.7 0.8 copy-done.2
  507.5 0.8 copy.59
  508.3 0.0 copy-done.4
  508.3 0.8 copy.60
  509.1 0.0 copy-done.3
  509.1 0.8 copy.61
  509.9 0.0 copy-done.5
  509.9 0.0 copy-done.6
  (23 shorter events, 0.4 us)
Async XLA Ops:
  501.8 2.3 copy-start.1
  503.2 2.6 copy-start.7
  503.3 2.5 copy-start
  506.5 1.0 copy-start.2
  506.5 1.8 copy-start.4
  506.6 2.5 copy-start.3
  506.7 3.2 copy-start.5
  506.7 3.2 copy-start.6

commit v6 on v5

--- a/solution.py
+++ b/solution.py
@@ -468,6 +468,7 @@
 
 MESH = pl.DeviceIdType.MESH
 TILE = 256
+WIDE = 512
 
 
 def flip(i, d):
@@ -542,8 +543,8 @@
     mid_grad_ref,
     gain_grad_ref,
     branch_all,
-    gate_up_terms,
-    gate_up_near,
+    gate_up_sum,
+    gate_up_send,
     down_terms,
     gate_w,
     up_w,
@@ -559,6 +560,7 @@
     pair_recv,
     z_send,
     z_recv,
+    first_recv,
     branch_low,
     staged,
     local_sem,
@@ -609,7 +611,7 @@
         return copy
 
     start_line, step_line, finish_line = line_gather(
-        remote, ctx, plane, 30, second_ref, lambda r, b: second_all.at[xor4(r, b), 0]
+        remote, ctx, plane, 32, second_ref, lambda r, b: second_all.at[xor4(r, b), 0]
     )
     start_line(0)
     gather_pair = {0: send(0, second_ref, second_all.at[0, 1], sibling)}
@@ -624,7 +626,7 @@
         second = lambda: second_all[d].reshape(pair, width)
 
         def step(t, carry):
-            at = pl.ds(pl.multiple_of(t * TILE, TILE), TILE)
+            at = pl.ds(pl.multiple_of(t * WIDE, WIDE), WIDE)
             act_grad = dot_nt(upstream_all[rows, :], down_w[at, :])
             gate = dot_nn(second(), gate_w[:, at])
             up_lin = dot_nn(second(), up_w[:, at])
@@ -637,19 +639,19 @@
             up_grad[rows, at] = (act_grad * swish).astype(BF16)
             return carry
 
-        lax.fori_loop(0, hidden // TILE, step, 0)
+        lax.fori_loop(0, hidden // WIDE, step, 0)
 
     def give_pair(d, base, product):
         which = 0 if base == 7 else 1
 
         def step(t, carry):
-            at = pl.ds(pl.multiple_of(t * TILE, TILE), TILE)
+            at = pl.ds(pl.multiple_of(t * WIDE, WIDE), WIDE)
             terms = product(at)
             held[d % 2, :, at] = terms[:tok]
             pair_send[which, d, :, at] = terms[tok:].astype(BF16)
             return carry
 
-        lax.fori_loop(0, width // TILE, step, 0)
+        lax.fori_loop(0, width // WIDE, step, 0)
         return send(base + d, pair_send.at[which, d], pair_recv.at[which, d], sibling)
 
     def give_plane(d, base, copy):
@@ -663,7 +665,7 @@
         copy = remote(
             base + 3 + d, z_send.at[which, d - 1], z_recv.at[which, d - 1], over_z[d]
         )
-        if which == 0:
+        if which == 0 or d == 1:
             copy.start()
         return copy
 
@@ -680,6 +682,7 @@
     pairs, planes = {}, {}
     for d in range(4):
         if d:
+            planes[d - 1] = give_plane(d - 1, 7, pairs[d - 1])
             step_line(d)
             gather_pair[d] = send(
                 3 + d, second_all.at[d, 0], second_all.at[d, 1], sibling
@@ -687,9 +690,23 @@
         gather_pair[d].wait_recv()
         forward(d)
         pairs[d] = give_pair(d, 7, back(d))
-        if d:
-            planes[d - 1] = give_plane(d - 1, 7, pairs[d - 1])
     planes[3] = give_plane(3, 7, pairs[3])
+
+    second_rows = second_all.reshape(8 * tok, width)
+    block = 2 * TILE
+
+    def terms(grads, d, target, first):
+        for h in range(2):
+            column = flip(chip, d) * block + h * TILE
+            left = second_rows[:, pl.ds(pl.multiple_of(column, TILE), TILE)]
+            target[pl.ds(first + h * TILE, TILE), :] = dot_tn(left, grads[...]).astype(BF16)
+
+    terms(gate_grad, 1, up_w, 0)
+    terms(gate_grad, 3, up_w, block)
+    first_gate = send(28, up_w.at[pl.ds(0, 2 * block)], first_recv.at[0], over_chips[1])
+    terms(up_grad, 2, up_w, 2 * block)
+    terms(up_grad, 3, up_w, 3 * block)
+    first_up = send(29, up_w.at[pl.ds(2 * block, 2 * block)], first_recv.at[1], over_chips[2])
 
     out_pairs, out_planes = {}, {}
     for d in range(4):
@@ -698,32 +715,12 @@
             out_planes[d - 1] = give_plane(d - 1, 14, out_pairs[d - 1])
     out_planes[3] = give_plane(3, 14, out_pairs[3])
 
-    second_rows = second_all.reshape(8 * tok, width)
-
-    def to_hbm(slot, target):
-        return pltpu.make_async_copy(staged.at[slot], target, staged_sem.at[slot])
-
-    chunks = (1, 2, 3, 0)
-    near = {}
-    for i, d in enumerate(chunks):
-        for h in range(2):
-            first = flip(chip, d) * (2 * TILE) + h * TILE
-            left = second_rows[:, pl.ds(pl.multiple_of(first, TILE), TILE)]
-            target = gate_up_terms.at[d, pl.ds(h * TILE, TILE)]
-            if i:
-                to_hbm(h, target).wait()
-            if h and 1 <= i <= 2:
-                done = chunks[i - 1]
-                near[done] = send(
-                    27 + done, gate_up_terms.at[done], gate_up_near.at[done - 1], over_chips[done]
-                )
-            staged[h, :, :hidden] = dot_tn(left, gate_grad[...]).astype(BF16)
-            staged[h, :, hidden:] = dot_tn(left, up_grad[...]).astype(BF16)
-            to_hbm(h, target).start()
+    terms(gate_grad, 2, gate_w, 2 * block)
+    terms(up_grad, 1, gate_w, 3 * block)
 
     for d in (1, 2, 3):
         planes[d].wait_recv()
-    for d in (1, 2, 3):
+    for d in (2, 3):
         out_planes[d].start()
     chunk = 32
     gain = gain_ref[...]
@@ -753,19 +750,53 @@
     keep = pltpu.make_async_copy(branch_low, branch_all.at[0, 0], local_sem.at[0])
     keep.start()
 
+    def to_hbm(slot, target):
+        return pltpu.make_async_copy(staged.at[slot], target, staged_sem.at[slot])
+
     def down_step(t):
         slot = t % 2
         target = down_terms.at[pl.ds(t * TILE, TILE)]
-        to_hbm(slot, target).wait()
+        if t > 1:
+            to_hbm(slot, target).wait()
         left = act[:, pl.ds(t * TILE, TILE)]
         staged[slot] = dot_tn(left, upstream_all[...]).astype(BF16)
         to_hbm(slot, target).start()
 
     for t in range(hidden // TILE):
         down_step(t)
+    terms(gate_grad, 0, gate_w, 0)
+    terms(up_grad, 0, gate_w, block)
     for d in (1, 2, 3):
         branch_chips[d].wait_recv()
         branch_pairs[d] = send(24 + d, branch_all.at[0, d], branch_all.at[1, d], sibling)
+
+    keep_second = [
+        pltpu.make_async_copy(
+            gate_w.at[pl.ds((2 + e) * block, block)], gate_up_send.at[e], local_sem.at[2 + e]
+        )
+        for e in range(2)
+    ]
+
+    def add_first(i, carry):
+        here = pl.ds(pl.multiple_of(i * 64, 64), 64)
+        for e in range(2):
+            mine = pl.ds(pl.multiple_of((2 + e) * block + i * 64, 64), 64)
+            far = pl.ds(pl.multiple_of(block + i * 64, 64), 64)
+            gate_w[mine, :] = (
+                gate_w[mine, :].astype(F32) + first_recv[e, far, :].astype(F32)
+            ).astype(BF16)
+            own = gate_w[pl.ds(pl.multiple_of(e * block + i * 64, 64), 64), :].astype(F32)
+            down_w[here, pl.ds(e * hidden, hidden)] = (
+                own + first_recv[e, here, :].astype(F32)
+            ).astype(BF16)
+        return carry
+
+    first_gate.wait_recv()
+    first_up.wait_recv()
+    lax.fori_loop(0, block // 64, add_first, 0)
+    keep_sum = pltpu.make_async_copy(down_w.at[pl.ds(0, block)], gate_up_sum, local_sem.at[1])
+    for copy in (keep_sum, *keep_second):
+        copy.start()
 
     for d in (1, 2, 3):
         out_planes[d].wait_recv()
@@ -789,10 +820,12 @@
             copy.wait_send()
     finish_line()
     keep.wait()
-    for d in (1, 2):
-        near[d].wait()
     for slot in range(2):
         to_hbm(slot, down_terms.at[pl.ds(0, TILE)]).wait()
+    first_gate.wait_send()
+    first_up.wait_send()
+    for copy in (keep_sum, *keep_second):
+        copy.wait()
 
 
 def mlp_of(normed_two, mid, upstream, gain, upstream_group, w_gate, w_up, down_rows):
@@ -810,8 +843,8 @@
             jax.ShapeDtypeStruct((tok, width), F32),
             jax.ShapeDtypeStruct((1, width), F32),
             jax.ShapeDtypeStruct((2, 4, tok, width), BF16),
-            jax.ShapeDtypeStruct((4, 2 * TILE, 2 * hidden), BF16),
-            jax.ShapeDtypeStruct((2, 2 * TILE, 2 * hidden), BF16),
+            jax.ShapeDtypeStruct((2 * TILE, 2 * hidden), BF16),
+            jax.ShapeDtypeStruct((2, 2 * TILE, hidden), BF16),
             jax.ShapeDtypeStruct((hidden, width), BF16),
         ],
         scratch_shapes=[
@@ -829,12 +862,13 @@
             pltpu.VMEM((2, 4, tok, width), BF16),
             pltpu.VMEM((2, 3, tok, width), BF16),
             pltpu.VMEM((2, 3, tok, width), BF16),
+            pltpu.VMEM((2, 4 * TILE, hidden), BF16),
             pltpu.VMEM((tok, width), BF16),
             pltpu.VMEM((2, TILE, width), BF16),
             pltpu.SemaphoreType.DMA((5,)),
             pltpu.SemaphoreType.DMA((2,)),
-            pltpu.SemaphoreType.DMA((36,)),
-            pltpu.SemaphoreType.DMA((36,)),
+            pltpu.SemaphoreType.DMA((38,)),
+            pltpu.SemaphoreType.DMA((38,)),
         ],
         compiler_params=pltpu.CompilerParams(
             collective_id=1, has_side_effects=True, vmem_limit_bytes=60 << 20
@@ -870,16 +904,19 @@
     upstream_hbm,
     second_ref,
     mid_ref,
-    normed_ref,
+    normed_hbm,
     query_ref,
     kv_ref,
     attended_ref,
     log_total_ref,
-    w_head,
+    head_hbm,
     w_sibling,
-    out_pair,
+    out_hbm_rows,
     down_rows,
     upstream_all,
+    normed_ref,
+    w_head,
+    out_pair,
     inputs_all,
     w_parts,
     attended_other,
@@ -1035,14 +1072,15 @@
         norm(1, d)
     step_head(3, pass_head)
 
+    start_out(0)
     down_z = {
         d: send(16 + d, down_block(flip(plane, d)), down_place(plane), over_z[d]) for d in others
     }
-    start_out(0)
+    keep_normed = local(2, normed_ref, normed_hbm)
+    keep_normed.start()
     local(6, mine, head_rows).wait()
     for d in others:
         remote(9 + d, mine, head_rows, over_chips[d]).wait_recv()
-    head_pair = send(16, w_head, w_sibling, sibling)
 
     def project(which, target, flat):
         def step(t, carry):
@@ -1057,6 +1095,14 @@
 
         lax.fori_loop(0, seq // TILE, step, 0)
 
+    keep_out.wait()
+
+    def pass_out(source):
+        columns = out_pair.at[0, :, at(source, shard)]
+        remote(23 + source, columns, out_pair.at[1, :, at(source, shard)], sibling).start()
+
+    pass_out(plane)
+    step_out(1, pass_out)
     mine_kv = kv_ref.at[core]
     project(1, mine_kv, True)
     kv_pair = [
@@ -1065,7 +1111,16 @@
         for e in range(2)
     ]
     project(0, query_ref, False)
-    step_out(1)
+    step_out(2, pass_out)
+    head_pair = send(16, w_head, w_sibling, sibling)
+    keep_head = local(6, w_head, head_hbm)
+    keep_head.start()
+    down_chips = {}
+    for d in others:
+        down_z[d].wait_recv()
+        block = down_place(flip(plane, d))
+        for e in others:
+            down_chips[e, d] = send(51 + 3 * e + d, block, block, over_chips[e])
     for copy in kv_pair:
         copy.wait_recv()
 
@@ -1084,20 +1139,14 @@
 
     lax.fori_loop(0, seq // TILE, attend_step, 0)
     attended_pair = send(22, attended_ref.at[pl.ds(half_seq, half_seq)], attended_other, sibling)
-    step_out(2)
-    for d in others:
-        down_z[d].wait_recv()
-    down_chips = {}
-    for e in others:
-        for d in others:
-            block = down_place(flip(plane, d))
-            down_chips[e, d] = send(51 + 3 * e + d, block, block, over_chips[e])
-    step_out(3)
+    step_out(3, pass_out)
     start_up(0)
-    keep_out.wait()
-    out_sibling = send(23, out_pair.at[0], out_pair.at[1], sibling)
+    for d in range(4):
+        columns = out_pair.at[1, :, pl.ds(d * shard, shard)]
+        remote(23 + d, columns, columns, sibling).wait_recv()
+    keep_rows = local(3, out_pair.at[0], out_hbm_rows)
+    keep_rows.start()
     attended_pair.wait_recv()
-    out_sibling.wait_recv()
 
     def out_step(t, carry):
         here = at(t, TILE)
@@ -1111,7 +1160,7 @@
 
     lax.fori_loop(0, width // TILE, out_step, 0)
     branch = {
-        d: send(23 + d, chip_send.at[d - 1], chip_recv.at[d - 1], over_chips[d]) for d in others
+        d: send(26 + d, chip_send.at[d - 1], chip_recv.at[d - 1], over_chips[d]) for d in others
     }
 
     upstream_pair = {0: send(33, upstream_hbm, upstream_all.at[0, 1], sibling)}
@@ -1145,8 +1194,13 @@
         upstream_pair[d].wait_send()
         input_pairs[d].wait_send()
     head_pair.wait_recv()
-    for copy in (head_pair, attended_pair, out_sibling, *kv_pair):
+    for copy in (head_pair, attended_pair, *kv_pair):
         copy.wait_send()
+    for copy in (keep_normed, keep_head, keep_rows):
+        copy.wait()
+    for d in range(4):
+        columns = out_pair.at[0, :, pl.ds(d * shard, shard)]
+        remote(23 + d, columns, columns, sibling).wait_send()
     keep_down.wait()
     for d in others:
         for e in others:
@@ -1171,7 +1225,7 @@
     return pl.pallas_call(
         front_kernel,
         in_specs=[vmem] * 8 + [hbm] * 6,
-        out_specs=[vmem] * 8 + [hbm] + [vmem] + [hbm] * 2,
+        out_specs=[vmem] * 2 + [hbm] + [vmem] * 4 + [hbm] * 5,
         out_shape=[
             jax.ShapeDtypeStruct((tok, width), BF16),
             jax.ShapeDtypeStruct((tok, width), F32),
@@ -1182,11 +1236,14 @@
             jax.ShapeDtypeStruct((seq, 1), F32),
             jax.ShapeDtypeStruct((2, width, HD), BF16),
             jax.ShapeDtypeStruct((2, width, HD), BF16),
-            jax.ShapeDtypeStruct((2, HD, width), BF16),
+            jax.ShapeDtypeStruct((HD, width), BF16),
             jax.ShapeDtypeStruct((hidden, width), BF16),
             jax.ShapeDtypeStruct((4, 2, tok, width), BF16),
         ],
         scratch_shapes=[
+            pltpu.VMEM((seq, width), BF16),
+            pltpu.VMEM((2, width, HD), BF16),
+            pltpu.VMEM((2, HD, width), BF16),
             pltpu.VMEM((2, 4, tok, width), BF16),
             pltpu.VMEM((4, 2, width // 4, HD), BF16),
             pltpu.VMEM((4 * tok, HD), BF16),
@@ -1221,17 +1278,17 @@
     code_ref,
     low_code_ref,
     key_code_ref,
-    normed_ref,
     query_ref,
     kv_ref,
     attended_ref,
     log_total_ref,
-    w_head,
-    w_sibling,
-    out_rows_ref,
+    normed_hbm,
+    head_hbm,
+    sibling_hbm,
+    out_rows_hbm,
     branch_hbm,
-    gate_up_terms,
-    gate_up_near,
+    gate_up_hbm,
+    gate_up_send,
     down_terms,
     grad_input_ref,
     gain_total_ref,
@@ -1239,6 +1296,10 @@
     head_in,
     gate_up_in,
     down_in,
+    normed_ref,
+    w_head,
+    w_sibling,
+    out_rows_ref,
     branch_all,
     d_attended,
     d_head,
@@ -1252,8 +1313,8 @@
     own_sum,
     chip_send,
     chip_recv,
-    gate_up_parts,
     gate_up_sum,
+    gate_up_recv,
     down_parts,
     down_sum,
     down_planes,
@@ -1301,9 +1362,12 @@
 
     loads = [
         local(0, branch_hbm, branch_all),
-        local(1, gate_up_terms.at[0], gate_up_parts.at[0]),
-        local(2, gate_up_near, gate_up_parts.at[pl.ds(1, 2)]),
+        local(1, out_rows_hbm, out_rows_ref),
+        local(2, normed_hbm, normed_ref),
         local(3, down_terms.at[:, chip], down_parts.at[0]),
+        local(4, head_hbm, w_head),
+        local(5, sibling_hbm, w_sibling),
+        local(6, gate_up_hbm, gate_up_sum),
     ]
     for load in loads:
         load.start()
@@ -1316,7 +1380,6 @@
         pl.semaphore_signal(barrier, inc=1, device_id=partner, device_id_type=MESH)
     pl.semaphore_wait(barrier, len(partners))
 
-    gate_up_far = send(0, gate_up_terms.at[3], gate_up_parts.at[3], over_chips[3])
     down_chips = {
         d: send(d, down_terms.at[:, flip(chip, d)], down_parts.at[d], over_chips[d])
         for d in others
@@ -1334,6 +1397,8 @@
     out_z = {
         d: send(3 + d, out_send.at[flip(plane, d)], out_recv.at[d - 1], over_z[d]) for d in others
     }
+
+    loads[1].wait()
 
     def attended_step(t, carry):
         here = at(t, TILE)
@@ -1386,6 +1451,8 @@
     lax.fori_loop(0, seq // TILE, kv_step, 0)
     head_pair = send(9, d_head.at[pl.ds(half_seq, half_seq)], d_other, sibling)
 
+    loads[2].wait()
+
     def head_step(t, carry):
         made = dot_tn(normed_ref[:, at(t, TILE)], d_head[...])
         head_terms[:, t] = made.reshape(4, share, 2 * HD).astype(BF16)
@@ -1397,6 +1464,8 @@
         for d in others
     }
 
+    loads[4].wait()
+    loads[5].wait()
     head_pair.wait_recv()
 
     def normed_step(t, carry):
@@ -1429,39 +1498,10 @@
         return carry
 
     lax.fori_loop(0, 4, down_step, 0)
-    down_z = {
-        d: send(15 + d, down_sum.at[flip(plane, d)], down_planes.at[plane], over_z[d])
-        for d in others
-    }
-    keep_down = local(3, down_sum.at[plane], down_planes.at[plane])
-    keep_down.start()
-
-    loads[1].wait()
-    loads[2].wait()
-    gate_up_far.wait_recv()
-
-    def gate_up_step(i, carry):
-        here = at(i, share)
-        total = gate_up_parts[0, here, :].astype(F32)
-        for d in others:
-            total = total + gate_up_parts[d, here, :].astype(F32)
-        gate_up_sum[i // 4, i % 4] = total.astype(BF16)
-        return carry
-
-    lax.fori_loop(0, 8, gate_up_step, 0)
-    place = gate_up_in.at[plane, core]
-    gate_up_z = {
-        d: send(18 + d, gate_up_sum.at[core, flip(plane, d)], place, over_z[d]) for d in others
-    }
-    gate_up_cross = {
-        d: send(22 + d, gate_up_sum.at[other_core, flip(plane, d)], place, over_z_cross[d])
-        for d in range(4)
-    }
-    keep_gate_up = local(1, gate_up_sum.at[core, plane], place)
-    keep_gate_up.start()
-
     for d in others:
         normed_chips[d].wait_recv()
+    gate_second = send(0, gate_up_send.at[0], gate_up_recv.at[0], over_chips[2])
+    up_second = send(46, gate_up_send.at[1], gate_up_recv.at[1], over_chips[1])
     chunk = 32
     gain = attn_gain_ref[...]
 
@@ -1487,14 +1527,14 @@
     gains_planes = {d: send(25 + d, gains, gains_z.at[d - 1], over_z[d]) for d in others}
 
     for d in others:
-        out_z[d].wait_recv()
-    total = out_send[plane].astype(F32)
-    for d in range(3):
-        total = total + out_recv[d].astype(F32)
-    grad_out_ref[...] = total
-
-    for d in others:
         head_z[d].wait_recv()
+    down_z = {
+        d: send(15 + d, down_sum.at[flip(plane, d)], down_planes.at[plane], over_z[d])
+        for d in others
+    }
+    keep_down = local(3, down_sum.at[plane], down_planes.at[plane])
+    keep_down.start()
+
 
     def head_sum(i, carry):
         total = head_terms[plane, i].astype(F32)
@@ -1530,6 +1570,43 @@
         d: send(39 + d, gains, gains_ctx.at[1, d], over_chips_cross[d]) for d in range(4)
     }
 
+    loads[6].wait()
+    gate_second.wait_recv()
+    up_second.wait_recv()
+    hidden = gate_up_recv.shape[2]
+
+    def gate_up_step(i, carry):
+        here = at(i, share)
+        for e in range(2):
+            columns = pl.ds(e * hidden, hidden)
+            gate_up_sum[here, columns] = (
+                gate_up_sum[here, columns].astype(F32) + gate_up_recv[e, here, :].astype(F32)
+            ).astype(BF16)
+        return carry
+
+    lax.fori_loop(0, 8, gate_up_step, 0)
+
+    place = gate_up_in.at[plane, core]
+
+    def gate_up_rows(to_core, to_plane):
+        return gate_up_sum.at[at(4 * to_core + to_plane, share), :]
+
+    gate_up_z = {
+        d: send(18 + d, gate_up_rows(core, flip(plane, d)), place, over_z[d]) for d in others
+    }
+    gate_up_cross = {
+        d: send(22 + d, gate_up_rows(other_core, flip(plane, d)), place, over_z_cross[d])
+        for d in range(4)
+    }
+    keep_gate_up = local(1, gate_up_rows(core, plane), place)
+    keep_gate_up.start()
+    for d in others:
+        out_z[d].wait_recv()
+    total = out_send[plane].astype(F32)
+    for d in range(3):
+        total = total + out_recv[d].astype(F32)
+    grad_out_ref[...] = total
+
     keep_down.wait()
     down_place = down_in.at[chip]
     for d in range(4):
@@ -1571,21 +1648,21 @@
         for copies in (gate_up_cross, head_cross):
             copies[d].wait()
         gains_cross[d].wait_send()
-    for copy in (gate_up_far, head_pair, *kv_pair):
+    for copy in (gate_second, up_second, head_pair, *kv_pair):
         copy.wait_send()
 
 
 def back_of(*operands):
-    inputs, query, out_rows = operands[0], operands[10], operands[16]
+    inputs, query = operands[0], operands[9]
     tok, width = inputs.shape
     seq = query.shape[0]
-    hidden = operands[20].shape[0] * operands[20].shape[1] * operands[20].shape[2]
+    hidden = operands[18].shape[-1] // 2
     share = HD // 4
     vmem = pl.BlockSpec(memory_space=pltpu.VMEM)
     hbm = pl.BlockSpec(memory_space=pl.ANY)
     return pl.pallas_call(
         back_kernel,
-        in_specs=[vmem] * 17 + [hbm] * 4,
+        in_specs=[vmem] * 13 + [hbm] * 8,
         out_specs=[vmem] * 6,
         out_shape=[
             jax.ShapeDtypeStruct((tok, width), BF16),
@@ -1596,6 +1673,10 @@
             jax.ShapeDtypeStruct((4, share, width), BF16),
         ],
         scratch_shapes=[
+            pltpu.VMEM((seq, width), BF16),
+            pltpu.VMEM((2, width, HD), BF16),
+            pltpu.VMEM((2, width, HD), BF16),
+            pltpu.VMEM((HD, width), BF16),
             pltpu.VMEM((seq, width), BF16),
             pltpu.VMEM((seq, HD), BF16),
             pltpu.VMEM((seq, 2 * HD), BF16),
@@ -1609,17 +1690,17 @@
             pltpu.VMEM((tok, width), F32),
             pltpu.VMEM((3, tok, width), BF16),
             pltpu.VMEM((3, tok, width), BF16),
-            pltpu.VMEM((4, 2 * TILE, 2 * hidden), BF16),
-            pltpu.VMEM((2, 4, share, 2 * hidden), BF16),
+            pltpu.VMEM((8 * share, 2 * hidden), BF16),
+            pltpu.VMEM((2, 8 * share, hidden), BF16),
             pltpu.VMEM((4, 4, share, width), BF16),
             pltpu.VMEM((4, share, width), BF16),
             pltpu.VMEM((4, share, width), BF16),
             pltpu.VMEM((8, width), F32),
             pltpu.VMEM((3, 8, width), F32),
             pltpu.VMEM((2, 4, 8, width), F32),
-            pltpu.SemaphoreType.DMA((5,)),
-            pltpu.SemaphoreType.DMA((46,)),
-            pltpu.SemaphoreType.DMA((46,)),
+            pltpu.SemaphoreType.DMA((7,)),
+            pltpu.SemaphoreType.DMA((47,)),
+            pltpu.SemaphoreType.DMA((47,)),
         ],
         compiler_params=pltpu.CompilerParams(
             collective_id=3, has_side_effects=True, vmem_limit_bytes=60 << 20
@@ -1688,7 +1769,7 @@
         log_total,
         w_head,
         w_sibling,
-        out_pair,
+        out_rows,
         down_rows,
         upstream_group,
     ) = front_of(
@@ -1707,7 +1788,15 @@
         w_down,
         upstream_low,
     )
-    output, mid_grad, mlp_gain_grad, branch_all, gate_up_terms, gate_up_near, down_terms = mlp_of(
+    (
+        output,
+        mid_grad,
+        mlp_gain_grad,
+        branch_all,
+        gate_up_sum,
+        gate_up_send,
+        down_terms,
+    ) = mlp_of(
         normed_two,
         mid,
         upstream_low,
@@ -1727,17 +1816,17 @@
         code_column,
         low_column,
         code_row,
-        normed_all,
         query,
         key_value,
         attended,
         log_total,
+        normed_all,
         w_head,
         w_sibling,
-        out_pair[0],
+        out_rows,
         branch_all.reshape(seq_rows, width),
-        gate_up_terms,
-        gate_up_near,
+        gate_up_sum,
+        gate_up_send,
         down_terms.reshape(planes, chips, -1, width),
     )
     hidden = gate_up_in.shape[-1] // 2

time: 510 us -> 459 us (0.900)
  Pallas kernels: 490 us -> 437 us
    pallas_call x1, Pallas kernels: 194 us -> 147 us  [back_of(): pl.pallas_call(back_kernel, in_specs=[vmem] * 13 + [hbm] * 8, out_specs=[...]
    pallas_call x1, Pallas kernels: 150 us -> 135 us  [front_of(): pl.pallas_call(front_kernel, in_specs=[vmem] * 8 + [hbm] * 6, out_specs=[...]
    pallas_call x1, Pallas kernels: 146 us -> 155 us  [mlp_of(): pl.pallas_call(mlp_kernel, in_specs=[vmem] * 4 + [hbm] * 4, out_specs=[vm...]
where the time goes in v6:
time: 459 us; the launch traced here: 455 us
  Pallas kernels  437 us (95%)
  other arithmetic  10.6 us (2%)
  local copies, waits for them, and re-layouts  6.45 us (1%)
    pallas_call x1, Pallas kernels, mlp_of(): pl.pallas_call(mlp_kernel, in_specs=[vmem] * 4 + [hbm] * 4, out_specs=[vm...  155 us
    pallas_call x1, Pallas kernels, back_of(): pl.pallas_call(back_kernel, in_specs=[vmem] * 13 + [hbm] * 8, out_specs=[...  147 us
    pallas_call x1, Pallas kernels, front_of(): pl.pallas_call(front_kernel, in_specs=[vmem] * 8 + [hbm] * 6, out_specs=[...  135 us

profile of v6, /device:TPU:0, one launch (start us, length us, event | category | flops | bytes accessed | tf_op | source)
XLA Modules:
  0.0 455.3 jit_solution(17764335928796710245)
XLA Ops:
  0.7 0.1 stack.35
  0.8 0.8 select_reduce_fusion
  1.6 0.9 convert_reduce_fusion.1
  2.5 0.1 iota_add_fusion
  2.6 0.1 convert_reduce_fusion
  2.7 0.6 add.137.key_code_ref
  3.3 0.2 copy.32
  3.5 0.2 copy.31
  3.8 0.9 max.10.low_code_ref
  4.6 1.0 copy.33.code_ref
  5.6 3.0 multiply_sine_fusion
  8.7 135.3 %shard_map.212 = (bf16[128,2048]{1,0:T(8,128)(2,1)}, f32[128,2048]{1,0:T(8,128)}, bf16[1024,2048]{1,0:T(8,128)(2,1)}, bf16[1024,256]{1,0:T(8,128)(2,1)}, bf16[2,...) custom-call(bf16[128,2048]{1,0:T(8,128)(2,1)} %bitcast.148, ...), custom_call_target="tpu_custom_call" | custom-call | flops 4294967296 | bytes 41943040 | tf_op jit(solution)/shard_map/pallas_call | solution.py:1225
  144.0 154.8 %shard_map.213 = (bf16[128,2048]{1,0:T(8,128)(2,1)}, f32[128,2048]{1,0:T(8,128)}, f32[1,2048]{1,0:T(1,128)}, bf16[2,4,128,2048]{3,2,1,0:T(8,128)(2,1)}, bf16[512...) custom-call(bf16[128,2048]{1,0:T(8,128)(2,1)} %get-tuple-element.36.second_ref, ...), custom_call_target="tpu_custom_call" | custom-call | flops 38654705664 | bytes 37748736 | tf_op jit(solution)/shard_map/pallas_call | solution.py:837
  298.8 147.2 %shard_map.214 = (bf16[128,2048]{1,0:T(8,128)(2,1)}, f32[8,2048]{1,0:T(8,128)}, f32[64,2048]{1,0:T(8,128)}, bf16[8,64,512]{2,1,0:T(8,128)(2,1)}, bf16[4,2,64,204...) custom-call(bf16[128,2048]{1,0:T(8,128)(2,1)} %bitcast.149, f32[128,2048]{1,0:T(8,128)} %get-tuple-element.41.mid_grad_ref, ...), custom_call_target="tpu_custom_call" | custom-call | flops 9126805504 | bytes 41943040 | tf_op jit(solution)/shard_map/pallas_call | solution.py:1663
  446.0 0.8 constant_dynamic-slice_fusion
  446.7 0.5 slice_bitcast_fusion.32
  447.2 0.0 copy-start.1
  447.2 1.2 convert_element_type.23
  448.6 0.0 copy-start.7
  448.7 0.0 copy-start
  448.7 0.8 pad_maximum_fusion
  449.5 0.0 copy-done.1
  449.5 1.6 bitcast_convert_fusion
  451.2 0.0 copy-done.7
  451.2 0.0 copy-done
  451.2 0.5 convert_element_type.24
  451.9 0.0 copy-start.2
  451.9 0.0 copy-start.4
  452.0 0.0 copy-start.3
  452.1 0.0 copy-start.5
  452.1 0.0 copy-start.6
  452.1 0.8 copy-done.2
  452.9 0.8 copy.59
  453.7 0.0 copy-done.4
  453.7 0.8 copy.60
  454.5 0.0 copy-done.3
  454.5 0.8 copy.61
  455.3 0.0 copy-done.5
  455.3 0.0 copy-done.6
  (23 shorter events, 0.4 us)
Async XLA Ops:
  447.2 2.3 copy-start.1
  448.6 2.6 copy-start.7
  448.7 2.5 copy-start
  451.9 1.0 copy-start.2
  451.9 1.8 copy-start.4
  452.0 2.5 copy-start.3
  452.1 3.2 copy-start.5
  452.1 3.2 copy-start.6

commit v7 on v6

--- a/solution.py
+++ b/solution.py
@@ -524,6 +524,55 @@
                     made().wait_send()
 
     return start, step, finish
+
+
+def line_sum(remote, over_z, plane, slot, own, recv, add):
+    is_end = jnp.logical_or(plane == 0, plane == 3)
+    is_inner = jnp.logical_and(plane > 0, plane < 3)
+
+    def near():
+        return remote(slot, own(1), recv.at[0], over_z[1])
+
+    def through(u):
+        return remote(slot + 1 + u, own(2 + u), recv.at[2 + u], over_z[1])
+
+    def far(u):
+        return remote(slot + 3 + u, own(3 - u), recv.at[1], over_z[3 - u], slot + 3)
+
+    def start():
+        @pl.when(is_end)
+        def _():
+            for u in range(2):
+                through(u).start()
+
+        near().start()
+
+    def pass_on():
+        @pl.when(is_inner)
+        def _():
+            for u in range(2):
+                through(u).wait_recv()
+                add(3 - u, 2 + u)
+                far(u).start()
+
+    def wait():
+        near().wait_recv()
+        far(0).wait_recv()
+
+    def finish():
+        near().wait_send()
+
+        @pl.when(is_end)
+        def _():
+            for u in range(2):
+                through(u).wait_send()
+
+        @pl.when(is_inner)
+        def _():
+            for u in range(2):
+                far(u).wait_send()
+
+    return start, pass_on, wait, finish
 
 
 def xor4(a, b):
@@ -665,7 +714,7 @@
         copy = remote(
             base + 3 + d, z_send.at[which, d - 1], z_recv.at[which, d - 1], over_z[d]
         )
-        if which == 0 or d == 1:
+        if which == 0:
             copy.start()
         return copy
 
@@ -715,13 +764,26 @@
             out_planes[d - 1] = give_plane(d - 1, 14, out_pairs[d - 1])
     out_planes[3] = give_plane(3, 14, out_pairs[3])
 
+    def add_out(d, i):
+        def step(t, carry):
+            at = pl.ds(pl.multiple_of(t * 32, 32), 32)
+            z_send[1, d - 1, at, :] = (
+                z_send[1, d - 1, at, :].astype(F32) + z_recv[1, i, at, :].astype(F32)
+            ).astype(BF16)
+            return carry
+
+        lax.fori_loop(0, tok // 32, step, 0)
+
+    start_sum, pass_sum, wait_sum, finish_sum = line_sum(
+        remote, over_z, plane, 38, lambda d: z_send.at[1, d - 1], z_recv.at[1], add_out
+    )
+    start_sum()
+
     terms(gate_grad, 2, gate_w, 2 * block)
     terms(up_grad, 1, gate_w, 3 * block)
 
     for d in (1, 2, 3):
         planes[d].wait_recv()
-    for d in (2, 3):
-        out_planes[d].start()
     chunk = 32
     gain = gain_ref[...]
 
@@ -744,7 +806,7 @@
 
     gain_grad_ref[...] = lax.fori_loop(0, tok // chunk, mid_step, jnp.zeros((1, width), F32))
     branch_chips = {
-        d: send(20 + d, branch_low, branch_all.at[0, d], over_chips[d]) for d in (1, 2, 3)
+        d: send(20 + d, branch_low, branch_all.at[0, d], over_chips[d]) for d in (1, 2)
     }
     branch_pairs = {0: send(24, branch_low, branch_all.at[1, 0], sibling)}
     keep = pltpu.make_async_copy(branch_low, branch_all.at[0, 0], local_sem.at[0])
@@ -766,9 +828,18 @@
         down_step(t)
     terms(gate_grad, 0, gate_w, 0)
     terms(up_grad, 0, gate_w, block)
-    for d in (1, 2, 3):
+    branch_far = {}
+    for d in (1, 2):
         branch_chips[d].wait_recv()
+        part = pl.ds((d - 1) * (tok // 2), tok // 2)
+        branch_far[d] = send(
+            23 + 20 * (d - 1), branch_all.at[0, d, part], branch_all.at[0, 3, part], over_chips[3 - d]
+        )
         branch_pairs[d] = send(24 + d, branch_all.at[0, d], branch_all.at[1, d], sibling)
+    pass_sum()
+    for d in (1, 2):
+        branch_far[d].wait_recv()
+    branch_pairs[3] = send(27, branch_all.at[0, 3], branch_all.at[1, 3], sibling)
 
     keep_second = [
         pltpu.make_async_copy(
@@ -798,13 +869,12 @@
     for copy in (keep_sum, *keep_second):
         copy.start()
 
-    for d in (1, 2, 3):
-        out_planes[d].wait_recv()
+    wait_sum()
 
     def out_step(i, carry):
         at = pl.ds(pl.multiple_of(i * chunk, chunk), chunk)
         total = mid_ref[at, :] + own_sum[1, at, :]
-        for d in range(3):
+        for d in range(2):
             total = total + z_recv[1, d, at, :].astype(F32)
         output_ref[at, :] = total.astype(BF16)
         return carry
@@ -816,8 +886,11 @@
         for copy in (gather_pair[d], pairs[d], out_pairs[d], branch_pairs[d]):
             copy.wait_send()
     for d in (1, 2, 3):
-        for copy in (planes[d], out_planes[d], branch_chips[d]):
-            copy.wait_send()
+        planes[d].wait_send()
+    for d in (1, 2):
+        branch_chips[d].wait_send()
+        branch_far[d].wait_send()
+    finish_sum()
     finish_line()
     keep.wait()
     for slot in range(2):
@@ -861,14 +934,14 @@
             pltpu.VMEM((2, 4, tok, width), BF16),
             pltpu.VMEM((2, 4, tok, width), BF16),
             pltpu.VMEM((2, 3, tok, width), BF16),
-            pltpu.VMEM((2, 3, tok, width), BF16),
+            pltpu.VMEM((2, 4, tok, width), BF16),
             pltpu.VMEM((2, 4 * TILE, hidden), BF16),
             pltpu.VMEM((tok, width), BF16),
             pltpu.VMEM((2, TILE, width), BF16),
             pltpu.SemaphoreType.DMA((5,)),
             pltpu.SemaphoreType.DMA((2,)),
-            pltpu.SemaphoreType.DMA((38,)),
-            pltpu.SemaphoreType.DMA((38,)),
+            pltpu.SemaphoreType.DMA((44,)),
+            pltpu.SemaphoreType.DMA((44,)),
         ],
         compiler_params=pltpu.CompilerParams(
             collective_id=1, has_side_effects=True, vmem_limit_bytes=60 << 20
@@ -1064,6 +1137,9 @@
     norm(0, 1)
     norm(0, 2)
     step_head(2, pass_head)
+    down_z = {
+        d: send(16 + d, down_block(flip(plane, d)), down_place(plane), over_z[d]) for d in others
+    }
     input_chips[3].wait_recv()
     input_pairs[3] = send(6, inputs_all.at[0, 3], inputs_all.at[1, 3], sibling)
     norm(0, 3)
@@ -1073,9 +1149,6 @@
     step_head(3, pass_head)
 
     start_out(0)
-    down_z = {
-        d: send(16 + d, down_block(flip(plane, d)), down_place(plane), over_z[d]) for d in others
-    }
     keep_normed = local(2, normed_ref, normed_hbm)
     keep_normed.start()
     local(6, mine, head_rows).wait()
@@ -1115,12 +1188,21 @@
     head_pair = send(16, w_head, w_sibling, sibling)
     keep_head = local(6, w_head, head_hbm)
     keep_head.start()
-    down_chips = {}
+    down_near, down_far = {}, {}
+    half_part = part // 2
+
+    def down_half(of_chip, column, second):
+        first = of_chip * part + second * half_part
+        return down_rows.at[
+            pl.ds(pl.multiple_of(first, half_part), half_part), at(column, shard)
+        ]
+
     for d in others:
         down_z[d].wait_recv()
         block = down_place(flip(plane, d))
-        for e in others:
-            down_chips[e, d] = send(51 + 3 * e + d, block, block, over_chips[e])
+        for e in (1, 2):
+            down_near[e, d] = send(51 + 3 * e + d, block, block, over_chips[e])
+    start_up(0)
     for copy in kv_pair:
         copy.wait_recv()
 
@@ -1140,7 +1222,6 @@
     lax.fori_loop(0, seq // TILE, attend_step, 0)
     attended_pair = send(22, attended_ref.at[pl.ds(half_seq, half_seq)], attended_other, sibling)
     step_out(3, pass_out)
-    start_up(0)
     for d in range(4):
         columns = out_pair.at[1, :, pl.ds(d * shard, shard)]
         remote(23 + d, columns, columns, sibling).wait_recv()
@@ -1163,6 +1244,12 @@
         d: send(26 + d, chip_send.at[d - 1], chip_recv.at[d - 1], over_chips[d]) for d in others
     }
 
+    for d in others:
+        column = flip(plane, d)
+        for e in (1, 2):
+            down_near[e, d].wait_recv()
+            block = down_half(flip(chip, e), column, e - 1)
+            down_far[e, d] = send(57 + 3 * e + d, block, block, over_chips[3 - e])
     upstream_pair = {0: send(33, upstream_hbm, upstream_all.at[0, 1], sibling)}
 
     def pass_up(d):
@@ -1203,8 +1290,9 @@
         remote(23 + d, columns, columns, sibling).wait_send()
     keep_down.wait()
     for d in others:
-        for e in others:
-            down_chips[e, d].wait()
+        for e in (1, 2):
+            down_near[e, d].wait_send()
+            down_far[e, d].wait()
         for copies in (input_chips, down_z, branch):
             copies[d].wait_send()
         remote(9 + d, mine, head_rows, over_chips[d]).wait_send()
@@ -1251,8 +1339,8 @@
             pltpu.VMEM((3, tok, width), BF16),
             pltpu.VMEM((3, tok, width), BF16),
             pltpu.SemaphoreType.DMA((7,)),
-            pltpu.SemaphoreType.DMA((64,)),
-            pltpu.SemaphoreType.DMA((64,)),
+            pltpu.SemaphoreType.DMA((67,)),
+            pltpu.SemaphoreType.DMA((67,)),
         ],
         compiler_params=pltpu.CompilerParams(
             collective_id=2, has_side_effects=True, vmem_limit_bytes=56 << 20
@@ -1316,6 +1404,9 @@
     gate_up_sum,
     gate_up_recv,
     down_parts,
+    down_first,
+    down_mid,
+    down_second,
     down_sum,
     down_planes,
     gains,
@@ -1342,12 +1433,12 @@
     def at(i, size):
         return pl.ds(pl.multiple_of(i * size, size), size)
 
-    def remote(slot, source, target, device):
+    def remote(slot, source, target, device, recv=None):
         return pltpu.make_async_remote_copy(
             src_ref=source,
             dst_ref=target,
             send_sem=send_sem.at[slot],
-            recv_sem=recv_sem.at[slot],
+            recv_sem=recv_sem.at[slot if recv is None else recv],
             device_id=device,
             device_id_type=MESH,
         )
@@ -1364,7 +1455,9 @@
         local(0, branch_hbm, branch_all),
         local(1, out_rows_hbm, out_rows_ref),
         local(2, normed_hbm, normed_ref),
-        local(3, down_terms.at[:, chip], down_parts.at[0]),
+        local(3, down_terms.at[:, chip], down_parts),
+        local(7, down_terms.at[:, flip(chip, 2), :, pl.ds(0, width // 2)], down_mid.at[0]),
+        local(8, down_terms.at[:, flip(chip, 1), :, pl.ds(width // 2, width // 2)], down_mid.at[1]),
         local(4, head_hbm, w_head),
         local(5, sibling_hbm, w_sibling),
         local(6, gate_up_hbm, gate_up_sum),
@@ -1380,10 +1473,20 @@
         pl.semaphore_signal(barrier, inc=1, device_id=partner, device_id_type=MESH)
     pl.semaphore_wait(barrier, len(partners))
 
-    down_chips = {
-        d: send(d, down_terms.at[:, flip(chip, d)], down_parts.at[d], over_chips[d])
-        for d in others
-    }
+    gate_second = send(0, gate_up_send.at[0], gate_up_recv.at[0], over_chips[2])
+    up_second = send(46, gate_up_send.at[1], gate_up_recv.at[1], over_chips[1])
+
+    half_width = width // 2
+    down_sent = [
+        send(
+            1 + 2 * e + u,
+            down_terms.at[:, flip(chip, (1 + e, 3)[u]), :, pl.ds(e * half_width, half_width)],
+            down_first.at[e, u],
+            over_chips[1 + e],
+        )
+        for e in range(2)
+        for u in range(2)
+    ]
 
     loads[0].wait()
 
@@ -1394,9 +1497,15 @@
         return carry
 
     lax.fori_loop(0, width // TILE, out_step, 0)
-    out_z = {
-        d: send(3 + d, out_send.at[flip(plane, d)], out_recv.at[d - 1], over_z[d]) for d in others
-    }
+
+    def add_out(d, i):
+        here = flip(plane, d)
+        out_send[here] = (out_send[here].astype(F32) + out_recv[i].astype(F32)).astype(BF16)
+
+    start_out, pass_out, wait_out, finish_out = line_sum(
+        remote, over_z, plane, 52, lambda d: out_send.at[flip(plane, d)], out_recv, add_out
+    )
+    start_out()
 
     loads[1].wait()
 
@@ -1436,6 +1545,36 @@
         )
         for e in range(2)
     ]
+    loads[8].wait()
+    gate_second.wait_recv()
+    up_second.wait_recv()
+    hidden = gate_up_recv.shape[2]
+
+    def gate_up_step(i, carry):
+        here = at(i, share)
+        for e in range(2):
+            columns = pl.ds(e * hidden, hidden)
+            gate_up_sum[here, columns] = (
+                gate_up_sum[here, columns].astype(F32) + gate_up_recv[e, here, :].astype(F32)
+            ).astype(BF16)
+        return carry
+
+    lax.fori_loop(0, 8, gate_up_step, 0)
+
+    place = gate_up_in.at[plane, core]
+
+    def gate_up_rows(to_core, to_plane):
+        return gate_up_sum.at[at(4 * to_core + to_plane, share), :]
+
+    gate_up_z = {
+        d: send(18 + d, gate_up_rows(core, flip(plane, d)), place, over_z[d]) for d in others
+    }
+    gate_up_cross = {
+        d: send(22 + d, gate_up_rows(other_core, flip(plane, d)), place, over_z_cross[d])
+        for d in range(4)
+    }
+    keep_gate_up = local(1, gate_up_rows(core, plane), place)
+    keep_gate_up.start()
     for copy in kv_pair:
         copy.wait_recv()
 
@@ -1459,13 +1598,25 @@
         return carry
 
     lax.fori_loop(0, width // TILE, head_step, 0)
-    head_z = {
-        d: send(9 + d, head_terms.at[flip(plane, d)], head_recv.at[d - 1], over_z[d])
-        for d in others
-    }
-
-    loads[4].wait()
-    loads[5].wait()
+
+    def add_head(d, i):
+        here = flip(plane, d)
+
+        def step(t, carry):
+            head_terms[here, t] = (
+                head_terms[here, t].astype(F32) + head_recv[i, t].astype(F32)
+            ).astype(BF16)
+            return carry
+
+        lax.fori_loop(0, 8, step, 0)
+
+    start_head, pass_head, wait_head, finish_head = line_sum(
+        remote, over_z, plane, 47, lambda d: head_terms.at[flip(plane, d)], head_recv, add_head
+    )
+    start_head()
+
+    loads[6].wait()
+    loads[7].wait()
     head_pair.wait_recv()
 
     def normed_step(t, carry):
@@ -1486,22 +1637,26 @@
         d: send(12 + d, chip_send.at[d - 1], chip_recv.at[d - 1], over_chips[d]) for d in others
     }
 
-    loads[3].wait()
-    for d in others:
-        down_chips[d].wait_recv()
-
-    def down_step(p, carry):
-        total = down_parts[0, p].astype(F32)
-        for d in others:
-            total = total + down_parts[d, p].astype(F32)
-        down_sum[p] = total.astype(BF16)
+    loads[4].wait()
+    loads[5].wait()
+
+    def down_mid_step(p, carry):
+        for e in range(2):
+            down_mid[e, p] = (
+                down_mid[e, p].astype(F32) + down_first[e, 1, p].astype(F32)
+            ).astype(BF16)
         return carry
 
-    lax.fori_loop(0, 4, down_step, 0)
+    for copy in down_sent:
+        copy.wait_recv()
+    lax.fori_loop(0, 4, down_mid_step, 0)
+    down_last = [
+        send(5 + e, down_mid.at[e], down_second.at[e], over_chips[2 - e]) for e in range(2)
+    ]
+    pass_out()
+    pass_head()
     for d in others:
         normed_chips[d].wait_recv()
-    gate_second = send(0, gate_up_send.at[0], gate_up_recv.at[0], over_chips[2])
-    up_second = send(46, gate_up_send.at[1], gate_up_recv.at[1], over_chips[1])
     chunk = 32
     gain = attn_gain_ref[...]
 
@@ -1522,12 +1677,25 @@
 
     gain_grad = lax.fori_loop(0, tok // chunk, input_step, jnp.zeros((1, width), F32))
     gains[...] = jnp.concatenate(
-        [gain_grad, mlp_gain_grad_ref[...], jnp.zeros((6, width), F32)], axis=0
+        [gain_grad, mlp_gain_grad_ref[...]], axis=0
     )
     gains_planes = {d: send(25 + d, gains, gains_z.at[d - 1], over_z[d]) for d in others}
 
-    for d in others:
-        head_z[d].wait_recv()
+    loads[3].wait()
+    for copy in down_last:
+        copy.wait_recv()
+
+    def down_step(p, carry):
+        for e in range(2):
+            columns = pl.ds(e * half_width, half_width)
+            down_sum[p, :, columns] = (
+                down_parts[p, :, columns].astype(F32)
+                + down_first[e, 0, p].astype(F32)
+                + down_second[e, p].astype(F32)
+            ).astype(BF16)
+        return carry
+
+    lax.fori_loop(0, 4, down_step, 0)
     down_z = {
         d: send(15 + d, down_sum.at[flip(plane, d)], down_planes.at[plane], over_z[d])
         for d in others
@@ -1536,9 +1704,10 @@
     keep_down.start()
 
 
+    wait_head()
     def head_sum(i, carry):
         total = head_terms[plane, i].astype(F32)
-        for d in range(3):
+        for d in range(2):
             total = total + head_recv[d, i].astype(F32)
         head_terms[plane, i] = total.astype(BF16)
         return carry
@@ -1570,40 +1739,9 @@
         d: send(39 + d, gains, gains_ctx.at[1, d], over_chips_cross[d]) for d in range(4)
     }
 
-    loads[6].wait()
-    gate_second.wait_recv()
-    up_second.wait_recv()
-    hidden = gate_up_recv.shape[2]
-
-    def gate_up_step(i, carry):
-        here = at(i, share)
-        for e in range(2):
-            columns = pl.ds(e * hidden, hidden)
-            gate_up_sum[here, columns] = (
-                gate_up_sum[here, columns].astype(F32) + gate_up_recv[e, here, :].astype(F32)
-            ).astype(BF16)
-        return carry
-
-    lax.fori_loop(0, 8, gate_up_step, 0)
-
-    place = gate_up_in.at[plane, core]
-
-    def gate_up_rows(to_core, to_plane):
-        return gate_up_sum.at[at(4 * to_core + to_plane, share), :]
-
-    gate_up_z = {
-        d: send(18 + d, gate_up_rows(core, flip(plane, d)), place, over_z[d]) for d in others
-    }
-    gate_up_cross = {
-        d: send(22 + d, gate_up_rows(other_core, flip(plane, d)), place, over_z_cross[d])
-        for d in range(4)
-    }
-    keep_gate_up = local(1, gate_up_rows(core, plane), place)
-    keep_gate_up.start()
-    for d in others:
-        out_z[d].wait_recv()
+    wait_out()
     total = out_send[plane].astype(F32)
-    for d in range(3):
+    for d in range(2):
         total = total + out_recv[d].astype(F32)
     grad_out_ref[...] = total
 
@@ -1641,14 +1779,16 @@
         gate_up_z[d].wait_recv()
         head_chips[d].wait_recv()
         for copies in (
-            down_chips, out_z, head_z, normed_chips, down_z, gate_up_z, head_chips, gains_chips
+            normed_chips, down_z, gate_up_z, head_chips, gains_chips
         ):
             copies[d].wait_send()
+    finish_out()
+    finish_head()
     for d in range(4):
         for copies in (gate_up_cross, head_cross):
             copies[d].wait()
         gains_cross[d].wait_send()
-    for copy in (gate_second, up_second, head_pair, *kv_pair):
+    for copy in (gate_second, up_second, head_pair, *kv_pair, *down_sent, *down_last):
         copy.wait_send()
 
 
@@ -1666,7 +1806,7 @@
         out_specs=[vmem] * 6,
         out_shape=[
             jax.ShapeDtypeStruct((tok, width), BF16),
-            jax.ShapeDtypeStruct((8, width), F32),
+            jax.ShapeDtypeStruct((2, width), F32),
             jax.ShapeDtypeStruct((share, width), F32),
             jax.ShapeDtypeStruct((8, share, 2 * HD), BF16),
             jax.ShapeDtypeStruct((4, 2, share, 2 * hidden), BF16),
@@ -1684,23 +1824,26 @@
             pltpu.VMEM((2, seq, HD), F32),
             pltpu.VMEM((seq, HD), F32),
             pltpu.VMEM((4, share, width), BF16),
-            pltpu.VMEM((3, share, width), BF16),
+            pltpu.VMEM((4, share, width), BF16),
             pltpu.VMEM((4, 8, share, 2 * HD), BF16),
-            pltpu.VMEM((3, 8, share, 2 * HD), BF16),
+            pltpu.VMEM((4, 8, share, 2 * HD), BF16),
             pltpu.VMEM((tok, width), F32),
             pltpu.VMEM((3, tok, width), BF16),
             pltpu.VMEM((3, tok, width), BF16),
             pltpu.VMEM((8 * share, 2 * hidden), BF16),
             pltpu.VMEM((2, 8 * share, hidden), BF16),
-            pltpu.VMEM((4, 4, share, width), BF16),
+            pltpu.VMEM((4, share, width), BF16),
+            pltpu.VMEM((2, 2, 4, share, width // 2), BF16),
+            pltpu.VMEM((2, 4, share, width // 2), BF16),
+            pltpu.VMEM((2, 4, share, width // 2), BF16),
             pltpu.VMEM((4, share, width), BF16),
             pltpu.VMEM((4, share, width), BF16),
-            pltpu.VMEM((8, width), F32),
-            pltpu.VMEM((3, 8, width), F32),
-            pltpu.VMEM((2, 4, 8, width), F32),
-            pltpu.SemaphoreType.DMA((7,)),
-            pltpu.SemaphoreType.DMA((47,)),
-            pltpu.SemaphoreType.DMA((47,)),
+            pltpu.VMEM((2, width), F32),
+            pltpu.VMEM((3, 2, width), F32),
+            pltpu.VMEM((2, 4, 2, width), F32),
+            pltpu.SemaphoreType.DMA((9,)),
+            pltpu.SemaphoreType.DMA((57,)),
+            pltpu.SemaphoreType.DMA((57,)),
         ],
         compiler_params=pltpu.CompilerParams(
             collective_id=3, has_side_effects=True, vmem_limit_bytes=60 << 20

time: 459 us -> 430 us (0.937)
  Pallas kernels: 437 us -> 409 us
    pallas_call x1, Pallas kernels: 155 us -> 141 us  [mlp_of(): pl.pallas_call(mlp_kernel, in_specs=[vmem] * 4 + [hbm] * 4, out_specs=[vm...]
    pallas_call x1, Pallas kernels: 135 us -> 124 us  [front_of(): pl.pallas_call(front_kernel, in_specs=[vmem] * 8 + [hbm] * 6, out_specs=[...]
where the time goes in v7:
time: 430 us; the launch traced here: 427 us
  Pallas kernels  409 us (95%)
  other arithmetic  10.6 us (2%)
  local copies, waits for them, and re-layouts  6.44 us (1%)
    pallas_call x1, Pallas kernels, back_of(): pl.pallas_call(back_kernel, in_specs=[vmem] * 13 + [hbm] * 8, out_specs=[...  145 us
    pallas_call x1, Pallas kernels, mlp_of(): pl.pallas_call(mlp_kernel, in_specs=[vmem] * 4 + [hbm] * 4, out_specs=[vm...  141 us
    pallas_call x1, Pallas kernels, front_of(): pl.pallas_call(front_kernel, in_specs=[vmem] * 8 + [hbm] * 6, out_specs=[...  124 us

profile of v7, /device:TPU:0, one launch (start us, length us, event | category | flops | bytes accessed | tf_op | source)
XLA Modules:
  0.0 427.0 jit_solution(4707829544520199870)
XLA Ops:
  0.7 0.1 stack.35
  0.8 0.8 select_reduce_fusion
  1.6 0.9 convert_reduce_fusion.1
  2.5 0.1 iota_add_fusion
  2.6 0.1 convert_reduce_fusion
  2.7 0.6 add.137.key_code_ref
  3.3 0.2 copy.32
  3.5 0.2 copy.31
  3.8 0.9 max.10.low_code_ref
  4.6 1.0 copy.33.code_ref
  5.6 3.0 multiply_sine_fusion
  8.7 123.7 %shard_map.212 = (bf16[128,2048]{1,0:T(8,128)(2,1)}, f32[128,2048]{1,0:T(8,128)}, bf16[1024,2048]{1,0:T(8,128)(2,1)}, bf16[1024,256]{1,0:T(8,128)(2,1)}, bf16[2,...) custom-call(bf16[128,2048]{1,0:T(8,128)(2,1)} %bitcast.148, ...), custom_call_target="tpu_custom_call" | custom-call | flops 4294967296 | bytes 41943040 | tf_op jit(solution)/shard_map/pallas_call | solution.py:1313
  132.4 140.7 %shard_map.213 = (bf16[128,2048]{1,0:T(8,128)(2,1)}, f32[128,2048]{1,0:T(8,128)}, f32[1,2048]{1,0:T(1,128)}, bf16[2,4,128,2048]{3,2,1,0:T(8,128)(2,1)}, bf16[512...) custom-call(bf16[128,2048]{1,0:T(8,128)(2,1)} %get-tuple-element.36.second_ref, ...), custom_call_target="tpu_custom_call" | custom-call | flops 38654705664 | bytes 37748736 | tf_op jit(solution)/shard_map/pallas_call | solution.py:910
  273.1 144.5 %shard_map.214 = (bf16[128,2048]{1,0:T(8,128)(2,1)}, f32[2,2048]{1,0:T(2,128)}, f32[64,2048]{1,0:T(8,128)}, bf16[8,64,512]{2,1,0:T(8,128)(2,1)}, bf16[4,2,64,204...) custom-call(bf16[128,2048]{1,0:T(8,128)(2,1)} %bitcast.149, f32[128,2048]{1,0:T(8,128)} %get-tuple-element.41.mid_grad_ref, ...), custom_call_target="tpu_custom_call" | custom-call | flops 9126805504 | bytes 41943040 | tf_op jit(solution)/shard_map/pallas_call | solution.py:1803
  417.6 0.7 constant_dynamic-slice_fusion
  418.4 0.5 slice_bitcast_fusion.32
  418.9 0.0 copy-start.1
  418.9 1.2 convert_element_type.23
  420.3 0.0 copy-start.7
  420.3 0.0 copy-start
  420.3 0.8 pad_maximum_fusion
  421.2 0.0 copy-done.1
  421.2 1.6 bitcast_convert_fusion
  422.8 0.0 copy-done.7
  422.8 0.0 copy-done
  422.8 0.5 convert_element_type.24
  423.5 0.0 copy-start.2
  423.6 0.0 copy-start.4
  423.6 0.0 copy-start.3
  423.7 0.0 copy-start.5
  423.8 0.0 copy-start.6
  423.8 0.8 copy-done.2
  424.6 0.8 copy.59
  425.4 0.0 copy-done.4
  425.4 0.8 copy.60
  426.2 0.0 copy-done.3
  426.2 0.8 copy.61
  427.0 0.0 copy-done.5
  427.0 0.0 copy-done.6
  (23 shorter events, 0.4 us)
Async XLA Ops:
  418.9 2.3 copy-start.1
  420.3 2.6 copy-start.7
  420.3 2.5 copy-start
  423.5 1.0 copy-start.2
  423.6 1.8 copy-start.4
  423.6 2.5 copy-start.3
  423.7 3.2 copy-start.5
  423.8 3.2 copy-start.6

commit v8 on v7

--- a/solution.py
+++ b/solution.py
@@ -700,12 +700,25 @@
             pair_send[which, d, :, at] = terms[tok:].astype(BF16)
             return carry
 
-        lax.fori_loop(0, width // WIDE, step, 0)
-        return send(base + d, pair_send.at[which, d], pair_recv.at[which, d], sibling)
-
-    def give_plane(d, base, copy):
+        copies = []
+        half_width = width // 2
+        for h in range(2):
+            lax.fori_loop(h * half_width // WIDE, (h + 1) * half_width // WIDE, step, 0)
+            columns = pl.ds(h * half_width, half_width)
+            copies.append(
+                send(
+                    (base + d) if h == 0 else (44 + 4 * which + d),
+                    pair_send.at[which, d, :, columns],
+                    pair_recv.at[which, d, :, columns],
+                    sibling,
+                )
+            )
+        return copies
+
+    def give_plane(d, base, copies):
         which = 0 if base == 7 else 1
-        copy.wait_recv()
+        for copy in copies:
+            copy.wait_recv()
         total = held[d % 2] + pair_recv[which, d].astype(F32)
         if d == 0:
             own_sum[which] = total
@@ -728,18 +741,22 @@
         rows = rows_of(d)
         return lambda at: dot_nn(act[rows, :], down_w[:, at])
 
+    def receive(d):
+        step_line(d)
+        gather_pair[d] = send(3 + d, second_all.at[d, 0], second_all.at[d, 1], sibling)
+
     pairs, planes = {}, {}
     for d in range(4):
-        if d:
-            planes[d - 1] = give_plane(d - 1, 7, pairs[d - 1])
-            step_line(d)
-            gather_pair[d] = send(
-                3 + d, second_all.at[d, 0], second_all.at[d, 1], sibling
-            )
         gather_pair[d].wait_recv()
         forward(d)
+        if d == 0:
+            receive(1)
         pairs[d] = give_pair(d, 7, back(d))
-    planes[3] = give_plane(3, 7, pairs[3])
+        if d == 1:
+            receive(2)
+        planes[d] = give_plane(d, 7, pairs[d])
+        if d == 2:
+            receive(3)
 
     second_rows = second_all.reshape(8 * tok, width)
     block = 2 * TILE
@@ -828,6 +845,7 @@
         down_step(t)
     terms(gate_grad, 0, gate_w, 0)
     terms(up_grad, 0, gate_w, block)
+    pass_sum()
     branch_far = {}
     for d in (1, 2):
         branch_chips[d].wait_recv()
@@ -836,7 +854,6 @@
             23 + 20 * (d - 1), branch_all.at[0, d, part], branch_all.at[0, 3, part], over_chips[3 - d]
         )
         branch_pairs[d] = send(24 + d, branch_all.at[0, d], branch_all.at[1, d], sibling)
-    pass_sum()
     for d in (1, 2):
         branch_far[d].wait_recv()
     branch_pairs[3] = send(27, branch_all.at[0, 3], branch_all.at[1, 3], sibling)
@@ -883,7 +900,7 @@
 
     for d in range(4):
         branch_pairs[d].wait_recv()
-        for copy in (gather_pair[d], pairs[d], out_pairs[d], branch_pairs[d]):
+        for copy in (gather_pair[d], *pairs[d], *out_pairs[d], branch_pairs[d]):
             copy.wait_send()
     for d in (1, 2, 3):
         planes[d].wait_send()
@@ -940,8 +957,8 @@
             pltpu.VMEM((2, TILE, width), BF16),
             pltpu.SemaphoreType.DMA((5,)),
             pltpu.SemaphoreType.DMA((2,)),
-            pltpu.SemaphoreType.DMA((44,)),
-            pltpu.SemaphoreType.DMA((44,)),
+            pltpu.SemaphoreType.DMA((52,)),
+            pltpu.SemaphoreType.DMA((52,)),
         ],
         compiler_params=pltpu.CompilerParams(
             collective_id=1, has_side_effects=True, vmem_limit_bytes=60 << 20

time: 430 us -> 421 us (0.979)
  Pallas kernels: 409 us -> 399 us
    pallas_call x1, Pallas kernels: 141 us -> 130 us  [mlp_of(): pl.pallas_call(mlp_kernel, in_specs=[vmem] * 4 + [hbm] * 4, out_specs=[vm...]
where the time goes in v8:
time: 421 us; the launch traced here: 417 us
  Pallas kernels  399 us (95%)
  other arithmetic  10.6 us (3%)
  local copies, waits for them, and re-layouts  6.44 us (2%)
    pallas_call x1, Pallas kernels, back_of(): pl.pallas_call(back_kernel, in_specs=[vmem] * 13 + [hbm] * 8, out_specs=[...  145 us
    pallas_call x1, Pallas kernels, mlp_of(): pl.pallas_call(mlp_kernel, in_specs=[vmem] * 4 + [hbm] * 4, out_specs=[vm...  130 us
    pallas_call x1, Pallas kernels, front_of(): pl.pallas_call(front_kernel, in_specs=[vmem] * 8 + [hbm] * 6, out_specs=[...  124 us

profile of v8, /device:TPU:0, one launch (start us, length us, event | category | flops | bytes accessed | tf_op | source)
XLA Modules:
  0.0 417.0 jit_solution(8799617093081972519)
XLA Ops:
  0.7 0.1 stack.35
  0.8 0.8 select_reduce_fusion
  1.6 0.9 convert_reduce_fusion.1
  2.5 0.1 iota_add_fusion
  2.6 0.1 convert_reduce_fusion
  2.7 0.6 add.137.key_code_ref
  3.3 0.2 copy.32
  3.5 0.2 copy.31
  3.8 0.9 max.10.low_code_ref
  4.6 1.0 copy.33.code_ref
  5.6 3.0 multiply_sine_fusion
  8.7 123.7 %shard_map.212 = (bf16[128,2048]{1,0:T(8,128)(2,1)}, f32[128,2048]{1,0:T(8,128)}, bf16[1024,2048]{1,0:T(8,128)(2,1)}, bf16[1024,256]{1,0:T(8,128)(2,1)}, bf16[2,...) custom-call(bf16[128,2048]{1,0:T(8,128)(2,1)} %bitcast.148, ...), custom_call_target="tpu_custom_call" | custom-call | flops 4294967296 | bytes 41943040 | tf_op jit(solution)/shard_map/pallas_call | solution.py:1330
  132.4 129.9 %shard_map.213 = (bf16[128,2048]{1,0:T(8,128)(2,1)}, f32[128,2048]{1,0:T(8,128)}, f32[1,2048]{1,0:T(1,128)}, bf16[2,4,128,2048]{3,2,1,0:T(8,128)(2,1)}, bf16[512...) custom-call(bf16[128,2048]{1,0:T(8,128)(2,1)} %get-tuple-element.36.second_ref, ...), custom_call_target="tpu_custom_call" | custom-call | flops 38654705664 | bytes 37748736 | tf_op jit(solution)/shard_map/pallas_call | solution.py:927
  262.3 145.0 %shard_map.214 = (bf16[128,2048]{1,0:T(8,128)(2,1)}, f32[2,2048]{1,0:T(2,128)}, f32[64,2048]{1,0:T(8,128)}, bf16[8,64,512]{2,1,0:T(8,128)(2,1)}, bf16[4,2,64,204...) custom-call(bf16[128,2048]{1,0:T(8,128)(2,1)} %bitcast.149, f32[128,2048]{1,0:T(8,128)} %get-tuple-element.41.mid_grad_ref, ...), custom_call_target="tpu_custom_call" | custom-call | flops 9126805504 | bytes 41943040 | tf_op jit(solution)/shard_map/pallas_call | solution.py:1820
  407.2 0.7 constant_dynamic-slice_fusion
  408.0 0.5 slice_bitcast_fusion.32
  408.5 0.0 copy-start.1
  408.5 1.2 convert_element_type.23
  409.9 0.0 copy-start.7
  409.9 0.0 copy-start
  409.9 0.8 pad_maximum_fusion
  410.8 0.0 copy-done.1
  410.8 1.6 bitcast_convert_fusion
  412.4 0.0 copy-done.7
  412.4 0.0 copy-done
  412.4 0.5 convert_element_type.24
  413.1 0.0 copy-start.2
  413.2 0.0 copy-start.4
  413.2 0.0 copy-start.3
  413.3 0.0 copy-start.5
  413.4 0.0 copy-start.6
  413.4 0.8 copy-done.2
  414.2 0.8 copy.59
  415.0 0.0 copy-done.4
  415.0 0.8 copy.60
  415.8 0.0 copy-done.3
  415.8 0.8 copy.61
  416.6 0.0 copy-done.5
  416.6 0.0 copy-done.6
  (23 shorter events, 0.4 us)
Async XLA Ops:
  408.5 2.3 copy-start.1
  409.9 2.6 copy-start.7
  409.9 2.5 copy-start
  413.1 1.0 copy-start.2
  413.2 1.8 copy-start.4
  413.2 2.5 copy-start.3
  413.3 3.2 copy-start.5
  413.4 3.2 copy-start.6

commit v9 on v8

--- a/solution.py
+++ b/solution.py
@@ -1202,9 +1202,6 @@
     ]
     project(0, query_ref, False)
     step_out(2, pass_out)
-    head_pair = send(16, w_head, w_sibling, sibling)
-    keep_head = local(6, w_head, head_hbm)
-    keep_head.start()
     down_near, down_far = {}, {}
     half_part = part // 2
 
@@ -1260,6 +1257,9 @@
     branch = {
         d: send(26 + d, chip_send.at[d - 1], chip_recv.at[d - 1], over_chips[d]) for d in others
     }
+    head_pair = send(16, w_head, w_sibling, sibling)
+    keep_head = local(6, w_head, head_hbm)
+    keep_head.start()
 
     for d in others:
         column = flip(plane, d)

time: 421 us -> 421 us (level)
  no operation moved by 1% of the time
where the time goes in v9:
time: 421 us; the launch traced here: 417 us
  Pallas kernels  399 us (95%)
  other arithmetic  10.6 us (3%)
  local copies, waits for them, and re-layouts  6.44 us (2%)
    pallas_call x1, Pallas kernels, back_of(): pl.pallas_call(back_kernel, in_specs=[vmem] * 13 + [hbm] * 8, out_specs=[...  145 us
    pallas_call x1, Pallas kernels, mlp_of(): pl.pallas_call(mlp_kernel, in_specs=[vmem] * 4 + [hbm] * 4, out_specs=[vm...  130 us
    pallas_call x1, Pallas kernels, front_of(): pl.pallas_call(front_kernel, in_specs=[vmem] * 8 + [hbm] * 6, out_specs=[...  124 us

profile of v9, /device:TPU:0, one launch (start us, length us, event | category | flops | bytes accessed | tf_op | source)
XLA Modules:
  0.0 417.0 jit_solution(9736335089211092555)
XLA Ops:
  0.7 0.1 stack.35
  0.8 0.8 select_reduce_fusion
  1.6 0.9 convert_reduce_fusion.1
  2.5 0.1 iota_add_fusion
  2.6 0.1 convert_reduce_fusion
  2.7 0.6 add.137.key_code_ref
  3.3 0.2 copy.32
  3.5 0.2 copy.31
  3.8 0.9 max.10.low_code_ref
  4.6 1.0 copy.33.code_ref
  5.6 3.0 multiply_sine_fusion
  8.7 123.7 %shard_map.212 = (bf16[128,2048]{1,0:T(8,128)(2,1)}, f32[128,2048]{1,0:T(8,128)}, bf16[1024,2048]{1,0:T(8,128)(2,1)}, bf16[1024,256]{1,0:T(8,128)(2,1)}, bf16[2,...) custom-call(bf16[128,2048]{1,0:T(8,128)(2,1)} %bitcast.148, ...), custom_call_target="tpu_custom_call" | custom-call | flops 4294967296 | bytes 41943040 | tf_op jit(solution)/shard_map/pallas_call | solution.py:1330
  132.4 129.9 %shard_map.213 = (bf16[128,2048]{1,0:T(8,128)(2,1)}, f32[128,2048]{1,0:T(8,128)}, f32[1,2048]{1,0:T(1,128)}, bf16[2,4,128,2048]{3,2,1,0:T(8,128)(2,1)}, bf16[512...) custom-call(bf16[128,2048]{1,0:T(8,128)(2,1)} %get-tuple-element.36.second_ref, ...), custom_call_target="tpu_custom_call" | custom-call | flops 38654705664 | bytes 37748736 | tf_op jit(solution)/shard_map/pallas_call | solution.py:927
  262.3 145.0 %shard_map.214 = (bf16[128,2048]{1,0:T(8,128)(2,1)}, f32[2,2048]{1,0:T(2,128)}, f32[64,2048]{1,0:T(8,128)}, bf16[8,64,512]{2,1,0:T(8,128)(2,1)}, bf16[4,2,64,204...) custom-call(bf16[128,2048]{1,0:T(8,128)(2,1)} %bitcast.149, f32[128,2048]{1,0:T(8,128)} %get-tuple-element.41.mid_grad_ref, ...), custom_call_target="tpu_custom_call" | custom-call | flops 9126805504 | bytes 41943040 | tf_op jit(solution)/shard_map/pallas_call | solution.py:1820
  407.3 0.7 constant_dynamic-slice_fusion
  408.0 0.5 slice_bitcast_fusion.32
  408.5 0.0 copy-start.1
  408.5 1.2 convert_element_type.23
  409.9 0.0 copy-start.7
  409.9 0.0 copy-start
  410.0 0.8 pad_maximum_fusion
  410.8 0.0 copy-done.1
  410.8 1.6 bitcast_convert_fusion
  412.4 0.0 copy-done.7
  412.4 0.0 copy-done
  412.4 0.5 convert_element_type.24
  413.2 0.0 copy-start.2
  413.2 0.0 copy-start.4
  413.3 0.0 copy-start.3
  413.4 0.0 copy-start.5
  413.4 0.0 copy-start.6
  413.4 0.8 copy-done.2
  414.2 0.8 copy.59
  415.0 0.0 copy-done.4
  415.0 0.8 copy.60
  415.8 0.0 copy-done.3
  415.8 0.8 copy.61
  416.6 0.0 copy-done.5
  416.6 0.0 copy-done.6
  (23 shorter events, 0.4 us)
Async XLA Ops:
  408.5 2.3 copy-start.1
  409.9 2.6 copy-start.7
  409.9 2.5 copy-start
  413.2 1.0 copy-start.2
  413.2 1.8 copy-start.4
  413.3 2.5 copy-start.3
  413.4 3.2 copy-start.5
  413.4 3.2 copy-start.6
